TPU v7x, 512 devices: a whole 4x4x16 slice. The times are simulated.
512 devices in a mesh: nodes: 128 (over z, x, core), mp: 4 (over y).
Axes of the slice: x: 4, y: 4, z: 16, core: 2. Of those that a mesh axis runs over, the one named last changes fastest.
Arguments:
- features: bfloat16 [16384, 1024], P('nodes'), may hold values from -24 to 24
- qkv_weight: bfloat16 [1024, 3, 1024], P(None, None, 'mp'), may hold values from -0.5 to 0.5
- vnode_emb: bfloat16 [4, 1024], replicated, may hold values from -6 to 6
- edge_bias: float32 [3, 8], P(None, 'mp'), may hold values from -1 to 1
- out_grad: bfloat16 [16384, 1024], P('nodes', 'mp'), may hold values from -6 to 6
- neighbours: int32 [4, 16384], P(None, 'nodes'), may hold values from 0 to 16383, as said below
- member: int32 [16384, 4], P('nodes'), may hold values 0 or 1
- tile_list: int32 [128, 3, 2], P('nodes'), may hold values from 0 to 2, as said below
- tile_count: int32 [128], P('nodes'), may hold values from 3 to 3
Outputs:
- feature_grad: bfloat16 [16384, 1024], P('nodes', 'mp')
- weight_grad: float32 [1024, 3, 1024], P('nodes', None, 'mp')
- vnode_grad: float32 [4, 1024], replicated
Inputs may be any that keep to these rules, and one draw needn't show every extreme that they name: `neighbours`: each row is a permutation of the 16384 nodes; for each row, exactly 1 of one shard's nodes have their neighbour on any one given shard. `tile_list`: for every shard the 3 entries list each pair (query block below 1, extended key block below 3) once: the 1 pairs (q, q + 1) of a query block q first, then (0, 0) and (0, 2).
All inputs are finite; a program needn't handle non-finite values. No bound on the sum of `member` on one device may be relied on, other than what follows from the above.
Results may differ from a plain program's by a relative error of at most 0.014.
Values may be sent and summed in bfloat16 or wider, within the bound.
No kernel may reach another device: no remote copies, remote signals or barrier semaphores. Data moves between devices by JAX's collectives and lax.ppermute only.
A program may use at most 64 MiB of HBM per device.

v0:
```python
import math

import jax
import jax.numpy as jnp
from jax import lax
from jax.sharding import PartitionSpec as P

HEAD = 128
TILE = 128
DEGREE = 4
VIRTUAL = 4


SHARPNESS = 8.0
EPSILON = 1e-06
PRECISE = lax.Precision.HIGHEST


def with_halo(cells, sides, width):
    for axis, dim in sides:
        count = lax.axis_size(axis)
        head = lax.slice_in_dim(cells, 0, width, axis=dim)
        tail = lax.slice_in_dim(cells, cells.shape[dim] - width, cells.shape[dim], axis=dim)
        cells = jnp.concatenate(
            [
                lax.ppermute(tail, axis, [(i, (i + 1) % count) for i in range(count)]),
                cells,
                lax.ppermute(head, axis, [((i + 1) % count, i) for i in range(count)]),
            ],
            axis=dim,
        )
    return cells


def unit_rows(values):
    return values * lax.rsqrt(jnp.mean(values * values, axis=-1, keepdims=True) + EPSILON)


def unit_grad(values, cotangent):
    return jax.vjp(unit_rows, values)[1](cotangent)[0]


def split_heads(values):
    return values.reshape(values.shape[:-1] + (values.shape[-1] // HEAD, HEAD))


def add_rows(target, piece, start_row):
    current = lax.dynamic_slice_in_dim(target, start_row, piece.shape[0], 0)
    return lax.dynamic_update_slice_in_dim(target, current + piece, start_row, 0)


def body(
    features, qkv_weight, vnode_emb, edge_bias, out_grad, neighbours, member, tile_list, tile_count
):
    row_count = features.shape[0]
    col_width = qkv_weight.shape[2]
    width_in = qkv_weight.shape[0]
    shard_count = lax.axis_size("nodes")
    group_size = row_count // shard_count
    score_scale = SHARPNESS / HEAD
    log_boost = math.log(TILE)
    flat_weight = qkv_weight.reshape(width_in, 3 * col_width)
    projected = jnp.dot(features, flat_weight, preferred_element_type=jnp.float32).reshape(
        row_count, 3, col_width
    )
    query = projected[:, 0]
    stored = projected[:, 1:].astype(jnp.bfloat16)
    kv_weight = qkv_weight[:, 1:].reshape(width_in, 2 * col_width)
    virtual_kv = jnp.dot(vnode_emb, kv_weight, preferred_element_type=jnp.float32).reshape(
        VIRTUAL, 2, col_width
    )
    extended = with_halo(stored, (("nodes", 0),), TILE)
    owners = neighbours // row_count
    order = jnp.argsort(owners, axis=1, stable=True)
    inverse = jnp.argsort(order, axis=1)
    perm_ids = jnp.arange(DEGREE, dtype=jnp.int32)[:, None]
    wanted = (neighbours % row_count)[perm_ids, order].reshape(DEGREE, shard_count, group_size)
    arrived = []
    served = []
    for perm_index in range(DEGREE):
        asked_rows = lax.all_to_all(
            wanted[perm_index], "nodes", split_axis=0, concat_axis=0, tiled=True
        )
        rows_in, asked_rows = (
            lax.all_to_all(stored[asked_rows], "nodes", split_axis=0, concat_axis=0, tiled=True),
            asked_rows,
        )
        arrived.append(rows_in)
        served.append(asked_rows)
    near_sorted = jnp.stack(arrived).reshape(DEGREE, row_count, 2, col_width)
    nearby = near_sorted[perm_ids, inverse].astype(jnp.float32)
    unit_q = unit_rows(split_heads(query))
    keys_ext = split_heads(extended[:, 0].astype(jnp.float32))
    values_ext = split_heads(extended[:, 1].astype(jnp.float32))
    unit_k = unit_rows(keys_ext)
    keys_near = split_heads(nearby[:, :, 0])
    values_near = split_heads(nearby[:, :, 1])
    unit_near = unit_rows(keys_near)
    keys_virtual = split_heads(virtual_kv[:, 0])
    values_virtual = split_heads(virtual_kv[:, 1])
    unit_virtual = unit_rows(keys_virtual)
    members = member.astype(jnp.float32)
    grad_out = split_heads(out_grad.astype(jnp.float32))
    head_count = col_width // HEAD
    listing = tile_list[0]
    how_many = tile_count[0]

    def tile_scores(tile_index):
        start_q = listing[tile_index, 0] * TILE
        start_k = listing[tile_index, 1] * TILE
        k_block = lax.dynamic_slice_in_dim(unit_k, start_k, TILE, 0)
        weights = jnp.exp(
            score_scale * jnp.einsum("qhd,khd->hqk", unit_q, k_block, precision=PRECISE)
            + edge_bias[0][:, None, None]
        )
        return (start_q, start_k, unit_q, k_block, weights)

    def forward_tile(tile_index, carried):
        totals, mixture = carried
        start_q, start_k, q_block, k_block, weights = tile_scores(tile_index)
        v_block = lax.dynamic_slice_in_dim(values_ext, start_k, TILE, 0)
        totals = add_rows(totals, jnp.sum(weights, axis=2).T, start_q)
        mixture = add_rows(
            mixture, jnp.einsum("hqk,khd->qhd", weights, v_block, precision=PRECISE), start_q
        )
        return (totals, mixture)

    empty_totals = jnp.zeros((row_count, head_count), jnp.float32)
    totals, mixture = lax.fori_loop(
        0, how_many, forward_tile, (empty_totals, jnp.zeros_like(unit_q))
    )
    near_weights = jnp.exp(
        score_scale * jnp.sum(unit_q[None] * unit_near, axis=-1) + edge_bias[1] + log_boost
    )
    totals = totals + jnp.sum(near_weights, axis=0)
    mixture = mixture + jnp.sum(near_weights[..., None] * values_near, axis=0)
    virtual_weights = (
        jnp.exp(
            score_scale * jnp.einsum("rhd,vhd->rhv", unit_q, unit_virtual, precision=PRECISE)
            + edge_bias[2][None, :, None]
            + log_boost
        )
        * members[:, None, :]
    )
    totals = totals + jnp.sum(virtual_weights, axis=2)
    mixture = mixture + jnp.einsum(
        "rhv,vhd->rhd", virtual_weights, values_virtual, precision=PRECISE
    )
    inv_totals = 1.0 / totals
    output = mixture * inv_totals[..., None]
    delta = jnp.sum(grad_out * output, axis=-1)

    def backward_tile(tile_index, carried):
        d_query, d_keys, d_values = carried
        start_q, start_k, q_block, k_block, weights = tile_scores(tile_index)
        v_block = lax.dynamic_slice_in_dim(values_ext, start_k, TILE, 0)
        probs = weights * inv_totals.T[:, :, None]
        d_probs = jnp.einsum("qhd,khd->hqk", grad_out, v_block, precision=PRECISE)
        d_scores = probs * (d_probs - delta.T[:, :, None]) * score_scale
        d_query = add_rows(
            d_query, jnp.einsum("hqk,khd->qhd", d_scores, k_block, precision=PRECISE), start_q
        )
        d_keys = add_rows(
            d_keys, jnp.einsum("hqk,qhd->khd", d_scores, q_block, precision=PRECISE), start_k
        )
        d_values = add_rows(
            d_values, jnp.einsum("hqk,qhd->khd", probs, grad_out, precision=PRECISE), start_k
        )
        return (d_query, d_keys, d_values)

    start_grads = (jnp.zeros_like(unit_q), jnp.zeros_like(unit_k), jnp.zeros_like(values_ext))
    d_unit_q, d_unit_k, d_values_ext = lax.fori_loop(0, how_many, backward_tile, start_grads)
    near_probs = near_weights * inv_totals[None]
    near_dprobs = jnp.sum(grad_out[None] * values_near, axis=-1)
    near_dscores = near_probs * (near_dprobs - delta[None]) * score_scale
    d_unit_q = d_unit_q + jnp.sum(near_dscores[..., None] * unit_near, axis=0)
    d_unit_near = near_dscores[..., None] * unit_q[None]
    d_values_near = near_probs[..., None] * grad_out[None]
    virtual_probs = virtual_weights * inv_totals[:, :, None]
    virtual_dprobs = jnp.einsum("rhd,vhd->rhv", grad_out, values_virtual, precision=PRECISE)
    virtual_dscores = virtual_probs * (virtual_dprobs - delta[:, :, None]) * score_scale
    d_unit_q = d_unit_q + jnp.einsum(
        "rhv,vhd->rhd", virtual_dscores, unit_virtual, precision=PRECISE
    )
    d_unit_virtual = jnp.einsum("rhv,rhd->vhd", virtual_dscores, unit_q, precision=PRECISE)
    d_values_virtual = jnp.einsum("rhv,rhd->vhd", virtual_probs, grad_out, precision=PRECISE)
    d_query_raw = unit_grad(split_heads(query), d_unit_q).reshape(row_count, col_width)
    d_keys_raw = unit_grad(keys_ext, d_unit_k).reshape(-1, col_width)
    grad_ext = jnp.stack([d_keys_raw, d_values_ext.reshape(-1, col_width)], axis=1)
    rims = jnp.concatenate([grad_ext[:TILE], grad_ext[-TILE:]], axis=0)
    returned = with_halo(rims.astype(jnp.bfloat16), (("nodes", 0),), TILE).astype(rims.dtype)
    local = grad_ext[TILE : TILE + row_count]
    local = local.at[:TILE].add(returned[:TILE])
    local = local.at[row_count - TILE :].add(returned[3 * TILE :])
    d_near_keys = unit_grad(keys_near, d_unit_near).reshape(DEGREE, row_count, col_width)
    grad_near = jnp.stack(
        [d_near_keys, d_values_near.reshape(DEGREE, row_count, col_width)], axis=2
    ).astype(jnp.bfloat16)
    grad_sorted = grad_near[perm_ids, order]
    for perm_index in range(DEGREE):
        came_back = lax.all_to_all(
            grad_sorted[perm_index].reshape(shard_count, group_size, 2, col_width),
            "nodes",
            split_axis=0,
            concat_axis=0,
            tiled=True,
        )
        local = local.at[served[perm_index].reshape(-1)].add(
            came_back.reshape(row_count, 2, col_width).astype(jnp.float32)
        )
    gradient_qkv = jnp.concatenate([d_query_raw[:, None], local], axis=1).astype(jnp.bfloat16)
    flat_grad = gradient_qkv.reshape(row_count, 3 * col_width)
    d_virtual = jnp.stack(
        [
            unit_grad(keys_virtual, d_unit_virtual).reshape(VIRTUAL, col_width),
            d_values_virtual.reshape(VIRTUAL, col_width),
        ],
        axis=1,
    )
    partial_features = jnp.dot(flat_grad, flat_weight.T, preferred_element_type=jnp.float32)
    feature_grad = lax.psum_scatter(
        partial_features.astype(jnp.bfloat16), "mp", scatter_dimension=1, tiled=True
    )
    out_scale = 1.0 / math.sqrt(row_count * shard_count)
    vnode_wide = vnode_emb.astype(jnp.float32)
    weight_rows = width_in // shard_count
    term = jnp.dot(features.T, flat_grad, preferred_element_type=jnp.float32).reshape(
        weight_rows * lax.axis_size("nodes"), 3, col_width
    )
    extra = jnp.einsum("vr,vtc->rtc", vnode_wide, d_virtual, precision=PRECISE)
    weight_grad = (
        lax.psum_scatter(
            term + jnp.concatenate([jnp.zeros_like(extra[:, :1]), extra], axis=1),
            "nodes",
            scatter_dimension=0,
            tiled=True,
        )
        * out_scale
    )
    vnode_part = jnp.einsum(
        "vtc,dtc->vd", d_virtual, qkv_weight[:, 1:].astype(jnp.float32), precision=PRECISE
    )
    vnode_grad = lax.psum(vnode_part, ("nodes", "mp")) * out_scale
    return (feature_grad, weight_grad, vnode_grad)


def solution(mesh):
    return jax.shard_map(
        body,
        mesh=mesh,
        in_specs=(
            P("nodes", None),
            P(None, None, "mp"),
            P(),
            P(None, "mp"),
            P("nodes", "mp"),
            P(None, "nodes"),
            P("nodes", None),
            P("nodes", None, None),
            P("nodes"),
        ),
        out_specs=(P("nodes", "mp"), P("nodes", None, "mp"), P()),
        check_vma=False,
    )
```

profile of v0, /device:TPU:2, one launch (start us, length us, event | category | flops | bytes accessed | tf_op | source)
XLA Modules:
  0.0 802.2 jit_solution(2348157193369594120)
XLA Ops:
  19.0 4.7 gather_fusion
  24.5 21.9 %all-to-all-start.6 = ((s32[128,1,1]{2,1,0:T(1,128)}), s32[128,1,1]{2,1,0:T(1,128)S(1)}, u32[]{:S(2)}, u32[]{:S(2)}) async-start(s32[128,1,1]{2,1,0:T(1,128)} %copy.371), calls=%async_computation.6 | async-start | bytes 131072 | tf_op jit(solution)/shard_map/all_to_all | solution.py:81
  47.9 12.3 %all-to-all-done.6 = s32[128,1,1]{2,1,0:T(1,128)S(1)} async-done(((s32[128,1,1]{2,1,0:T(1,128)}), s32[128,1,1]{2,1,0:T(1,128)S(1)}, u32[]{:S(2)}, u32[]{:S(2)}) %all-to-all-start.6) | async-done | bytes 544 | tf_op jit(solution)/shard_map/all_to_all | solution.py:81
  60.2 6.7 all-to-all-start.4
  72.6 8.3 %all-to-all-done.4 = s32[128,1,1]{2,1,0:T(1,128)S(1)} async-done(((s32[128,1,1]{2,1,0:T(1,128)}), s32[128,1,1]{2,1,0:T(1,128)S(1)}, u32[]{:S(2)}, u32[]{:S(2)}) %all-to-all-start.4) | async-done | bytes 544 | tf_op jit(solution)/shard_map/all_to_all | solution.py:81
  81.0 8.2 %all-to-all-start.2 = ((s32[128,1,1]{2,1,0:T(1,128)}), s32[128,1,1]{2,1,0:T(1,128)S(1)}, u32[]{:S(2)}, u32[]{:S(2)}) async-start(s32[128,1,1]{2,1,0:T(1,128)} %copy.365), calls=%async_computation.2 | async-start | bytes 131072 | tf_op jit(solution)/shard_map/all_to_all | solution.py:81
  89.2 9.2 %fusion.84 = (s32[128]{0:T(128)S(1)}, s32[128]{0:T(128)S(1)}, s32[128]{0:T(128)S(1)}, s32[128]{0:T(128)S(1)}) fusion(s32[128,1,1]{2,1,0:T(1,128)S(1)} %all-to-all-done.6, s32[128,1,1]{2,1,0:T(1,128)S(1)} %all-to-all-done.4), kind=kLoop, calls=%fused_computation.208 | loop fusion | flops 768 | bytes 3072 | tf_op jit(solution)/shard_map/all_to_all | solution.py:81
  103.0 11.5 %all-to-all-start = ((s32[128,1,1]{2,1,0:T(1,128)}), s32[128,1,1]{2,1,0:T(1,128)S(1)}, u32[]{:S(2)}, u32[]{:S(2)}) async-start(s32[128,1,1]{2,1,0:T(1,128)} %copy.362), calls=%async_computation | async-start | bytes 131072 | tf_op jit(solution)/shard_map/all_to_all | solution.py:81
  116.0 12.4 %all-to-all-done = s32[128,1,1]{2,1,0:T(1,128)S(1)} async-done(((s32[128,1,1]{2,1,0:T(1,128)}), s32[128,1,1]{2,1,0:T(1,128)S(1)}, u32[]{:S(2)}, u32[]{:S(2)}) %all-to-all-start) | async-done | bytes 544 | tf_op jit(solution)/shard_map/all_to_all | solution.py:81
  128.4 7.1 all-to-all-start.7
  135.5 9.2 %fusion.86 = (s32[128]{0:T(128)S(1)}, s32[128]{0:T(128)S(1)}, s32[128]{0:T(128)S(1)}, s32[128]{0:T(128)S(1)}) fusion(s32[128,1,1]{2,1,0:T(1,128)S(1)} %all-to-all-done.2, s32[128,1,1]{2,1,0:T(1,128)S(1)} %all-to-all-done), kind=kLoop, calls=%fused_computation.210 | loop fusion | flops 768 | bytes 3072 | tf_op jit(solution)/shard_map/all_to_all | solution.py:81
  151.7 16.0 %all-to-all-start.5 = ((bf16[128,1,2,256]{3,2,1,0:T(2,128)(2,1)}), bf16[128,1,2,256]{3,2,1,0:T(2,128)(2,1)S(1)}, u32[]{:S(2)}, u32[]{:S(2)}) async-start(bf16[128,1,2,256]{3,2,1,0:T(2,128)(2,1)} %bitcast.29), calls=%async_computation.5 | async-start | bytes 262144 | tf_op jit(solution)/shard_map/all_to_all | solution.py:85
  169.6 14.1 %all-to-all-done.5 = bf16[128,1,2,256]{3,2,1,0:T(2,128)(2,1)S(1)} async-done(((bf16[128,1,2,256]{3,2,1,0:T(2,128)(2,1)}), bf16[128,1,2,256]{3,2,1,0:T(2,128)(2,1)S(1)}, u32[]{:S(2)}, u32[]{:S(2)}) %all-to-all-start.5) | async-done | bytes 131104 | tf_op jit(solution)/shard_map/all_to_all | solution.py:85
  183.7 7.4 all-to-all-start.3
  192.2 15.1 %all-to-all-done.3 = bf16[128,1,2,256]{3,2,1,0:T(2,128)(2,1)S(1)} async-done(((bf16[128,1,2,256]{3,2,1,0:T(2,128)(2,1)}), bf16[128,1,2,256]{3,2,1,0:T(2,128)(2,1)S(1)}, u32[]{:S(2)}, u32[]{:S(2)}) %all-to-all-start.3) | async-done | bytes 131104 | tf_op jit(solution)/shard_map/all_to_all | solution.py:85
  207.3 7.0 all-to-all-start.1
  214.4 12.9 %while.30 = (s32[]{:T(128)}, f32[128,2]{0,1:T(2,128)S(1)}, f32[128,2,128]{0,2,1:T(8,128)S(1)}, s32[]{:T(128)}, s32[3,2]{0,1:T(2,128)S(1)}, /*index=5*/f32[384,2,...) while((s32[]{:T(128)}, f32[128,2]{0,1:T(2,128)S(1)}, ...), condition=%wide.region_4.5_spmd, body=%wide.region_2.4_spmd.sunk | while | flops 100794376 | bytes 1184493 | solution.py:129
  245.4 22.8 %while.31 = (s32[]{:T(128)}, f32[128,2,128]{0,2,1:T(8,128)S(1)}, f32[384,2,128]{2,0,1:T(8,128)S(1)}, f32[384,2,128]{2,1,0:T(2,128)S(1)}, s32[]{:T(128)}, /*index...) while((s32[]{:T(128)}, f32[128,2,128]{0,2,1:T(8,128)S(1)}, ...), condition=%wide.region_15.16_spmd, body=%wide.region_14.15_spmd.sunk | while | flops 251953152 | bytes 3279641 | solution.py:172
  292.3 16.5 %all-to-all-start.8 = ((bf16[128,1,2,256]{3,2,1,0:T(2,128)(2,1)}), bf16[128,1,2,256]{3,2,1,0:T(2,128)(2,1)S(1)}, u32[]{:S(2)}, u32[]{:S(2)}) async-start(bf16[128,1,2,256]{3,2,1,0:T(2,128)(2,1)} %get-tuple-element.413), calls=%async_computation.8 | async-start | bytes 262144 | tf_op jit(solution)/shard_map/all_to_all | solution.py:201
  309.6 15.3 %all-to-all-done.8 = bf16[128,1,2,256]{3,2,1,0:T(2,128)(2,1)S(1)} async-done(((bf16[128,1,2,256]{3,2,1,0:T(2,128)(2,1)}), bf16[128,1,2,256]{3,2,1,0:T(2,128)(2,1)S(1)}, u32[]{:S(2)}, u32[]{:S(2)}) %all-to-all-start.8) | async-done | bytes 131104 | tf_op jit(solution)/shard_map/all_to_all | solution.py:201
  324.9 7.1 all-to-all-start.9
  335.1 13.0 %all-to-all-done.9 = bf16[128,1,2,256]{3,2,1,0:T(2,128)(2,1)S(1)} async-done(((bf16[128,1,2,256]{3,2,1,0:T(2,128)(2,1)}), bf16[128,1,2,256]{3,2,1,0:T(2,128)(2,1)S(1)}, u32[]{:S(2)}, u32[]{:S(2)}) %all-to-all-start.9) | async-done | bytes 131104 | tf_op jit(solution)/shard_map/all_to_all | solution.py:201
  348.1 7.1 all-to-all-start.10
  356.9 14.4 %all-to-all-done.10 = bf16[128,1,2,256]{3,2,1,0:T(2,128)(2,1)S(1)} async-done(((bf16[128,1,2,256]{3,2,1,0:T(2,128)(2,1)}), bf16[128,1,2,256]{3,2,1,0:T(2,128)(2,1)S(1)}, u32[]{:S(2)}, u32[]{:S(2)}) %all-to-all-start.10) | async-done | bytes 131104 | tf_op jit(solution)/shard_map/all_to_all | solution.py:201
  371.3 7.2 all-to-all-start.11
  378.7 5.2 scatter_fusion
  384.0 5.2 scatter_fusion.1
  389.3 5.2 scatter_fusion.2
  394.9 5.2 scatter_fusion.3
  411.3 104.8 %psum.7 = f32[4,1024]{1,0:T(4,128)S(1)} all-reduce(f32[4,1024]{1,0:T(4,128)S(1)} %convolution_bitcast_fusion.8), channel_id=1, replica_groups=mesh['nodes'=128,'mp'=4] {'nodes','mp'}, use_global_device_ids=true, to_apply=%region_28.29 | all-reduce | flops 4096 | bytes 32768 | tf_op jit(solution)/shard_map/psum | solution.py:243
  516.7 248.4 %all-reduce.4.cloned.1.call-done = f32[1024,3,256]{2,1,0:T(4,128)} async-done(((f32[1024,3,256]{2,1,0:T(4,128)}), f32[1024,3,256]{2,1,0:T(4,128)}) %all-reduce.4.cloned.1.call-update) | async-done | bytes 3145744
  766.5 28.7 %reduce-scatter.2.cloned.1.call-done = bf16[128,256]{1,0:T(8,128)(2,1)} async-done(((bf16[128,1024]{1,0:T(8,128)(2,1)}), bf16[128,256]{1,0:T(8,128)(2,1)}) %reduce-scatter.2.cloned.1.call-update) | async-done | bytes 65552 | tf_op jit(solution)/shard_map/reduce_scatter | solution.py:221
  (312 shorter events, 114.0 us)
Async XLA Ops:
  9.7 158.7 %collective-permute-start.1 = (bf16[128,2,256]{2,0,1:T(8,128)(2,1)S(1)}, bf16[128,2,256]{2,0,1:T(8,128)(2,1)S(1)}, u32[]{:S(2)}, u32[]{:S(2)}) collective-permute-start(bf16[128,2,256]{2,0,1:T(8,128)(2,1)S(1)} %slice.232), channel_id=1, source_target_pairs={{4,0},{8,4},{12,8},{16,12},{20,16},{24,20},{28,24},{32,28},{36,32}... | collective-permute-start | bytes 393224 | tf_op jit(solution)/shard_map/ppermute | solution.py:28
  11.8 156.6 %collective-permute-start = (bf16[128,2,256]{2,0,1:T(8,128)(2,1)S(1)}, bf16[128,2,256]{2,0,1:T(8,128)(2,1)}, u32[]{:S(2)}, u32[]{:S(2)}) collective-permute-start(bf16[128,2,256]{2,0,1:T(8,128)(2,1)S(1)} %slice.232), channel_id=1, source_target_pairs={{0,4},{4,8},{8,12},{12,16},{16,20},{20,24},{24,28},{28,32},{32,36}... | collective-permute-start | bytes 393224 | tf_op jit(solution)/shard_map/ppermute | solution.py:26
  17.5 51.0 %copy-start.35 = (f32[4,2]{1,0:T(4,128)}, f32[4,2]{1,0:T(4,128)S(1)}, u32[]{:S(2)}) copy-start(f32[4,2]{1,0:T(4,128)S(1)} %multiply_reduce_fusion.10) | copy-start | bytes 100
  17.7 51.2 %copy-start.14 = (bf16[128,256]{1,0:T(8,128)(2,1)S(1)}, bf16[128,256]{1,0:T(8,128)(2,1)}, u32[]{:S(2)}) copy-start(bf16[128,256]{1,0:T(8,128)(2,1)} %param.25) | copy-start | bytes 196612
  24.5 35.8 %all-to-all-start.6 = ((s32[128,1,1]{2,1,0:T(1,128)}), s32[128,1,1]{2,1,0:T(1,128)S(1)}, u32[]{:S(2)}, u32[]{:S(2)}) async-start(s32[128,1,1]{2,1,0:T(1,128)} %copy.371), calls=%async_computation.6 | async-start | bytes 131072 | tf_op jit(solution)/shard_map/all_to_all | solution.py:81
  47.2 104.5 %copy-start.39 = (f32[4,2]{0,1:T(2,128)}, f32[4,2]{0,1:T(2,128)S(1)}, u32[]{:S(2)}) copy-start(f32[4,2]{0,1:T(2,128)S(1)} %copy.378) | copy-start | bytes 100
  60.2 20.7 %all-to-all-start.4 = ((s32[128,1,1]{2,1,0:T(1,128)}), s32[128,1,1]{2,1,0:T(1,128)S(1)}, u32[]{:S(2)}, u32[]{:S(2)}) async-start(s32[128,1,1]{2,1,0:T(1,128)} %copy.368), calls=%async_computation.4 | async-start | bytes 131072 | tf_op jit(solution)/shard_map/all_to_all | solution.py:81
  66.9 100.8 %sort.39.cloned.1.call-start = ((), (), s32[]{:S(2)}) async-start(), calls=%async_computation.16 | async-start | bytes 12320 | tf_op jit(solution)/shard_map/jit(argsort)/sort | solution.py:75
  68.9 169.0 %copy-start.11 = (f32[128,2,128]{2,1,0:T(2,128)}, f32[128,2,128]{2,1,0:T(2,128)S(1)}, u32[]{:S(2)}) copy-start(f32[128,2,128]{2,1,0:T(2,128)S(1)} %copy.361) | copy-start | bytes 393220
  81.0 22.0 %all-to-all-start.2 = ((s32[128,1,1]{2,1,0:T(1,128)}), s32[128,1,1]{2,1,0:T(1,128)S(1)}, u32[]{:S(2)}, u32[]{:S(2)}) async-start(s32[128,1,1]{2,1,0:T(1,128)} %copy.365), calls=%async_computation.2 | async-start | bytes 131072 | tf_op jit(solution)/shard_map/all_to_all | solution.py:81
  103.0 25.5 %all-to-all-start = ((s32[128,1,1]{2,1,0:T(1,128)}), s32[128,1,1]{2,1,0:T(1,128)S(1)}, u32[]{:S(2)}, u32[]{:S(2)}) async-start(s32[128,1,1]{2,1,0:T(1,128)} %copy.362), calls=%async_computation | async-start | bytes 131072 | tf_op jit(solution)/shard_map/all_to_all | solution.py:81
  128.4 23.2 %all-to-all-start.7 = ((bf16[128,1,2,256]{3,2,1,0:T(2,128)(2,1)}), bf16[128,1,2,256]{3,2,1,0:T(2,128)(2,1)S(1)}, u32[]{:S(2)}, u32[]{:S(2)}) async-start(bf16[128,1,2,256]{3,2,1,0:T(2,128)(2,1)} %bitcast.33), calls=%async_computation.7 | async-start | bytes 262144 | tf_op jit(solution)/shard_map/all_to_all | solution.py:85
  151.7 32.1 %all-to-all-start.5 = ((bf16[128,1,2,256]{3,2,1,0:T(2,128)(2,1)}), bf16[128,1,2,256]{3,2,1,0:T(2,128)(2,1)S(1)}, u32[]{:S(2)}, u32[]{:S(2)}) async-start(bf16[128,1,2,256]{3,2,1,0:T(2,128)(2,1)} %bitcast.29), calls=%async_computation.5 | async-start | bytes 262144 | tf_op jit(solution)/shard_map/all_to_all | solution.py:85
  169.4 44.9 %copy-start.53 = (s32[1,3,2]{1,2,0:T(2,128)S(1)}, s32[1,3,2]{1,2,0:T(2,128)}, u32[]{:S(2)}) copy-start(s32[1,3,2]{1,2,0:T(2,128)} %param.28) | copy-start | bytes 76
  183.7 23.5 %all-to-all-start.3 = ((bf16[128,1,2,256]{3,2,1,0:T(2,128)(2,1)}), bf16[128,1,2,256]{3,2,1,0:T(2,128)(2,1)S(1)}, u32[]{:S(2)}, u32[]{:S(2)}) async-start(bf16[128,1,2,256]{3,2,1,0:T(2,128)(2,1)} %bitcast.25), calls=%async_computation.3 | async-start | bytes 262144 | tf_op jit(solution)/shard_map/all_to_all | solution.py:85
  207.3 23.1 %all-to-all-start.1 = ((bf16[128,1,2,256]{3,2,1,0:T(2,128)(2,1)}), bf16[128,1,2,256]{3,2,1,0:T(2,128)(2,1)S(1)}, u32[]{:S(2)}, u32[]{:S(2)}) async-start(bf16[128,1,2,256]{3,2,1,0:T(2,128)(2,1)} %bitcast.21), calls=%async_computation.1 | async-start | bytes 262144 | tf_op jit(solution)/shard_map/all_to_all | solution.py:85
  272.1 83.3 %collective-permute-start.3 = (bf16[128,2,256]{2,1,0:T(2,128)(2,1)}, bf16[128,2,256]{2,1,0:T(2,128)(2,1)}, u32[]{:S(2)}, u32[]{:S(2)}) collective-permute-start(bf16[128,2,256]{2,1,0:T(2,128)(2,1)} %get-tuple-element.417), channel_id=1, source_target_pairs={{4,0},{8,4},{12,8},{16,12},{20,16},{24,20},{28,24},{32,28},{36,32}... | collective-permute-start | bytes 393224 | tf_op jit(solution)/shard_map/ppermute | solution.py:28
  274.1 81.4 %collective-permute-start.2 = (bf16[128,2,256]{2,1,0:T(2,128)(2,1)}, bf16[128,2,256]{2,1,0:T(2,128)(2,1)}, u32[]{:S(2)}, u32[]{:S(2)}) collective-permute-start(bf16[128,2,256]{2,1,0:T(2,128)(2,1)} %get-tuple-element.416), channel_id=1, source_target_pairs={{0,4},{4,8},{8,12},{12,16},{16,20},{20,24},{24,28},{28,32},{32,36}... | collective-permute-start | bytes 393224 | tf_op jit(solution)/shard_map/ppermute | solution.py:26
  287.2 44.7 %copy-start.40 = (f32[4,2]{0,1:T(2,128)S(1)}, f32[4,2]{0,1:T(2,128)}, u32[]{:S(2)}) copy-start(f32[4,2]{0,1:T(2,128)} %copy-done.39) | copy-start | bytes 100
  287.2 44.9 %copy-start.10 = (f32[128,2,128]{0,2,1:T(8,128)S(1)}, f32[128,2,128]{0,2,1:T(8,128)}, u32[]{:S(2)}) copy-start(f32[128,2,128]{0,2,1:T(8,128)} %copy-done.9) | copy-start | bytes 393220
  288.4 44.3 %copy-start.32 = (bf16[4,1024]{1,0:T(4,128)(2,1)S(1)}, bf16[4,1024]{1,0:T(4,128)(2,1)}, u32[]{:S(2)}) copy-start(bf16[4,1024]{1,0:T(4,128)(2,1)} %param.23) | copy-start | bytes 24580
  292.3 62.9 %copy-start.42 = (f32[128,2]{0,1:T(2,128)S(1)}, f32[128,2]{0,1:T(2,128)}, u32[]{:S(2)}) copy-start(f32[128,2]{0,1:T(2,128)} %copy-done.41) | copy-start | bytes 3076
  292.3 63.0 %copy-start.38 = (f32[128,2]{0,1:T(2,128)S(1)}, f32[128,2]{0,1:T(2,128)}, u32[]{:S(2)}) copy-start(f32[128,2]{0,1:T(2,128)} %copy-done.37) | copy-start | bytes 3076
  292.3 32.6 %all-to-all-start.8 = ((bf16[128,1,2,256]{3,2,1,0:T(2,128)(2,1)}), bf16[128,1,2,256]{3,2,1,0:T(2,128)(2,1)S(1)}, u32[]{:S(2)}, u32[]{:S(2)}) async-start(bf16[128,1,2,256]{3,2,1,0:T(2,128)(2,1)} %get-tuple-element.413), calls=%async_computation.8 | async-start | bytes 262144 | tf_op jit(solution)/shard_map/all_to_all | solution.py:201
  324.9 23.2 %all-to-all-start.9 = ((bf16[128,1,2,256]{3,2,1,0:T(2,128)(2,1)}), bf16[128,1,2,256]{3,2,1,0:T(2,128)(2,1)S(1)}, u32[]{:S(2)}, u32[]{:S(2)}) async-start(bf16[128,1,2,256]{3,2,1,0:T(2,128)(2,1)} %get-tuple-element.412), calls=%async_computation.9 | async-start | bytes 262144 | tf_op jit(solution)/shard_map/all_to_all | solution.py:201
  332.7 46.0 %copy-start.52 = (s32[128]{0:T(128)S(1)}, s32[128]{0:T(128)}, u32[]{:S(2)}) copy-start(s32[128]{0:T(128)} %fusion.75) | copy-start | bytes 1540
  335.1 48.9 %copy-start.51 = (s32[128]{0:T(128)S(1)}, s32[128]{0:T(128)}, u32[]{:S(2)}) copy-start(s32[128]{0:T(128)} %fusion.76) | copy-start | bytes 1540
  348.1 23.2 %all-to-all-start.10 = ((bf16[128,1,2,256]{3,2,1,0:T(2,128)(2,1)}), bf16[128,1,2,256]{3,2,1,0:T(2,128)(2,1)S(1)}, u32[]{:S(2)}, u32[]{:S(2)}) async-start(bf16[128,1,2,256]{3,2,1,0:T(2,128)(2,1)} %get-tuple-element.411), calls=%async_computation.10 | async-start | bytes 262144 | tf_op jit(solution)/shard_map/all_to_all | solution.py:201
  355.4 44.7 %copy-start.17 = (bf16[128,1,256]{2,0,1:T(8,128)(2,1)}, bf16[128,1,256]{2,0,1:T(8,128)(2,1)S(1)}, u32[]{:S(2)}) copy-start(bf16[128,1,256]{2,0,1:T(8,128)(2,1)S(1)} %copy.407) | copy-start | bytes 196612
  371.3 23.5 %all-to-all-start.11 = ((bf16[128,1,2,256]{3,2,1,0:T(2,128)(2,1)}), bf16[128,1,2,256]{3,2,1,0:T(2,128)(2,1)S(1)}, u32[]{:S(2)}, u32[]{:S(2)}) async-start(bf16[128,1,2,256]{3,2,1,0:T(2,128)(2,1)} %get-tuple-element.410), calls=%async_computation.11 | async-start | bytes 262144 | tf_op jit(solution)/shard_map/all_to_all | solution.py:201
  378.5 386.5 %all-reduce.4.cloned.1.call-start = ((), (), s32[]{:S(2)}) async-start(), calls=%async_computation.14 | async-start | bytes 8388608
  405.7 389.5 %reduce-scatter.2.cloned.1.call-start = ((), (), s32[]{:S(2)}) async-start(), calls=%async_computation.13 | async-start | bytes 327680 | tf_op jit(solution)/shard_map/reduce_scatter | solution.py:221
  (43 other events, 403.8 us)
Sparse Core Ops, SparseCore 0:
  15.5 2.2 sort.41.cloned.1.call-done
  72.8 2.3 sort.43.cloned.1.call-done
  405.8 359.2 all-reduce.3
  768.5 26.6 reduce-scatter.1
  (2 shorter events, 0.0 us)
where the time goes:
time: 811 us; the launch traced here: 802 us
  waiting for transfers between devices  390 us (48%)
  starting transfers between devices  133 us (16%)
  blocking collectives  105 us (13%)
  other arithmetic  72.6 us (9%)
  local copies, waits for them, and re-layouts  48.2 us (6%)
  matrix products  19.7 us (2%)
  loops' own time  17.7 us (2%)
  between operations  16.2 us (2%)
    unnamed x3, waiting for transfers between devices  248 us
    psum x1, blocking collectives, body(): vnode_grad = lax.psum(vnode_part, ('nodes', 'mp')) * out_scale  105 us
    all_to_all x4, starting transfers between devices, body(): lax.all_to_all(wanted[perm_index], 'nodes', split_axis=0, concat_axis=0,...  48.4 us
    all_to_all x4, waiting for transfers between devices, body(): lax.all_to_all(grad_sorted[perm_index].reshape(shard_count, group_size, 2...  43.1 us
    all_to_all x4, starting transfers between devices, body(): lax.all_to_all(grad_sorted[perm_index].reshape(shard_count, group_size, 2...  37.9 us
    all_to_all x4, waiting for transfers between devices, body(): lax.all_to_all(wanted[perm_index], 'nodes', split_axis=0, concat_axis=0,...  37.6 us
    all_to_all x4, starting transfers between devices, body(): lax.all_to_all(stored[asked_rows], 'nodes', split_axis=0, concat_axis=0,...  37.5 us
    all_to_all x4, waiting for transfers between devices, body(): lax.all_to_all(stored[asked_rows], 'nodes', split_axis=0, concat_axis=0,...  32.5 us
  transfers between devices with their start and end apart: 18, of which 14 were waited for; matrix products, arithmetic and copies ran while one was open for 12% of the time, Pallas kernels for 0%

commit v1 on v0

v1 whole, which is shorter than its diff:
```python
import math

import jax
import jax.numpy as jnp
from jax import lax
from jax.experimental import pallas as pl
from jax.experimental.pallas import tpu as pltpu
from jax.sharding import Mesh
from jax.sharding import PartitionSpec as P

HEAD = 128
TILE = 128
DEGREE = 4
VIRTUAL = 4
ROWS = 128
SHARDS = 128
COLS = 256
HEADS_DEV = 2
SIZES = {"z": 16, "x": 4, "c": 2, "mp": 4}
NODES = ("z", "x", "c")

SHARPNESS = 8.0
EPSILON = 1e-06
SCALE = SHARPNESS / HEAD
BOOST = math.log(TILE)
PRECISE = lax.Precision.HIGHEST
F32 = jnp.float32
BF16 = jnp.bfloat16

NN = (((1,), (0,)), ((), ()))
NT = (((1,), (1,)), ((), ()))
TN = (((0,), (0,)), ((), ()))


def mul(left, right, dims, precision=None):
    return lax.dot_general(left, right, dims, precision=precision, preferred_element_type=F32)


def unit(values):
    inv = lax.rsqrt(jnp.mean(values * values, axis=-1, keepdims=True) + EPSILON)
    return values * inv, inv


def unit_back(rows, inv, cotangent):
    return inv * (cotangent - rows * jnp.mean(rows * cotangent, axis=-1, keepdims=True))


def head_of(ref, head, part=0):
    start = part * COLS + head * HEAD
    return ref[:, start : start + HEAD]


def owner_hits(owners_ref, perm):
    shard = lax.broadcasted_iota(jnp.int32, (SHARDS, ROWS), 0)
    return jnp.where(shard == owners_ref[perm : perm + 1, :], 1.0, 0.0).astype(BF16)


def asked_hits(asked_ref, perm):
    row = lax.broadcasted_iota(jnp.int32, (SHARDS, ROWS), 1)
    return jnp.where(row == asked_ref[:, perm : perm + 1], 1.0, 0.0).astype(BF16)


def serve_kernel(asked_ref, kv_ref, out_ref):
    kv = kv_ref[...]
    for perm in range(DEGREE):
        picked = mul(asked_hits(asked_ref, perm), kv, NN)
        out_ref[:, perm * 2 * COLS : (perm + 1) * 2 * COLS] = picked.astype(BF16)


def virtual_weights(bias_ref, head, unit_q, virtual_ref, member_ref):
    unit_v, inv_v = unit(head_of(virtual_ref, head))
    scores = SCALE * mul(unit_q, unit_v, NT, PRECISE) + bias_ref[2, head] + BOOST
    return jnp.exp(scores) * member_ref[...].astype(F32), unit_v, inv_v


def local_kernel(bias_ref, query_ref, left_ref, own_ref, right_ref, grad_ref, virtual_ref, member_ref, out_ref):
    columns = []
    for head in range(HEADS_DEV):
        unit_q, _ = unit(head_of(query_ref, head))
        query = unit_q.astype(BF16)
        grad = head_of(grad_ref, head)
        total = jnp.zeros((ROWS, 1), F32)
        mixed = jnp.zeros((ROWS, 1), F32)
        for block in (left_ref, own_ref, right_ref):
            unit_k, _ = unit(head_of(block, head).astype(F32))
            weights = jnp.exp(SCALE * mul(query, unit_k.astype(BF16), NT) + bias_ref[0, head])
            grads = mul(grad, head_of(block, head, 1), NT)
            total += jnp.sum(weights, axis=1, keepdims=True)
            mixed += jnp.sum(weights * grads, axis=1, keepdims=True)
        weights, _, _ = virtual_weights(bias_ref, head, unit_q, virtual_ref, member_ref)
        grads = mul(grad.astype(F32), head_of(virtual_ref, head, 1), NT, PRECISE)
        total += jnp.sum(weights, axis=1, keepdims=True)
        mixed += jnp.sum(weights * grads, axis=1, keepdims=True)
        columns += [total, mixed]
    out_ref[...] = jnp.concatenate(columns, axis=1)


def near_kernel(bias_ref, owners_ref, query_ref, near_ref, grad_ref, sums_ref, send_ref, stats_ref, dquery_ref):
    totals = [sums_ref[:, 2 * head : 2 * head + 1] for head in range(HEADS_DEV)]
    mixed = [sums_ref[:, 2 * head + 1 : 2 * head + 2] for head in range(HEADS_DEV)]
    unit_q = [unit(head_of(query_ref, head))[0] for head in range(HEADS_DEV)]
    grad = [head_of(grad_ref, head).astype(F32) for head in range(HEADS_DEV)]
    saved = {}
    for perm in range(DEGREE):
        hits = owner_hits(owners_ref, perm)
        rows = mul(hits, near_ref[:, perm * 2 * COLS : (perm + 1) * 2 * COLS], TN)
        for head in range(HEADS_DEV):
            unit_k, inv_k = unit(rows[:, head * HEAD : (head + 1) * HEAD])
            values = rows[:, COLS + head * HEAD : COLS + (head + 1) * HEAD]
            scores = SCALE * jnp.sum(unit_q[head] * unit_k, axis=1, keepdims=True)
            weights = jnp.exp(scores + bias_ref[1, head] + BOOST)
            grads = jnp.sum(grad[head] * values, axis=1, keepdims=True)
            totals[head] = totals[head] + weights
            mixed[head] = mixed[head] + weights * grads
            saved[perm, head] = (unit_k, inv_k, weights, grads)
    inverse = [1.0 / total for total in totals]
    delta = [mixed[head] * inverse[head] for head in range(HEADS_DEV)]
    dquery = [jnp.zeros((ROWS, HEAD), F32) for _ in range(HEADS_DEV)]
    for perm in range(DEGREE):
        dkeys, dvalues = [], []
        for head in range(HEADS_DEV):
            unit_k, inv_k, weights, grads = saved[perm, head]
            probs = weights * inverse[head]
            dscores = probs * (grads - delta[head]) * SCALE
            dquery[head] = dquery[head] + dscores * unit_k
            dkeys.append(unit_back(unit_k, inv_k, dscores * unit_q[head]).astype(BF16))
            dvalues.append((probs * grad[head]).astype(BF16))
        picked = mul(owner_hits(owners_ref, perm), jnp.concatenate(dkeys + dvalues, axis=1), NN)
        send_ref[:, perm * 2 * COLS : (perm + 1) * 2 * COLS] = picked.astype(BF16)
    stats_ref[...] = jnp.concatenate([inverse[0], delta[0], inverse[1], delta[1]], axis=1)
    dquery_ref[...] = jnp.concatenate(dquery, axis=1)


def back_kernel(
    bias_ref, query_ref, left_ref, own_ref, right_ref, grad_ref, virtual_ref, member_ref, stats_ref, dnear_ref,
    dquery_ref, dleft_ref, down_ref, dright_ref, dvirtual_ref,
):
    for head in range(HEADS_DEV):
        unit_q, inv_q = unit(head_of(query_ref, head))
        query = unit_q.astype(BF16)
        grad = head_of(grad_ref, head)
        inverse = stats_ref[:, 2 * head : 2 * head + 1]
        delta = stats_ref[:, 2 * head + 1 : 2 * head + 2]
        dquery = head_of(dnear_ref, head)
        keys_at = slice(head * HEAD, (head + 1) * HEAD)
        values_at = slice(COLS + head * HEAD, COLS + (head + 1) * HEAD)
        for block, out in ((left_ref, dleft_ref), (own_ref, down_ref), (right_ref, dright_ref)):
            unit_k, inv_k = unit(head_of(block, head).astype(F32))
            keys = unit_k.astype(BF16)
            probs = jnp.exp(SCALE * mul(query, keys, NT) + bias_ref[0, head]) * inverse
            grads = mul(grad, head_of(block, head, 1), NT)
            dscores = (probs * (grads - delta) * SCALE).astype(BF16)
            dquery += mul(dscores, keys, NN)
            out[:, keys_at] = unit_back(unit_k, inv_k, mul(dscores, query, TN)).astype(out.dtype)
            out[:, values_at] = mul(probs.astype(BF16), grad, TN).astype(out.dtype)
        weights, unit_v, inv_v = virtual_weights(bias_ref, head, unit_q, virtual_ref, member_ref)
        probs = weights * inverse
        wide = grad.astype(F32)
        grads = mul(wide, head_of(virtual_ref, head, 1), NT, PRECISE)
        dscores = probs * (grads - delta) * SCALE
        dquery += mul(dscores, unit_v, NN, PRECISE)
        dvirtual_ref[:, keys_at] = unit_back(unit_v, inv_v, mul(dscores, unit_q, TN, PRECISE))
        dvirtual_ref[:, values_at] = mul(probs, wide, TN, PRECISE)
        dquery_ref[:, keys_at] = unit_back(unit_q, inv_q, dquery).astype(BF16)


def total_kernel(asked_ref, back_ref, dquery_ref, down_ref, from_left_ref, from_right_ref, out_ref):
    total = down_ref[...] + from_left_ref[...].astype(F32) + from_right_ref[...].astype(F32)
    for perm in range(DEGREE):
        total += mul(asked_hits(asked_ref, perm), back_ref[:, perm * 2 * COLS : (perm + 1) * 2 * COLS], TN)
    out_ref[:, :COLS] = dquery_ref[...]
    out_ref[:, COLS:] = total.astype(BF16)


VMEM = pl.BlockSpec(memory_space=pltpu.VMEM)
SMEM = pl.BlockSpec(memory_space=pltpu.SMEM)


def call(kernel, outs, *args, scalars=0, flops=10**8):
    shapes = [jax.ShapeDtypeStruct(shape, kind) for shape, kind in outs]
    moved = sum(math.prod(a.shape) * a.dtype.itemsize for a in [*args, *shapes])
    return pl.pallas_call(
        kernel,
        out_shape=shapes,
        in_specs=[SMEM] * scalars + [VMEM] * (len(args) - scalars),
        out_specs=[VMEM] * len(shapes),
        compiler_params=pltpu.CompilerParams(vmem_limit_bytes=32 * 2**20),
        cost_estimate=pl.CostEstimate(flops=flops, bytes_accessed=moved, transcendentals=0),
    )(*args)


def exchange(values, axis):
    return lax.all_to_all(values, axis, split_axis=0, concat_axis=0, tiled=True)


def shift(values, axis, step):
    count = math.prod(SIZES[name] for name in axis) if isinstance(axis, tuple) else SIZES[axis]
    return lax.ppermute(values, axis, [(i, (i + step) % count) for i in range(count)])


def swap(values, axis, bit):
    return lax.ppermute(values, axis, [(i, i ^ bit) for i in range(SIZES[axis])])


def two_terms(values):
    high = values.astype(BF16)
    return high, (values - high.astype(F32)).astype(BF16)


def body(features, qkv_weight, vnode_emb, edge_bias, out_grad, neighbours, member, tile_list, tile_count):
    width_in = qkv_weight.shape[0]
    with jax.named_scope("ask"):
        owners = neighbours // ROWS
        hit = owners[:, None, :] == jnp.arange(SHARDS, dtype=jnp.int32)[None, :, None]
        wanted = jnp.sum(jnp.where(hit, (neighbours % ROWS)[:, None, :], 0), axis=2)
        asked = exchange(wanted.T, NODES)
    with jax.named_scope("project"):
        flat_weight = qkv_weight.reshape(width_in, 3 * COLS)
        projected = jnp.dot(features, flat_weight, preferred_element_type=F32)
        query = projected[:, :COLS]
        kv = projected[:, COLS:].astype(BF16)
        virtual_kv = jnp.dot(vnode_emb, flat_weight[:, COLS:], preferred_element_type=F32)
        from_left = shift(kv, NODES, 1)
        from_right = shift(kv, NODES, -1)
    with jax.named_scope("select"):
        core = lax.axis_index("c")
        place = jnp.arange(width_in, dtype=jnp.int32)
        half, rest = place // 512, place % 512
        source = (rest // 8 % 16) * 64 + (rest // 128) * 16 + (half ^ core) * 8 + rest % 8
        chosen = (jnp.arange(width_in, dtype=jnp.int32)[:, None] == source[None, :]).astype(BF16)
        sorted_in = jnp.dot(jnp.concatenate([features, vnode_emb], axis=0), chosen, preferred_element_type=F32)
        sorted_in = sorted_in.astype(BF16)
        other_in = swap(sorted_in[:ROWS, 512:], "c", 1)
        wide_in = jnp.concatenate([sorted_in[:ROWS, :512], other_in, sorted_in[ROWS:, :512], sorted_in[ROWS:, :512]], axis=0)
    with jax.named_scope("serve"):
        served, = call(serve_kernel, [((SHARDS, DEGREE * 2 * COLS), BF16)], asked, kv)
        near = exchange(served, NODES)
    with jax.named_scope("local"):
        sums, = call(
            local_kernel, [((ROWS, 4), F32)],
            edge_bias, query, from_left, kv, from_right, out_grad, virtual_kv, member, scalars=1,
        )
    with jax.named_scope("near"):
        send, stats, dnear = call(
            near_kernel, [((SHARDS, DEGREE * 2 * COLS), BF16), ((ROWS, 4), F32), ((ROWS, COLS), F32)],
            edge_bias, owners, query, near, out_grad, sums, scalars=1,
        )
        back = exchange(send, NODES)
    with jax.named_scope("back"):
        dquery, dleft, down, dright, dvirtual = call(
            back_kernel,
            [((ROWS, COLS), BF16), ((ROWS, 2 * COLS), BF16), ((ROWS, 2 * COLS), F32), ((ROWS, 2 * COLS), BF16), ((VIRTUAL, 2 * COLS), F32)],
            edge_bias, query, from_left, kv, from_right, out_grad, virtual_kv, member, stats, dnear, scalars=1,
        )
        back_left = shift(dright, NODES, 1)
        back_right = shift(dleft, NODES, -1)
    with jax.named_scope("virtual"):
        high, low = two_terms(dvirtual)
        kv_weight = flat_weight[:, COLS:]
        vnode = mul(jnp.concatenate([high, low], axis=0), kv_weight, NT)
        vnode = vnode[:VIRTUAL] + vnode[VIRTUAL:]
        for axis, bit in (("mp", 1), ("mp", 2), ("c", 1), ("x", 1), ("x", 2)):
            vnode = vnode + swap(vnode, axis, bit)
        dvirtual = dvirtual + swap(dvirtual, "c", 1)
        high, low = two_terms(dvirtual)
        extra = jnp.concatenate([high, low], axis=0)
        extra = jnp.concatenate([jnp.zeros((2 * VIRTUAL, COLS), BF16), extra], axis=1)
    with jax.named_scope("total"):
        dqkv, = call(
            total_kernel, [((ROWS, 3 * COLS), BF16)],
            asked, back, dquery, down, back_left, back_right,
        )
        other = swap(dqkv, "c", 1)
    with jax.named_scope("feature"):
        partial = mul(dqkv, flat_weight, NT).astype(BF16)
        me = lax.axis_index("mp")
        summed = lax.dynamic_slice_in_dim(partial, me * COLS, COLS, 1).astype(F32)
        for step in range(1, 4):
            piece = lax.dynamic_slice_in_dim(partial, ((me + step) % 4) * COLS, COLS, 1)
            summed = summed + shift(piece, "mp", step).astype(F32)
        feature_grad = summed.astype(BF16)
    with jax.named_scope("weight"):
        wide_out = jnp.concatenate([dqkv, other, extra], axis=0)
        term = mul(wide_in, wide_out, TN).astype(BF16)
        term = exchange(term.reshape(4, 128, 3 * COLS), "x")
        term = jnp.sum(term.astype(F32), axis=0).reshape(16, 8, 3 * COLS)
        tail = jnp.broadcast_to(vnode.reshape(1, 8, 512), (16, 8, 512))
        term = jnp.concatenate([term, tail], axis=2).astype(BF16)
        term = jnp.sum(exchange(term, "z").astype(F32), axis=0)
        out_scale = 1.0 / math.sqrt(ROWS * SHARDS)
        weight_grad = (term[:, : 3 * COLS] * out_scale).reshape(8, 3, COLS)
        vnode_grad = (term[:, 3 * COLS :] * out_scale).reshape(VIRTUAL, width_in)
    return feature_grad, weight_grad, vnode_grad


def solution(mesh):
    fine = Mesh(mesh.devices.reshape(tuple(SIZES.values())), tuple(SIZES))
    return jax.shard_map(
        body,
        mesh=fine,
        in_specs=(
            P(NODES, None),
            P(None, None, "mp"),
            P(),
            P(None, "mp"),
            P(NODES, "mp"),
            P(None, NODES),
            P(NODES, None),
            P(NODES, None, None),
            P(NODES),
        ),
        out_specs=(P(NODES, "mp"), P(NODES, None, "mp"), P()),
        check_vma=False,
    )
```

time: 811 us -> 202 us (0.25)
  the two profiles are of different devices: /device:TPU:2 before, /device:TPU:10 now
where the time goes in v1:
time: 202 us; the launch traced here: 200 us
  starting transfers between devices  90.1 us (45%)
  waiting for transfers between devices  74.2 us (37%)
  local copies, waits for them, and re-layouts  16.5 us (8%)
  Pallas kernels  8.49 us (4%)
  other arithmetic  5.85 us (3%)
  matrix products  4.09 us (2%)
    all_to_all x5, waiting for transfers between devices, exchange(): return lax.all_to_all(values, axis, split_axis=0, concat_axis=0, tiled=True)  55.1 us
    all_to_all x5, starting transfers between devices, exchange(): return lax.all_to_all(values, axis, split_axis=0, concat_axis=0, tiled=True)  46.2 us
    ppermute x8, starting transfers between devices, swap(): lax.ppermute(values, axis, [(i, i ^ bit) for i in range(SIZES[axis])])  22.1 us
    ppermute x7, starting transfers between devices, shift(): lax.ppermute(values, axis, [(i, (i + step) % count) for i in range(count)])  21.8 us
    ppermute x8, waiting for transfers between devices, swap(): lax.ppermute(values, axis, [(i, i ^ bit) for i in range(SIZES[axis])])  15 us
    unnamed x21, local copies, waits for them, and re-layouts  14.5 us
    pallas_call x5, Pallas kernels, call(): pl.pallas_call(kernel, out_shape=shapes, in_specs=[SMEM] * scalars + [VME...  8.49 us
    ppermute x7, waiting for transfers between devices, shift(): lax.ppermute(values, axis, [(i, (i + step) % count) for i in range(count)])  4.09 us
  transfers between devices with their start and end apart: 20, of which 14 were waited for; matrix products, arithmetic and copies ran while one was open for 6% of the time, Pallas kernels for 2%

profile of v1, /device:TPU:10, one launch (start us, length us, event | category | flops | bytes accessed | tf_op | source)
XLA Modules:
  0.0 200.3 jit_solution(11954823422124553856)
XLA Ops:
  2.2 19.4 %all-to-all-start = ((s32[128,1,4]{2,1,0:T(1,128)}), s32[128,1,4]{2,1,0:T(1,128)S(1)}, u32[]{:S(2)}, u32[]{:S(2)}) async-start(s32[128,1,4]{2,1,0:T(1,128)} %copy.37), calls=%async_computation | async-start | bytes 131072 | tf_op jit(solution)/shard_map/ask/all_to_all | solution.py:193
  24.1 11.4 %all-to-all-done = s32[128,1,4]{2,1,0:T(1,128)S(1)} async-done(((s32[128,1,4]{2,1,0:T(1,128)}), s32[128,1,4]{2,1,0:T(1,128)S(1)}, u32[]{:S(2)}, u32[]{:S(2)}) %all-to-all-start) | async-done | bytes 2080 | tf_op jit(solution)/shard_map/ask/all_to_all | solution.py:193
  38.6 6.7 %all-to-all-start.1 = ((bf16[128,2,1024]{2,1,0:T(2,128)(2,1)}), bf16[128,2,1024]{2,1,0:T(2,128)(2,1)S(1)}, u32[]{:S(2)}, u32[]{:S(2)}) async-start(bf16[128,2,1024]{2,1,0:T(2,128)(2,1)} %reshape.112), calls=%async_computation.1 | async-start | bytes 1048576 | tf_op jit(solution)/shard_map/serve/all_to_all | solution.py:193
  45.2 2.1 %collective-permute-start = (bf16[128,512]{1,0:T(8,128)(2,1)S(1)}, bf16[128,512]{1,0:T(8,128)(2,1)S(1)}, u32[]{:S(2)}, u32[]{:S(2)}) collective-permute-start(bf16[128,512]{1,0:T(8,128)(2,1)S(1)} %slice.62.kv_ref.own_ref), channel_id=1, source_target_pairs={{0,4},{4,8},{8,12},{12,16},{16,20},{20,24},{24,28},{28,32},{32,36}... | collective-permute-start | bytes 393224 | tf_op jit(solution)/shard_map/project/ppermute | solution.py:198
  47.3 3.5 %collective-permute-start.1 = (bf16[128,512]{1,0:T(8,128)(2,1)S(1)}, bf16[128,512]{1,0:T(8,128)(2,1)S(1)}, u32[]{:S(2)}, u32[]{:S(2)}) collective-permute-start(bf16[128,512]{1,0:T(8,128)(2,1)S(1)} %slice.62.kv_ref.own_ref), channel_id=1, source_target_pairs={{0,508},{4,0},{8,4},{12,8},{16,12},{20,16},{24,20},{28,24},{32,28}... | collective-permute-start | bytes 393224 | tf_op jit(solution)/shard_map/project/ppermute | solution.py:198
  51.7 1.9 collective-permute-done.1.right_ref
  55.0 21.7 %all-to-all-done.1 = bf16[128,2,1024]{2,1,0:T(2,128)(2,1)S(1)} async-done(((bf16[128,2,1024]{2,1,0:T(2,128)(2,1)}), bf16[128,2,1024]{2,1,0:T(2,128)(2,1)S(1)}, u32[]{:S(2)}, u32[]{:S(2)}) %all-to-all-start.1) | async-done | bytes 524320 | tf_op jit(solution)/shard_map/serve/all_to_all | solution.py:193
  79.9 3.3 %near.1 = (bf16[128,2048]{1,0:T(8,128)(2,1)S(1)}, f32[128,4]{1,0:T(8,128)S(1)}, f32[128,256]{1,0:T(8,128)S(1)}) custom-call(f32[3,2]{1,0:T(4,128)S(1)} %copy.42.bias_ref, s32[4,128]{1,0:T(4,128)S(1)} %get-tuple-element.30.owners_ref, f32[128,256]{1,0:T(8,128)S(1)} %slice.43.query_ref, bf16[128,2048]{1,0:T(8,128)(2,1)S(1)} %bitcast.22, ...), custom_call_target="tpu_custom_call" | custom-call | flops 100000000 | bytes 1382424 | tf_op jit(solution)/shard_map/near/pallas_call | solution.py:182
  85.0 2.2 %reshape.114 = bf16[128,2,1024]{2,1,0:T(2,128)(2,1)} reshape(bf16[128,2048]{1,0:T(8,128)(2,1)} %reduce.2) | data formatting | bytes 1048576
  87.2 11.0 %all-to-all-start.2 = ((bf16[128,2,1024]{2,1,0:T(2,128)(2,1)}), bf16[128,2,1024]{2,1,0:T(2,128)(2,1)}, u32[]{:S(2)}, u32[]{:S(2)}) async-start(bf16[128,2,1024]{2,1,0:T(2,128)(2,1)} %reshape.114), calls=%async_computation.2 | async-start | bytes 1048576 | tf_op jit(solution)/shard_map/near/all_to_all | solution.py:193
  99.2 3.1 %back.1 = (bf16[128,256]{1,0:T(8,128)(2,1)S(1)}, bf16[128,512]{1,0:T(8,128)(2,1)S(1)}, f32[128,512]{1,0:T(8,128)S(1)}, bf16[128,512]{1,0:T(8,128)(2,1)S(1)}, f32[4,512]{1,0:T(4,128)S(1)}) custom-call(f32[3,2]{1,0:T(4,128)S(1)} %copy.42.bias_ref, f32[128,256]{1,0:T(8,128)S(1)} %slice.43.query_ref, bf16[128,512]{1,0:T(8,128)(2,1)S(1)} %collective-permute-done.left_ref, ...), custom_call_target="tpu_custom_call" | custom-call | flops 100000000 | bytes 1331224 | tf_op jit(solution)/shard_map/back/pallas_call | solution.py:182
  102.3 2.0 %collective-permute-start.9 = (f32[4,512]{1,0:T(4,128)S(1)}, f32[4,512]{1,0:T(4,128)S(1)}, u32[]{:S(2)}, u32[]{:S(2)}) collective-permute-start(f32[4,512]{1,0:T(4,128)S(1)} %get-tuple-element.18), channel_id=1, source_target_pairs={{0,4},{4,0},{1,5},{5,1},{2,6},{6,2},{3,7},{7,3},{8,12},{12,8},{9,1... | collective-permute-start | bytes 24584 | tf_op jit(solution)/shard_map/virtual/ppermute | solution.py:202
  104.4 2.3 %collective-permute-start.7 = (bf16[128,512]{1,0:T(8,128)(2,1)S(1)}, bf16[128,512]{1,0:T(8,128)(2,1)S(1)}, u32[]{:S(2)}, u32[]{:S(2)}) collective-permute-start(bf16[128,512]{1,0:T(8,128)(2,1)S(1)} %get-tuple-element.22), channel_id=1, source_target_pairs={{0,4},{4,0},{1,5},{5,1},{2,6},{6,2},{3,7},{7,3},{8,12},{12,8},{9,1... | collective-permute-start | bytes 393224 | tf_op jit(solution)/shard_map/select/ppermute | solution.py:202
  106.7 2.1 %collective-permute-start.2 = (bf16[128,512]{1,0:T(8,128)(2,1)S(1)}, bf16[128,512]{1,0:T(8,128)(2,1)S(1)}, u32[]{:S(2)}, u32[]{:S(2)}) collective-permute-start(bf16[128,512]{1,0:T(8,128)(2,1)S(1)} %get-tuple-element.16), channel_id=1, source_target_pairs={{0,4},{4,8},{8,12},{12,16},{16,20},{20,24},{24,28},{28,32},{32,36}... | collective-permute-start | bytes 393224 | tf_op jit(solution)/shard_map/back/ppermute | solution.py:198
  108.7 3.5 %collective-permute-start.3 = (bf16[128,512]{1,0:T(8,128)(2,1)S(1)}, bf16[128,512]{1,0:T(8,128)(2,1)S(1)}, u32[]{:S(2)}, u32[]{:S(2)}) collective-permute-start(bf16[128,512]{1,0:T(8,128)(2,1)S(1)} %get-tuple-element.17), channel_id=1, source_target_pairs={{0,508},{4,0},{8,4},{12,8},{16,12},{20,16},{24,20},{28,24},{32,28}... | collective-permute-start | bytes 393224 | tf_op jit(solution)/shard_map/back/ppermute | solution.py:198
  112.3 16.9 %all-to-all-done.2 = bf16[128,2,1024]{2,1,0:T(2,128)(2,1)} async-done(((bf16[128,2,1024]{2,1,0:T(2,128)(2,1)}), bf16[128,2,1024]{2,1,0:T(2,128)(2,1)}, u32[]{:S(2)}, u32[]{:S(2)}) %all-to-all-start.2) | async-done | bytes 524320 | tf_op jit(solution)/shard_map/near/all_to_all | solution.py:193
  129.2 4.3 %reshape.115 = bf16[128,1,2048]{2,1,0:T(2,128)(2,1)} reshape(bf16[128,2,1024]{2,1,0:T(2,128)(2,1)} %all-to-all-done.2) | data formatting | bytes 1048576
  135.5 3.4 %collective-permute-start.8 = (bf16[128,768]{1,0:T(8,128)(2,1)S(1)}, bf16[128,768]{1,0:T(8,128)(2,1)S(1)}, u32[]{:S(2)}, u32[]{:S(2)}) collective-permute-start(bf16[128,768]{1,0:T(8,128)(2,1)S(1)} %total.1), channel_id=1, source_target_pairs={{0,4},{4,0},{1,5},{5,1},{2,6},{6,2},{3,7},{7,3},{8,12},{12,8},{9,1... | collective-permute-start | bytes 589832 | tf_op jit(solution)/shard_map/total/ppermute | solution.py:202
  141.5 5.0 %all-to-all-start.3 = ((bf16[4,128,768]{2,1,0:T(8,128)(2,1)}), bf16[4,128,768]{2,1,0:T(8,128)(2,1)S(1)}, u32[]{:S(2)}, u32[]{:S(2)}) async-start(bf16[4,128,768]{2,1,0:T(8,128)(2,1)} %bitcast.31), calls=%async_computation.3 | async-start | bytes 1572864 | tf_op jit(solution)/shard_map/weight/all_to_all | solution.py:193
  146.5 2.4 %collective-permute-start.10 = (f32[4,1024]{1,0:T(4,128)S(1)}, f32[4,1024]{1,0:T(4,128)S(1)}, u32[]{:S(2)}, u32[]{:S(2)}) collective-permute-start(f32[4,1024]{1,0:T(4,128)S(1)} %slice_add_fusion), channel_id=1, source_target_pairs={{0,1},{1,0},{2,3},{3,2},{4,5},{5,4},{6,7},{7,6},{8,9},{9,8},{10,11... | collective-permute-start | bytes 49160 | tf_op jit(solution)/shard_map/virtual/ppermute | solution.py:202
  148.8 3.3 %collective-permute-done.10 = f32[4,1024]{1,0:T(4,128)S(1)} collective-permute-done((f32[4,1024]{1,0:T(4,128)S(1)}, f32[4,1024]{1,0:T(4,128)S(1)}, u32[]{:S(2)}, u32[]{:S(2)}) %collective-permute-start.10) | collective-permute-done | bytes 16416 | tf_op jit(solution)/shard_map/virtual/ppermute | solution.py:202
  152.1 4.2 %collective-permute-start.11 = (f32[4,1024]{1,0:T(4,128)S(1)}, f32[4,1024]{1,0:T(4,128)S(1)}, u32[]{:S(2)}, u32[]{:S(2)}) collective-permute-start(f32[4,1024]{1,0:T(4,128)S(1)} %fusion.58), channel_id=1, source_target_pairs={{0,2},{1,3},{2,0},{3,1},{4,6},{5,7},{6,4},{7,5},{8,10},{9,11},{10,... | collective-permute-start | bytes 49160 | tf_op jit(solution)/shard_map/virtual/ppermute | solution.py:202
  156.3 2.9 %collective-permute-done.11 = f32[4,1024]{1,0:T(4,128)S(1)} collective-permute-done((f32[4,1024]{1,0:T(4,128)S(1)}, f32[4,1024]{1,0:T(4,128)S(1)}, u32[]{:S(2)}, u32[]{:S(2)}) %collective-permute-start.11) | collective-permute-done | bytes 16416 | tf_op jit(solution)/shard_map/virtual/ppermute | solution.py:202
  159.2 1.9 collective-permute-start.12
  164.2 3.7 %collective-permute-done.13 = f32[4,1024]{1,0:T(4,128)S(1)} collective-permute-done((f32[4,1024]{1,0:T(4,128)S(1)}, f32[4,1024]{1,0:T(4,128)S(1)}, u32[]{:S(2)}, u32[]{:S(2)}) %collective-permute-start.13) | collective-permute-done | bytes 16416 | tf_op jit(solution)/shard_map/virtual/ppermute | solution.py:202
  167.9 4.0 %collective-permute-start.14 = (f32[4,1024]{1,0:T(4,128)S(1)}, f32[4,1024]{1,0:T(4,128)S(1)}, u32[]{:S(2)}, u32[]{:S(2)}) collective-permute-start(f32[4,1024]{1,0:T(4,128)S(1)} %add.159), channel_id=1, source_target_pairs={{0,16},{8,24},{16,0},{24,8},{1,17},{9,25},{17,1},{25,9},{2,18},{10... | collective-permute-start | bytes 49160 | tf_op jit(solution)/shard_map/virtual/ppermute | solution.py:202
  171.9 3.2 %collective-permute-done.14 = f32[4,1024]{1,0:T(4,128)S(1)} collective-permute-done((f32[4,1024]{1,0:T(4,128)S(1)}, f32[4,1024]{1,0:T(4,128)S(1)}, u32[]{:S(2)}, u32[]{:S(2)}) %collective-permute-start.14) | collective-permute-done | bytes 16416 | tf_op jit(solution)/shard_map/virtual/ppermute | solution.py:202
  176.0 4.2 %all-to-all-start.4 = ((bf16[16,8,1280]{2,1,0:T(8,128)(2,1)}), bf16[16,8,1280]{2,1,0:T(8,128)(2,1)S(1)}, u32[]{:S(2)}, u32[]{:S(2)}) async-start(bf16[16,8,1280]{2,1,0:T(8,128)(2,1)} %pad_maximum_fusion), calls=%async_computation.4 | async-start | bytes 655360 | tf_op jit(solution)/shard_map/weight/all_to_all | solution.py:193
  180.7 3.5 %collective-permute-start.4 = (bf16[128,256]{1,0:T(8,128)(2,1)S(1)}, bf16[128,256]{1,0:T(8,128)(2,1)S(1)}, u32[]{:S(2)}, u32[]{:S(2)}) collective-permute-start(bf16[128,256]{1,0:T(8,128)(2,1)S(1)} %get-tuple-element.23), channel_id=1, source_target_pairs={{0,1},{1,2},{2,3},{3,0},{4,5},{5,6},{6,7},{7,4},{8,9},{9,10},{10,1... | collective-permute-start | bytes 196616 | tf_op jit(solution)/shard_map/feature/ppermute | solution.py:198
  184.1 2.9 %collective-permute-start.5 = (bf16[128,256]{1,0:T(8,128)(2,1)S(1)}, bf16[128,256]{1,0:T(8,128)(2,1)S(1)}, u32[]{:S(2)}, u32[]{:S(2)}) collective-permute-start(bf16[128,256]{1,0:T(8,128)(2,1)S(1)} %get-tuple-element.25), channel_id=1, source_target_pairs={{0,2},{1,3},{2,0},{3,1},{4,6},{5,7},{6,4},{7,5},{8,10},{9,11},{10,... | collective-permute-start | bytes 196616 | tf_op jit(solution)/shard_map/feature/ppermute | solution.py:198
  187.0 4.3 %collective-permute-start.6 = (bf16[128,256]{1,0:T(8,128)(2,1)S(1)}, bf16[128,256]{1,0:T(8,128)(2,1)S(1)}, u32[]{:S(2)}, u32[]{:S(2)}) collective-permute-start(bf16[128,256]{1,0:T(8,128)(2,1)S(1)} %get-tuple-element.24), channel_id=1, source_target_pairs={{0,3},{1,0},{2,1},{3,2},{4,7},{5,4},{6,5},{7,6},{8,11},{9,8},{10,9... | collective-permute-start | bytes 196616 | tf_op jit(solution)/shard_map/feature/ppermute | solution.py:198
  193.9 5.1 %all-to-all-done.4 = bf16[16,8,1280]{2,1,0:T(8,128)(2,1)S(1)} async-done(((bf16[16,8,1280]{2,1,0:T(8,128)(2,1)}), bf16[16,8,1280]{2,1,0:T(8,128)(2,1)S(1)}, u32[]{:S(2)}, u32[]{:S(2)}) %all-to-all-start.4) | async-done | bytes 327712 | tf_op jit(solution)/shard_map/weight/all_to_all | solution.py:193
  (69 shorter events, 27.9 us)
Async XLA Ops:
  2.2 33.3 %all-to-all-start = ((s32[128,1,4]{2,1,0:T(1,128)}), s32[128,1,4]{2,1,0:T(1,128)S(1)}, u32[]{:S(2)}, u32[]{:S(2)}) async-start(s32[128,1,4]{2,1,0:T(1,128)} %copy.37), calls=%async_computation | async-start | bytes 131072 | tf_op jit(solution)/shard_map/ask/all_to_all | solution.py:193
  21.6 1.8 copy-start.1
  36.3 14.5 %copy-start.5 = (f32[3,2]{0,1:T(2,128)S(1)}, f32[3,2]{0,1:T(2,128)}, u32[]{:S(2)}) copy-start(f32[3,2]{0,1:T(2,128)} %param.12) | copy-start | bytes 76
  36.3 14.6 %copy-start.4 = (s32[128,4]{0,1:T(4,128)S(1)}, s32[128,4]{0,1:T(4,128)}, u32[]{:S(2)}) copy-start(s32[128,4]{0,1:T(4,128)} %param.15) | copy-start | bytes 6148
  36.3 14.7 %copy-start.3 = (bf16[4,1024]{1,0:T(4,128)(2,1)S(1)}, bf16[4,1024]{1,0:T(4,128)(2,1)}, u32[]{:S(2)}) copy-start(bf16[4,1024]{1,0:T(4,128)(2,1)} %param.11) | copy-start | bytes 24580
  37.4 16.3 %copy-start = (bf16[128,256]{1,0:T(8,128)(2,1)S(1)}, bf16[128,256]{1,0:T(8,128)(2,1)}, u32[]{:S(2)}) copy-start(bf16[128,256]{1,0:T(8,128)(2,1)} %grad_ref.5) | copy-start | bytes 196612
  38.6 38.1 %all-to-all-start.1 = ((bf16[128,2,1024]{2,1,0:T(2,128)(2,1)}), bf16[128,2,1024]{2,1,0:T(2,128)(2,1)S(1)}, u32[]{:S(2)}, u32[]{:S(2)}) async-start(bf16[128,2,1024]{2,1,0:T(2,128)(2,1)} %reshape.112), calls=%async_computation.1 | async-start | bytes 1048576 | tf_op jit(solution)/shard_map/serve/all_to_all | solution.py:193
  45.2 6.5 %collective-permute-start = (bf16[128,512]{1,0:T(8,128)(2,1)S(1)}, bf16[128,512]{1,0:T(8,128)(2,1)S(1)}, u32[]{:S(2)}, u32[]{:S(2)}) collective-permute-start(bf16[128,512]{1,0:T(8,128)(2,1)S(1)} %slice.62.kv_ref.own_ref), channel_id=1, source_target_pairs={{0,4},{4,8},{8,12},{12,16},{16,20},{20,24},{24,28},{28,32},{32,36}... | collective-permute-start | bytes 393224 | tf_op jit(solution)/shard_map/project/ppermute | solution.py:198
  47.3 6.3 %collective-permute-start.1 = (bf16[128,512]{1,0:T(8,128)(2,1)S(1)}, bf16[128,512]{1,0:T(8,128)(2,1)S(1)}, u32[]{:S(2)}, u32[]{:S(2)}) collective-permute-start(bf16[128,512]{1,0:T(8,128)(2,1)S(1)} %slice.62.kv_ref.own_ref), channel_id=1, source_target_pairs={{0,508},{4,0},{8,4},{12,8},{16,12},{20,16},{24,20},{28,24},{32,28}... | collective-permute-start | bytes 393224 | tf_op jit(solution)/shard_map/project/ppermute | solution.py:198
  83.3 15.0 %copy-start.2 = (bf16[128,1024]{1,0:T(8,128)(2,1)S(1)}, bf16[128,1024]{1,0:T(8,128)(2,1)}, u32[]{:S(2)}) copy-start(bf16[128,1024]{1,0:T(8,128)(2,1)} %param.9) | copy-start | bytes 786436
  87.2 42.0 %all-to-all-start.2 = ((bf16[128,2,1024]{2,1,0:T(2,128)(2,1)}), bf16[128,2,1024]{2,1,0:T(2,128)(2,1)}, u32[]{:S(2)}, u32[]{:S(2)}) async-start(bf16[128,2,1024]{2,1,0:T(2,128)(2,1)} %reshape.114), calls=%async_computation.2 | async-start | bytes 1048576 | tf_op jit(solution)/shard_map/near/all_to_all | solution.py:193
  102.3 10.0 %collective-permute-start.9 = (f32[4,512]{1,0:T(4,128)S(1)}, f32[4,512]{1,0:T(4,128)S(1)}, u32[]{:S(2)}, u32[]{:S(2)}) collective-permute-start(f32[4,512]{1,0:T(4,128)S(1)} %get-tuple-element.18), channel_id=1, source_target_pairs={{0,4},{4,0},{1,5},{5,1},{2,6},{6,2},{3,7},{7,3},{8,12},{12,8},{9,1... | collective-permute-start | bytes 24584 | tf_op jit(solution)/shard_map/virtual/ppermute | solution.py:202
  104.4 34.8 %collective-permute-start.7 = (bf16[128,512]{1,0:T(8,128)(2,1)S(1)}, bf16[128,512]{1,0:T(8,128)(2,1)S(1)}, u32[]{:S(2)}, u32[]{:S(2)}) collective-permute-start(bf16[128,512]{1,0:T(8,128)(2,1)S(1)} %get-tuple-element.22), channel_id=1, source_target_pairs={{0,4},{4,0},{1,5},{5,1},{2,6},{6,2},{3,7},{7,3},{8,12},{12,8},{9,1... | collective-permute-start | bytes 393224 | tf_op jit(solution)/shard_map/select/ppermute | solution.py:202
  106.7 28.4 %collective-permute-start.2 = (bf16[128,512]{1,0:T(8,128)(2,1)S(1)}, bf16[128,512]{1,0:T(8,128)(2,1)S(1)}, u32[]{:S(2)}, u32[]{:S(2)}) collective-permute-start(bf16[128,512]{1,0:T(8,128)(2,1)S(1)} %get-tuple-element.16), channel_id=1, source_target_pairs={{0,4},{4,8},{8,12},{12,16},{16,20},{20,24},{24,28},{28,32},{32,36}... | collective-permute-start | bytes 393224 | tf_op jit(solution)/shard_map/back/ppermute | solution.py:198
  108.7 26.3 %collective-permute-start.3 = (bf16[128,512]{1,0:T(8,128)(2,1)S(1)}, bf16[128,512]{1,0:T(8,128)(2,1)S(1)}, u32[]{:S(2)}, u32[]{:S(2)}) collective-permute-start(bf16[128,512]{1,0:T(8,128)(2,1)S(1)} %get-tuple-element.17), channel_id=1, source_target_pairs={{0,508},{4,0},{8,4},{12,8},{16,12},{20,16},{24,20},{28,24},{32,28}... | collective-permute-start | bytes 393224 | tf_op jit(solution)/shard_map/back/ppermute | solution.py:198
  135.5 4.5 %collective-permute-start.8 = (bf16[128,768]{1,0:T(8,128)(2,1)S(1)}, bf16[128,768]{1,0:T(8,128)(2,1)S(1)}, u32[]{:S(2)}, u32[]{:S(2)}) collective-permute-start(bf16[128,768]{1,0:T(8,128)(2,1)S(1)} %total.1), channel_id=1, source_target_pairs={{0,4},{4,0},{1,5},{5,1},{2,6},{6,2},{3,7},{7,3},{8,12},{12,8},{9,1... | collective-permute-start | bytes 589832 | tf_op jit(solution)/shard_map/total/ppermute | solution.py:202
  141.5 33.6 %all-to-all-start.3 = ((bf16[4,128,768]{2,1,0:T(8,128)(2,1)}), bf16[4,128,768]{2,1,0:T(8,128)(2,1)S(1)}, u32[]{:S(2)}, u32[]{:S(2)}) async-start(bf16[4,128,768]{2,1,0:T(8,128)(2,1)} %bitcast.31), calls=%async_computation.3 | async-start | bytes 1572864 | tf_op jit(solution)/shard_map/weight/all_to_all | solution.py:193
  146.5 5.6 %collective-permute-start.10 = (f32[4,1024]{1,0:T(4,128)S(1)}, f32[4,1024]{1,0:T(4,128)S(1)}, u32[]{:S(2)}, u32[]{:S(2)}) collective-permute-start(f32[4,1024]{1,0:T(4,128)S(1)} %slice_add_fusion), channel_id=1, source_target_pairs={{0,1},{1,0},{2,3},{3,2},{4,5},{5,4},{6,7},{7,6},{8,9},{9,8},{10,11... | collective-permute-start | bytes 49160 | tf_op jit(solution)/shard_map/virtual/ppermute | solution.py:202
  152.1 7.1 %collective-permute-start.11 = (f32[4,1024]{1,0:T(4,128)S(1)}, f32[4,1024]{1,0:T(4,128)S(1)}, u32[]{:S(2)}, u32[]{:S(2)}) collective-permute-start(f32[4,1024]{1,0:T(4,128)S(1)} %fusion.58), channel_id=1, source_target_pairs={{0,2},{1,3},{2,0},{3,1},{4,6},{5,7},{6,4},{7,5},{8,10},{9,11},{10,... | collective-permute-start | bytes 49160 | tf_op jit(solution)/shard_map/virtual/ppermute | solution.py:202
  159.2 3.1 %collective-permute-start.12 = (f32[4,1024]{1,0:T(4,128)S(1)}, f32[4,1024]{1,0:T(4,128)S(1)}, u32[]{:S(2)}, u32[]{:S(2)}) collective-permute-start(f32[4,1024]{1,0:T(4,128)S(1)} %add.157), channel_id=1, source_target_pairs={{0,4},{4,0},{1,5},{5,1},{2,6},{6,2},{3,7},{7,3},{8,12},{12,8},{9,1... | collective-permute-start | bytes 49160 | tf_op jit(solution)/shard_map/virtual/ppermute | solution.py:202
  162.3 5.6 %collective-permute-start.13 = (f32[4,1024]{1,0:T(4,128)S(1)}, f32[4,1024]{1,0:T(4,128)S(1)}, u32[]{:S(2)}, u32[]{:S(2)}) collective-permute-start(f32[4,1024]{1,0:T(4,128)S(1)} %add.158), channel_id=1, source_target_pairs={{0,8},{8,0},{16,24},{24,16},{1,9},{9,1},{17,25},{25,17},{2,10},{10... | collective-permute-start | bytes 49160 | tf_op jit(solution)/shard_map/virtual/ppermute | solution.py:202
  167.9 7.1 %collective-permute-start.14 = (f32[4,1024]{1,0:T(4,128)S(1)}, f32[4,1024]{1,0:T(4,128)S(1)}, u32[]{:S(2)}, u32[]{:S(2)}) collective-permute-start(f32[4,1024]{1,0:T(4,128)S(1)} %add.159), channel_id=1, source_target_pairs={{0,16},{8,24},{16,0},{24,8},{1,17},{9,25},{17,1},{25,9},{2,18},{10... | collective-permute-start | bytes 49160 | tf_op jit(solution)/shard_map/virtual/ppermute | solution.py:202
  176.0 23.0 %all-to-all-start.4 = ((bf16[16,8,1280]{2,1,0:T(8,128)(2,1)}), bf16[16,8,1280]{2,1,0:T(8,128)(2,1)S(1)}, u32[]{:S(2)}, u32[]{:S(2)}) async-start(bf16[16,8,1280]{2,1,0:T(8,128)(2,1)} %pad_maximum_fusion), calls=%async_computation.4 | async-start | bytes 655360 | tf_op jit(solution)/shard_map/weight/all_to_all | solution.py:193
  180.7 10.7 %collective-permute-start.4 = (bf16[128,256]{1,0:T(8,128)(2,1)S(1)}, bf16[128,256]{1,0:T(8,128)(2,1)S(1)}, u32[]{:S(2)}, u32[]{:S(2)}) collective-permute-start(bf16[128,256]{1,0:T(8,128)(2,1)S(1)} %get-tuple-element.23), channel_id=1, source_target_pairs={{0,1},{1,2},{2,3},{3,0},{4,5},{5,6},{6,7},{7,4},{8,9},{9,10},{10,1... | collective-permute-start | bytes 196616 | tf_op jit(solution)/shard_map/feature/ppermute | solution.py:198
  184.1 7.7 %collective-permute-start.5 = (bf16[128,256]{1,0:T(8,128)(2,1)S(1)}, bf16[128,256]{1,0:T(8,128)(2,1)S(1)}, u32[]{:S(2)}, u32[]{:S(2)}) collective-permute-start(bf16[128,256]{1,0:T(8,128)(2,1)S(1)} %get-tuple-element.25), channel_id=1, source_target_pairs={{0,2},{1,3},{2,0},{3,1},{4,6},{5,7},{6,4},{7,5},{8,10},{9,11},{10,... | collective-permute-start | bytes 196616 | tf_op jit(solution)/shard_map/feature/ppermute | solution.py:198
  187.0 6.2 %collective-permute-start.6 = (bf16[128,256]{1,0:T(8,128)(2,1)S(1)}, bf16[128,256]{1,0:T(8,128)(2,1)S(1)}, u32[]{:S(2)}, u32[]{:S(2)}) collective-permute-start(bf16[128,256]{1,0:T(8,128)(2,1)S(1)} %get-tuple-element.24), channel_id=1, source_target_pairs={{0,3},{1,0},{2,1},{3,2},{4,7},{5,4},{6,5},{7,6},{8,11},{9,8},{10,9... | collective-permute-start | bytes 196616 | tf_op jit(solution)/shard_map/feature/ppermute | solution.py:198

commit v2 on v1

--- a/solution.py
+++ b/solution.py
@@ -16,6 +16,7 @@
 SHARDS = 128
 COLS = 256
 HEADS_DEV = 2
+SLOTS = 2 * DEGREE
 SIZES = {"z": 16, "x": 4, "c": 2, "mp": 4}
 NODES = ("z", "x", "c")
 
@@ -50,21 +51,21 @@
     return ref[:, start : start + HEAD]
 
 
-def owner_hits(owners_ref, perm):
-    shard = lax.broadcasted_iota(jnp.int32, (SHARDS, ROWS), 0)
-    return jnp.where(shard == owners_ref[perm : perm + 1, :], 1.0, 0.0).astype(BF16)
-
-
-def asked_hits(asked_ref, perm):
-    row = lax.broadcasted_iota(jnp.int32, (SHARDS, ROWS), 1)
-    return jnp.where(row == asked_ref[:, perm : perm + 1], 1.0, 0.0).astype(BF16)
+def ones_where(condition):
+    return jnp.where(condition, 1.0, 0.0).astype(BF16)
 
 
 def serve_kernel(asked_ref, kv_ref, out_ref):
-    kv = kv_ref[...]
-    for perm in range(DEGREE):
-        picked = mul(asked_hits(asked_ref, perm), kv, NN)
-        out_ref[:, perm * 2 * COLS : (perm + 1) * 2 * COLS] = picked.astype(BF16)
+    asked = asked_ref[:, 0, :].astype(F32).astype(BF16)
+    place = lax.broadcasted_iota(jnp.int32, (SHARDS * SLOTS, SHARDS), 0)
+    shard = lax.broadcasted_iota(jnp.int32, (SHARDS * SLOTS, SHARDS), 1)
+    spread = mul(ones_where(place // SLOTS == shard), asked, NN)
+    own_slot = lax.broadcasted_iota(jnp.int32, spread.shape, 0) % SLOTS
+    slot = lax.broadcasted_iota(jnp.int32, spread.shape, 1)
+    row = jnp.sum(jnp.where(slot == own_slot, spread, 0.0), axis=1, keepdims=True).astype(jnp.int32)
+    hits = ones_where(lax.broadcasted_iota(jnp.int32, (SHARDS * SLOTS, 2 * ROWS), 1) == row)
+    rows = jnp.concatenate([kv_ref[:, :COLS], kv_ref[:, COLS:]], axis=0)
+    out_ref[...] = mul(hits, rows, NN).astype(BF16)
 
 
 def virtual_weights(bias_ref, head, unit_q, virtual_ref, member_ref):
@@ -95,18 +96,20 @@
     out_ref[...] = jnp.concatenate(columns, axis=1)
 
 
-def near_kernel(bias_ref, owners_ref, query_ref, near_ref, grad_ref, sums_ref, send_ref, stats_ref, dquery_ref):
+def near_kernel(bias_ref, columns_ref, codes_ref, query_ref, near_ref, grad_ref, sums_ref, send_ref, stats_ref, dquery_ref, pieces):
     totals = [sums_ref[:, 2 * head : 2 * head + 1] for head in range(HEADS_DEV)]
     mixed = [sums_ref[:, 2 * head + 1 : 2 * head + 2] for head in range(HEADS_DEV)]
+    place = lax.broadcasted_iota(jnp.int32, (ROWS, SHARDS * SLOTS), 1)
+    received = near_ref[...]
     unit_q = [unit(head_of(query_ref, head))[0] for head in range(HEADS_DEV)]
     grad = [head_of(grad_ref, head).astype(F32) for head in range(HEADS_DEV)]
     saved = {}
     for perm in range(DEGREE):
-        hits = owner_hits(owners_ref, perm)
-        rows = mul(hits, near_ref[:, perm * 2 * COLS : (perm + 1) * 2 * COLS], TN)
+        key_rows = mul(ones_where(place == columns_ref[:, 2 * perm : 2 * perm + 1]), received, NN)
+        value_rows = mul(ones_where(place == columns_ref[:, 2 * perm + 1 : 2 * perm + 2]), received, NN)
         for head in range(HEADS_DEV):
-            unit_k, inv_k = unit(rows[:, head * HEAD : (head + 1) * HEAD])
-            values = rows[:, COLS + head * HEAD : COLS + (head + 1) * HEAD]
+            unit_k, inv_k = unit(key_rows[:, head * HEAD : (head + 1) * HEAD])
+            values = value_rows[:, head * HEAD : (head + 1) * HEAD]
             scores = SCALE * jnp.sum(unit_q[head] * unit_k, axis=1, keepdims=True)
             weights = jnp.exp(scores + bias_ref[1, head] + BOOST)
             grads = jnp.sum(grad[head] * values, axis=1, keepdims=True)
@@ -117,16 +120,20 @@
     delta = [mixed[head] * inverse[head] for head in range(HEADS_DEV)]
     dquery = [jnp.zeros((ROWS, HEAD), F32) for _ in range(HEADS_DEV)]
     for perm in range(DEGREE):
-        dkeys, dvalues = [], []
         for head in range(HEADS_DEV):
             unit_k, inv_k, weights, grads = saved[perm, head]
             probs = weights * inverse[head]
             dscores = probs * (grads - delta[head]) * SCALE
             dquery[head] = dquery[head] + dscores * unit_k
-            dkeys.append(unit_back(unit_k, inv_k, dscores * unit_q[head]).astype(BF16))
-            dvalues.append((probs * grad[head]).astype(BF16))
-        picked = mul(owner_hits(owners_ref, perm), jnp.concatenate(dkeys + dvalues, axis=1), NN)
-        send_ref[:, perm * 2 * COLS : (perm + 1) * 2 * COLS] = picked.astype(BF16)
+            at = slice(head * HEAD, (head + 1) * HEAD)
+            keys_at = slice(2 * perm * ROWS, (2 * perm + 1) * ROWS)
+            values_at = slice((2 * perm + 1) * ROWS, (2 * perm + 2) * ROWS)
+            pieces[keys_at, at] = unit_back(unit_k, inv_k, dscores * unit_q[head]).astype(BF16)
+            pieces[values_at, at] = (probs * grad[head]).astype(BF16)
+    returned = pieces[...]
+    for block in range(SLOTS):
+        place = lax.broadcasted_iota(jnp.int32, (ROWS, SLOTS * ROWS), 0) + block * ROWS
+        send_ref[block * ROWS : (block + 1) * ROWS, :] = mul(ones_where(place == codes_ref[...]), returned, NN).astype(BF16)
     stats_ref[...] = jnp.concatenate([inverse[0], delta[0], inverse[1], delta[1]], axis=1)
     dquery_ref[...] = jnp.concatenate(dquery, axis=1)
 
@@ -164,19 +171,34 @@
         dquery_ref[:, keys_at] = unit_back(unit_q, inv_q, dquery).astype(BF16)
 
 
-def total_kernel(asked_ref, back_ref, dquery_ref, down_ref, from_left_ref, from_right_ref, out_ref):
-    total = down_ref[...] + from_left_ref[...].astype(F32) + from_right_ref[...].astype(F32)
-    for perm in range(DEGREE):
-        total += mul(asked_hits(asked_ref, perm), back_ref[:, perm * 2 * COLS : (perm + 1) * 2 * COLS], TN)
-    out_ref[:, :COLS] = dquery_ref[...]
-    out_ref[:, COLS:] = total.astype(BF16)
+def total_kernel(asked_ref, back_ref, dquery_ref, down_ref, from_left_ref, from_right_ref, tail_ref, out_ref):
+    place = lax.broadcasted_iota(jnp.int32, (2 * ROWS, SHARDS * SLOTS), 0)
+    near = mul(ones_where(place == asked_ref[...]), back_ref[...], NN)
+    rim = from_left_ref[...].astype(F32) + from_right_ref[...].astype(F32)
+    total = down_ref[...] + rim
+    out_ref[:ROWS, :COLS] = dquery_ref[...]
+    out_ref[:ROWS, COLS : 2 * COLS] = (total[:, :COLS] + near[:ROWS]).astype(BF16)
+    out_ref[:ROWS, 2 * COLS :] = (total[:, COLS:] + near[ROWS:]).astype(BF16)
+    out_ref[ROWS:, :] = tail_ref[...]
+
+
+def weight_kernel(in_own_ref, in_other_ref, own_ref, other_ref, out_ref):
+    own, other = own_ref[...], other_ref[...]
+    vnode = own[ROWS + 16 :].astype(F32) + other[ROWS + 16 :].astype(F32)
+    high, low = two_terms(vnode[:8] + vnode[8:])
+    tail = jnp.concatenate([high.astype(F32), low.astype(F32)], axis=0).astype(BF16)
+    for part in range(4):
+        at = slice(part * 128, (part + 1) * 128)
+        term = mul(in_own_ref[at, :], own, NN) + mul(in_other_ref[at, :], other, NN)
+        out_ref[part, :128, :] = term.astype(BF16)
+        out_ref[part, 128:, :] = tail
 
 
 VMEM = pl.BlockSpec(memory_space=pltpu.VMEM)
 SMEM = pl.BlockSpec(memory_space=pltpu.SMEM)
 
 
-def call(kernel, outs, *args, scalars=0, flops=10**8):
+def call(kernel, outs, *args, scalars=0, scratch=(), flops=10**8):
     shapes = [jax.ShapeDtypeStruct(shape, kind) for shape, kind in outs]
     moved = sum(math.prod(a.shape) * a.dtype.itemsize for a in [*args, *shapes])
     return pl.pallas_call(
@@ -184,6 +206,7 @@
         out_shape=shapes,
         in_specs=[SMEM] * scalars + [VMEM] * (len(args) - scalars),
         out_specs=[VMEM] * len(shapes),
+        scratch_shapes=list(scratch),
         compiler_params=pltpu.CompilerParams(vmem_limit_bytes=32 * 2**20),
         cost_estimate=pl.CostEstimate(flops=flops, bytes_accessed=moved, transcendentals=0),
     )(*args)
@@ -213,7 +236,9 @@
         owners = neighbours // ROWS
         hit = owners[:, None, :] == jnp.arange(SHARDS, dtype=jnp.int32)[None, :, None]
         wanted = jnp.sum(jnp.where(hit, (neighbours % ROWS)[:, None, :], 0), axis=2)
-        asked = exchange(wanted.T, NODES)
+        wanted = jnp.stack([wanted, wanted + ROWS], axis=1).reshape(SLOTS, SHARDS)
+        asked = exchange(wanted.T.reshape(SHARDS, 1, SLOTS), NODES)
+        codes = jnp.repeat(owners, 2, axis=0) * SLOTS + jnp.arange(SLOTS, dtype=jnp.int32)[:, None]
     with jax.named_scope("project"):
         flat_weight = qkv_weight.reshape(width_in, 3 * COLS)
         projected = jnp.dot(features, flat_weight, preferred_element_type=F32)
@@ -227,14 +252,14 @@
         place = jnp.arange(width_in, dtype=jnp.int32)
         half, rest = place // 512, place % 512
         source = (rest // 8 % 16) * 64 + (rest // 128) * 16 + (half ^ core) * 8 + rest % 8
-        chosen = (jnp.arange(width_in, dtype=jnp.int32)[:, None] == source[None, :]).astype(BF16)
-        sorted_in = jnp.dot(jnp.concatenate([features, vnode_emb], axis=0), chosen, preferred_element_type=F32)
-        sorted_in = sorted_in.astype(BF16)
-        other_in = swap(sorted_in[:ROWS, 512:], "c", 1)
-        wide_in = jnp.concatenate([sorted_in[:ROWS, :512], other_in, sorted_in[ROWS:, :512], sorted_in[ROWS:, :512]], axis=0)
+        chosen = (source[:, None] == jnp.arange(width_in, dtype=jnp.int32)[None, :]).astype(BF16)
+        rows_in = jnp.concatenate([features, vnode_emb, vnode_emb, jnp.zeros((24, width_in), BF16)], axis=0)
+        sorted_in = mul(chosen, rows_in, NT).astype(BF16)
+        in_own = sorted_in[:512]
+        in_other = jnp.concatenate([swap(sorted_in[512:, :ROWS], "c", 1), in_own[:, ROWS:]], axis=1)
     with jax.named_scope("serve"):
-        served, = call(serve_kernel, [((SHARDS, DEGREE * 2 * COLS), BF16)], asked, kv)
-        near = exchange(served, NODES)
+        served, = call(serve_kernel, [((SHARDS * SLOTS, COLS), BF16)], asked, kv)
+        near = exchange(served.reshape(SHARDS, SLOTS, COLS), NODES).reshape(SHARDS * SLOTS, COLS)
     with jax.named_scope("local"):
         sums, = call(
             local_kernel, [((ROWS, 4), F32)],
@@ -242,10 +267,11 @@
         )
     with jax.named_scope("near"):
         send, stats, dnear = call(
-            near_kernel, [((SHARDS, DEGREE * 2 * COLS), BF16), ((ROWS, 4), F32), ((ROWS, COLS), F32)],
-            edge_bias, owners, query, near, out_grad, sums, scalars=1,
+            near_kernel, [((SHARDS * SLOTS, COLS), BF16), ((ROWS, 4), F32), ((ROWS, COLS), F32)],
+            edge_bias, codes.T, codes.reshape(1, SLOTS * ROWS), query, near, out_grad, sums, scalars=1,
+            scratch=[pltpu.VMEM((SLOTS * ROWS, COLS), BF16)],
         )
-        back = exchange(send, NODES)
+        back = exchange(send.reshape(SHARDS, SLOTS, COLS), NODES).reshape(SHARDS * SLOTS, COLS)
     with jax.named_scope("back"):
         dquery, dleft, down, dright, dvirtual = call(
             back_kernel,
@@ -255,24 +281,21 @@
         back_left = shift(dright, NODES, 1)
         back_right = shift(dleft, NODES, -1)
     with jax.named_scope("virtual"):
-        high, low = two_terms(dvirtual)
-        kv_weight = flat_weight[:, COLS:]
-        vnode = mul(jnp.concatenate([high, low], axis=0), kv_weight, NT)
+        split = jnp.concatenate(two_terms(dvirtual), axis=0)
+        vnode = mul(split, flat_weight[:, COLS:], NT)
         vnode = vnode[:VIRTUAL] + vnode[VIRTUAL:]
-        for axis, bit in (("mp", 1), ("mp", 2), ("c", 1), ("x", 1), ("x", 2)):
-            vnode = vnode + swap(vnode, axis, bit)
-        dvirtual = dvirtual + swap(dvirtual, "c", 1)
-        high, low = two_terms(dvirtual)
-        extra = jnp.concatenate([high, low], axis=0)
-        extra = jnp.concatenate([jnp.zeros((2 * VIRTUAL, COLS), BF16), extra], axis=1)
+        for bit in (1, 2):
+            vnode = vnode + swap(vnode, "mp", bit)
+        vnode = jnp.concatenate(two_terms(vnode.reshape(8, 512)), axis=0)
+        tail = jnp.concatenate([jnp.pad(split, ((0, 8), (COLS, 0))), jnp.pad(vnode, ((0, 0), (0, COLS)))], axis=0)
     with jax.named_scope("total"):
-        dqkv, = call(
-            total_kernel, [((ROWS, 3 * COLS), BF16)],
-            asked, back, dquery, down, back_left, back_right,
+        own, = call(
+            total_kernel, [((ROWS + 32, 3 * COLS), BF16)],
+            asked.reshape(1, SHARDS * SLOTS), back, dquery, down, back_left, back_right, tail,
         )
-        other = swap(dqkv, "c", 1)
+        other = swap(own, "c", 1)
     with jax.named_scope("feature"):
-        partial = mul(dqkv, flat_weight, NT).astype(BF16)
+        partial = mul(own[:ROWS], flat_weight, NT).astype(BF16)
         me = lax.axis_index("mp")
         summed = lax.dynamic_slice_in_dim(partial, me * COLS, COLS, 1).astype(F32)
         for step in range(1, 4):
@@ -280,12 +303,11 @@
             summed = summed + shift(piece, "mp", step).astype(F32)
         feature_grad = summed.astype(BF16)
     with jax.named_scope("weight"):
-        wide_out = jnp.concatenate([dqkv, other, extra], axis=0)
-        term = mul(wide_in, wide_out, TN).astype(BF16)
-        term = exchange(term.reshape(4, 128, 3 * COLS), "x")
-        term = jnp.sum(term.astype(F32), axis=0).reshape(16, 8, 3 * COLS)
-        tail = jnp.broadcast_to(vnode.reshape(1, 8, 512), (16, 8, 512))
-        term = jnp.concatenate([term, tail], axis=2).astype(BF16)
+        term, = call(weight_kernel, [((4, 144, 3 * COLS), BF16)], in_own, in_other, own, other, flops=3 * 10**8)
+        term = jnp.sum(exchange(term, "x").astype(F32), axis=0)
+        vnode = term[128:136, :512] + term[136:, :512]
+        tail = jnp.broadcast_to(vnode[None], (16, 8, 512))
+        term = jnp.concatenate([term[:128].reshape(16, 8, 3 * COLS), tail], axis=2).astype(BF16)
         term = jnp.sum(exchange(term, "z").astype(F32), axis=0)
         out_scale = 1.0 / math.sqrt(ROWS * SHARDS)
         weight_grad = (term[:, : 3 * COLS] * out_scale).reshape(8, 3, COLS)

time: 202 us -> 177 us (0.88)
  the two profiles are of different devices: /device:TPU:10 before, /device:TPU:32 now
where the time goes in v2:
time: 177 us; the launch traced here: 176 us
  starting transfers between devices  79.4 us (45%)
  waiting for transfers between devices  53.6 us (30%)
  blocking collectives  16.6 us (9%)
  Pallas kernels  11.7 us (7%)
  local copies, waits for them, and re-layouts  5.94 us (3%)
  other arithmetic  4 us (2%)
  matrix products  3.8 us (2%)
    all_to_all x4, starting transfers between devices, exchange(): return lax.all_to_all(values, axis, split_axis=0, concat_axis=0, tiled=True)  43.3 us
    all_to_all x4, waiting for transfers between devices, exchange(): return lax.all_to_all(values, axis, split_axis=0, concat_axis=0, tiled=True)  30.2 us
    ppermute x7, starting transfers between devices, shift(): lax.ppermute(values, axis, [(i, (i + step) % count) for i in range(count)])  23.3 us
    ppermute x7, waiting for transfers between devices, shift(): lax.ppermute(values, axis, [(i, (i + step) % count) for i in range(count)])  22.4 us
    all_to_all x1, blocking collectives, exchange(): return lax.all_to_all(values, axis, split_axis=0, concat_axis=0, tiled=True)  16.6 us
    ppermute x4, starting transfers between devices, swap(): lax.ppermute(values, axis, [(i, i ^ bit) for i in range(SIZES[axis])])  12.8 us
    pallas_call x6, Pallas kernels, call(): pl.pallas_call(kernel, out_shape=shapes, in_specs=[SMEM] * scalars + [VME...  11.7 us
  transfers between devices with their start and end apart: 15, of which 9 were waited for; matrix products, arithmetic and copies ran while one was open for 5% of the time, Pallas kernels for 3%

profile of v2, /device:TPU:32, one launch (start us, length us, event | category | flops | bytes accessed | tf_op | source)
XLA Modules:
  0.0 176.1 jit_solution(13661995369703696851)
XLA Ops:
  2.2 19.0 %all-to-all-start = ((s32[128,1,8]{2,1,0:T(1,128)}), s32[128,1,8]{2,1,0:T(1,128)S(1)}, u32[]{:S(2)}, u32[]{:S(2)}) async-start(s32[128,1,8]{2,1,0:T(1,128)} %bitcast.3), calls=%async_computation | async-start | bytes 131072 | tf_op jit(solution)/shard_map/ask/all_to_all | solution.py:216
  21.3 1.8 copy.30
  24.5 11.1 %all-to-all-done.asked_ref = s32[128,1,8]{2,1,0:T(1,128)S(1)} async-done(((s32[128,1,8]{2,1,0:T(1,128)}), s32[128,1,8]{2,1,0:T(1,128)S(1)}, u32[]{:S(2)}, u32[]{:S(2)}) %all-to-all-start) | async-done | bytes 4128 | tf_op jit(solution)/shard_map/ask/all_to_all | solution.py:216
  35.6 1.5 serve.1
  37.0 6.2 %all-to-all-start.1 = ((bf16[128,8,256]{2,1,0:T(8,128)(2,1)}), bf16[128,8,256]{2,1,0:T(8,128)(2,1)S(1)}, u32[]{:S(2)}, u32[]{:S(2)}) async-start(bf16[128,8,256]{2,1,0:T(8,128)(2,1)} %bitcast.9), calls=%async_computation.1 | async-start | bytes 1048576 | tf_op jit(solution)/shard_map/serve/all_to_all | solution.py:216
  43.3 2.1 %collective-permute-start = (bf16[128,512]{1,0:T(8,128)(2,1)S(1)}, bf16[128,512]{1,0:T(8,128)(2,1)S(1)}, u32[]{:S(2)}, u32[]{:S(2)}) collective-permute-start(bf16[128,512]{1,0:T(8,128)(2,1)S(1)} %slice.92.kv_ref.own_ref), channel_id=1, source_target_pairs={{0,4},{4,8},{8,12},{12,16},{16,20},{20,24},{24,28},{28,32},{32,36}... | collective-permute-start | bytes 393224 | tf_op jit(solution)/shard_map/project/ppermute | solution.py:221
  45.3 5.6 %collective-permute-start.1 = (bf16[128,512]{1,0:T(8,128)(2,1)S(1)}, bf16[128,512]{1,0:T(8,128)(2,1)S(1)}, u32[]{:S(2)}, u32[]{:S(2)}) collective-permute-start(bf16[128,512]{1,0:T(8,128)(2,1)S(1)} %slice.92.kv_ref.own_ref), channel_id=1, source_target_pairs={{0,508},{4,0},{8,4},{12,8},{16,12},{20,16},{24,20},{28,24},{32,28}... | collective-permute-start | bytes 393224 | tf_op jit(solution)/shard_map/project/ppermute | solution.py:221
  52.6 14.2 %collective-permute-done.left_ref = bf16[128,512]{1,0:T(8,128)(2,1)S(1)} collective-permute-done((bf16[128,512]{1,0:T(8,128)(2,1)S(1)}, bf16[128,512]{1,0:T(8,128)(2,1)S(1)}, u32[]{:S(2)}, u32[]{:S(2)}) %collective-permute-start) | collective-permute-done | bytes 131104 | tf_op jit(solution)/shard_map/project/ppermute | solution.py:221
  66.8 1.3 local.1.sums_ref
  68.1 8.2 %all-to-all-done.1 = bf16[128,8,256]{2,1,0:T(8,128)(2,1)S(1)} async-done(((bf16[128,8,256]{2,1,0:T(8,128)(2,1)}), bf16[128,8,256]{2,1,0:T(8,128)(2,1)S(1)}, u32[]{:S(2)}, u32[]{:S(2)}) %all-to-all-start.1) | async-done | bytes 524320 | tf_op jit(solution)/shard_map/serve/all_to_all | solution.py:216
  76.3 4.9 %near.1 = (bf16[1024,256]{1,0:T(8,128)(2,1)}, f32[128,4]{1,0:T(8,128)S(1)}, f32[128,256]{1,0:T(8,128)S(1)}) custom-call(f32[3,2]{1,0:T(4,128)S(1)} %copy.33.bias_ref, s32[128,8]{1,0:T(8,128)S(1)} %add_bitcast_fusion.columns_ref, s32[1,1024]{1,0:T(1,128)S(1)} %add.165.codes_ref, f32[128,256]{1,0:T(8,128)S(1)} %slice.60.query_ref, ...), custom_call_target="tpu_custom_call" | custom-call | flops 100000000 | bytes 1388568 | tf_op jit(solution)/shard_map/near/pallas_call | solution.py:204
  81.2 8.9 %all-to-all-start.2 = ((bf16[128,8,256]{2,1,0:T(8,128)(2,1)}), bf16[128,8,256]{2,1,0:T(8,128)(2,1)S(1)}, u32[]{:S(2)}, u32[]{:S(2)}) async-start(bf16[128,8,256]{2,1,0:T(8,128)(2,1)} %bitcast.11), calls=%async_computation.2 | async-start | bytes 1048576 | tf_op jit(solution)/shard_map/near/all_to_all | solution.py:216
  90.2 3.1 %back.1 = (bf16[128,256]{1,0:T(8,128)(2,1)S(1)}, bf16[128,512]{1,0:T(8,128)(2,1)S(1)}, f32[128,512]{1,0:T(8,128)S(1)}, bf16[128,512]{1,0:T(8,128)(2,1)S(1)}, f32[4,512]{1,0:T(4,128)S(1)}) custom-call(f32[3,2]{1,0:T(4,128)S(1)} %copy.33.bias_ref, f32[128,256]{1,0:T(8,128)S(1)} %slice.60.query_ref, bf16[128,512]{1,0:T(8,128)(2,1)S(1)} %collective-permute-done.left_ref, ...), custom_call_target="tpu_custom_call" | custom-call | flops 100000000 | bytes 1331224 | tf_op jit(solution)/shard_map/back/pallas_call | solution.py:204
  93.3 1.5 fusion.3
  94.8 3.5 %collective-permute-start.4 = (f32[4,1024]{1,0:T(4,128)S(1)}, f32[4,1024]{1,0:T(4,128)S(1)}, u32[]{:S(2)}, u32[]{:S(2)}) collective-permute-start(f32[4,1024]{1,0:T(4,128)S(1)} %slice_add_fusion.1), channel_id=1, source_target_pairs={{0,1},{1,0},{2,3},{3,2},{4,5},{5,4},{6,7},{7,6},{8,9},{9,8},{10,11... | collective-permute-start | bytes 49160 | tf_op jit(solution)/shard_map/virtual/ppermute | solution.py:225
  98.3 0.9 fusion.2
  99.2 1.9 %collective-permute-start.9 = (bf16[512,128]{1,0:T(8,128)(2,1)S(1)}, bf16[512,128]{1,0:T(8,128)(2,1)S(1)}, u32[]{:S(2)}, u32[]{:S(2)}) collective-permute-start(bf16[512,128]{1,0:T(8,128)(2,1)S(1)} %slice.67), channel_id=1, source_target_pairs={{0,4},{4,0},{1,5},{5,1},{2,6},{6,2},{3,7},{7,3},{8,12},{12,8},{9,1... | collective-permute-start | bytes 393224 | tf_op jit(solution)/shard_map/select/ppermute | solution.py:225
  102.6 4.8 %collective-permute-start.5 = (f32[4,1024]{1,0:T(4,128)S(1)}, f32[4,1024]{1,0:T(4,128)S(1)}, u32[]{:S(2)}, u32[]{:S(2)}) collective-permute-start(f32[4,1024]{1,0:T(4,128)S(1)} %fusion.49), channel_id=1, source_target_pairs={{0,2},{1,3},{2,0},{3,1},{4,6},{5,7},{6,4},{7,5},{8,10},{9,11},{10,... | collective-permute-start | bytes 49160 | tf_op jit(solution)/shard_map/virtual/ppermute | solution.py:225
  107.5 2.1 %collective-permute-start.2 = (bf16[128,512]{1,0:T(8,128)(2,1)S(1)}, bf16[128,512]{1,0:T(8,128)(2,1)S(1)}, u32[]{:S(2)}, u32[]{:S(2)}) collective-permute-start(bf16[128,512]{1,0:T(8,128)(2,1)S(1)} %get-tuple-element.16), channel_id=1, source_target_pairs={{0,4},{4,8},{8,12},{12,16},{16,20},{20,24},{24,28},{28,32},{32,36}... | collective-permute-start | bytes 393224 | tf_op jit(solution)/shard_map/back/ppermute | solution.py:221
  109.6 5.5 %collective-permute-start.3 = (bf16[128,512]{1,0:T(8,128)(2,1)S(1)}, bf16[128,512]{1,0:T(8,128)(2,1)S(1)}, u32[]{:S(2)}, u32[]{:S(2)}) collective-permute-start(bf16[128,512]{1,0:T(8,128)(2,1)S(1)} %get-tuple-element.17), channel_id=1, source_target_pairs={{0,508},{4,0},{8,4},{12,8},{16,12},{20,16},{24,20},{28,24},{32,28}... | collective-permute-start | bytes 393224 | tf_op jit(solution)/shard_map/back/ppermute | solution.py:221
  115.2 2.8 %collective-permute-done.2.from_left_ref = bf16[128,512]{1,0:T(8,128)(2,1)S(1)} collective-permute-done((bf16[128,512]{1,0:T(8,128)(2,1)S(1)}, bf16[128,512]{1,0:T(8,128)(2,1)S(1)}, u32[]{:S(2)}, u32[]{:S(2)}) %collective-permute-start.2) | collective-permute-done | bytes 131104 | tf_op jit(solution)/shard_map/back/ppermute | solution.py:221
  118.1 5.1 %all-to-all-done.2 = bf16[128,8,256]{2,1,0:T(8,128)(2,1)S(1)} async-done(((bf16[128,8,256]{2,1,0:T(8,128)(2,1)}), bf16[128,8,256]{2,1,0:T(8,128)(2,1)S(1)}, u32[]{:S(2)}, u32[]{:S(2)}) %all-to-all-start.2) | async-done | bytes 524320 | tf_op jit(solution)/shard_map/near/all_to_all | solution.py:216
  123.4 2.6 %collective-permute-start.10 = (bf16[160,768]{1,0:T(8,128)(2,1)S(1)}, bf16[160,768]{1,0:T(8,128)(2,1)S(1)}, u32[]{:S(2)}, u32[]{:S(2)}) collective-permute-start(bf16[160,768]{1,0:T(8,128)(2,1)S(1)} %total.1.own_ref), channel_id=1, source_target_pairs={{0,4},{4,0},{1,5},{5,1},{2,6},{6,2},{3,7},{7,3},{8,12},{12,8},{9,1... | collective-permute-start | bytes 737288 | tf_op jit(solution)/shard_map/total/ppermute | solution.py:225
  126.2 1.0 collective-permute-done.10.other_ref
  127.7 16.6 %all_to_all.25 = bf16[4,144,768]{2,1,0:T(8,128)(2,1)S(1)} all-to-all(bf16[4,144,768]{2,1,0:T(8,128)(2,1)S(1)} %weight.1), channel_id=1, replica_groups=mesh['z'=16,'x'=4,'c'=2,'mp'=4] {'x'}, dimensions={0} | all-to-all | bytes 1769472 | tf_op jit(solution)/shard_map/weight/all_to_all | solution.py:216
  145.2 9.2 %all-to-all-start.4 = ((bf16[16,8,1280]{2,1,0:T(8,128)(2,1)}), bf16[16,8,1280]{2,1,0:T(8,128)(2,1)S(1)}, u32[]{:S(2)}, u32[]{:S(2)}) async-start(bf16[16,8,1280]{2,1,0:T(8,128)(2,1)} %pad_maximum_fusion), calls=%async_computation.4 | async-start | bytes 655360 | tf_op jit(solution)/shard_map/weight/all_to_all | solution.py:216
  154.9 2.1 %collective-permute-start.8 = (bf16[128,256]{1,0:T(8,128)(2,1)S(1)}, bf16[128,256]{1,0:T(8,128)(2,1)S(1)}, u32[]{:S(2)}, u32[]{:S(2)}) collective-permute-start(bf16[128,256]{1,0:T(8,128)(2,1)S(1)} %get-tuple-element.24), channel_id=1, source_target_pairs={{0,3},{1,0},{2,1},{3,2},{4,7},{5,4},{6,5},{7,6},{8,11},{9,8},{10,9... | collective-permute-start | bytes 196616 | tf_op jit(solution)/shard_map/feature/ppermute | solution.py:221
  157.1 3.9 %collective-permute-start.7 = (bf16[128,256]{1,0:T(8,128)(2,1)S(1)}, bf16[128,256]{1,0:T(8,128)(2,1)S(1)}, u32[]{:S(2)}, u32[]{:S(2)}) collective-permute-start(bf16[128,256]{1,0:T(8,128)(2,1)S(1)} %get-tuple-element.25), channel_id=1, source_target_pairs={{0,2},{1,3},{2,0},{3,1},{4,6},{5,7},{6,4},{7,5},{8,10},{9,11},{10,... | collective-permute-start | bytes 196616 | tf_op jit(solution)/shard_map/feature/ppermute | solution.py:221
  161.0 1.9 %collective-permute-start.6 = (bf16[128,256]{1,0:T(8,128)(2,1)S(1)}, bf16[128,256]{1,0:T(8,128)(2,1)S(1)}, u32[]{:S(2)}, u32[]{:S(2)}) collective-permute-start(bf16[128,256]{1,0:T(8,128)(2,1)S(1)} %get-tuple-element.23), channel_id=1, source_target_pairs={{0,1},{1,2},{2,3},{3,0},{4,5},{5,6},{6,7},{7,4},{8,9},{9,10},{10,1... | collective-permute-start | bytes 196616 | tf_op jit(solution)/shard_map/feature/ppermute | solution.py:221
  162.9 1.8 %collective-permute-done.7 = bf16[128,256]{1,0:T(8,128)(2,1)S(1)} collective-permute-done((bf16[128,256]{1,0:T(8,128)(2,1)S(1)}, bf16[128,256]{1,0:T(8,128)(2,1)S(1)}, u32[]{:S(2)}, u32[]{:S(2)}) %collective-permute-start.7) | collective-permute-done | bytes 65568 | tf_op jit(solution)/shard_map/feature/ppermute | solution.py:221
  164.7 3.6 %collective-permute-done.6 = bf16[128,256]{1,0:T(8,128)(2,1)S(1)} collective-permute-done((bf16[128,256]{1,0:T(8,128)(2,1)S(1)}, bf16[128,256]{1,0:T(8,128)(2,1)S(1)}, u32[]{:S(2)}, u32[]{:S(2)}) %collective-permute-start.6) | collective-permute-done | bytes 65568 | tf_op jit(solution)/shard_map/feature/ppermute | solution.py:221
  169.0 5.8 %all-to-all-done.4 = bf16[16,8,1280]{2,1,0:T(8,128)(2,1)S(1)} async-done(((bf16[16,8,1280]{2,1,0:T(8,128)(2,1)}), bf16[16,8,1280]{2,1,0:T(8,128)(2,1)S(1)}, u32[]{:S(2)}, u32[]{:S(2)}) %all-to-all-start.4) | async-done | bytes 327712 | tf_op jit(solution)/shard_map/weight/all_to_all | solution.py:216
  (72 shorter events, 10.5 us)
Async XLA Ops:
  2.2 33.3 %all-to-all-start = ((s32[128,1,8]{2,1,0:T(1,128)}), s32[128,1,8]{2,1,0:T(1,128)S(1)}, u32[]{:S(2)}, u32[]{:S(2)}) async-start(s32[128,1,8]{2,1,0:T(1,128)} %bitcast.3), calls=%async_computation | async-start | bytes 131072 | tf_op jit(solution)/shard_map/ask/all_to_all | solution.py:216
  21.2 1.8 %copy-start.4 = (bf16[128,1024]{1,0:T(8,128)(2,1)S(1)}, bf16[128,1024]{1,0:T(8,128)(2,1)}, u32[]{:S(2)}) copy-start(bf16[128,1024]{1,0:T(8,128)(2,1)} %param.9) | copy-start | bytes 786436
  23.0 29.2 %copy-start.1 = (bf16[1024,3,256]{0,2,1:T(8,128)(2,1)}, bf16[1024,3,256]{0,2,1:T(8,128)(2,1)S(1)}, u32[]{:S(2)}) copy-start(bf16[1024,3,256]{0,2,1:T(8,128)(2,1)S(1)} %copy.30) | copy-start | bytes 4718596
  23.7 0.7 copy-start.3
  24.4 27.4 %copy-start.7 = (f32[3,2]{0,1:T(2,128)S(1)}, f32[3,2]{0,1:T(2,128)}, u32[]{:S(2)}) copy-start(f32[3,2]{0,1:T(2,128)} %param.12) | copy-start | bytes 76
  24.4 27.6 %copy-start.6 = (s32[128,4]{0,1:T(4,128)S(1)}, s32[128,4]{0,1:T(4,128)}, u32[]{:S(2)}) copy-start(s32[128,4]{0,1:T(4,128)} %param.15) | copy-start | bytes 6148
  24.4 27.8 %copy-start.5 = (bf16[4,1024]{1,0:T(4,128)(2,1)S(1)}, bf16[4,1024]{1,0:T(4,128)(2,1)}, u32[]{:S(2)}) copy-start(bf16[4,1024]{1,0:T(4,128)(2,1)} %param.11) | copy-start | bytes 24580
  24.5 42.3 %copy-start = (bf16[128,256]{1,0:T(8,128)(2,1)S(1)}, bf16[128,256]{1,0:T(8,128)(2,1)}, u32[]{:S(2)}) copy-start(bf16[128,256]{1,0:T(8,128)(2,1)} %grad_ref.5) | copy-start | bytes 196612
  37.0 39.3 %all-to-all-start.1 = ((bf16[128,8,256]{2,1,0:T(8,128)(2,1)}), bf16[128,8,256]{2,1,0:T(8,128)(2,1)S(1)}, u32[]{:S(2)}, u32[]{:S(2)}) async-start(bf16[128,8,256]{2,1,0:T(8,128)(2,1)} %bitcast.9), calls=%async_computation.1 | async-start | bytes 1048576 | tf_op jit(solution)/shard_map/serve/all_to_all | solution.py:216
  43.3 23.5 %collective-permute-start = (bf16[128,512]{1,0:T(8,128)(2,1)S(1)}, bf16[128,512]{1,0:T(8,128)(2,1)S(1)}, u32[]{:S(2)}, u32[]{:S(2)}) collective-permute-start(bf16[128,512]{1,0:T(8,128)(2,1)S(1)} %slice.92.kv_ref.own_ref), channel_id=1, source_target_pairs={{0,4},{4,8},{8,12},{12,16},{16,20},{20,24},{24,28},{28,32},{32,36}... | collective-permute-start | bytes 393224 | tf_op jit(solution)/shard_map/project/ppermute | solution.py:221
  45.3 21.5 %collective-permute-start.1 = (bf16[128,512]{1,0:T(8,128)(2,1)S(1)}, bf16[128,512]{1,0:T(8,128)(2,1)S(1)}, u32[]{:S(2)}, u32[]{:S(2)}) collective-permute-start(bf16[128,512]{1,0:T(8,128)(2,1)S(1)} %slice.92.kv_ref.own_ref), channel_id=1, source_target_pairs={{0,508},{4,0},{8,4},{12,8},{16,12},{20,16},{24,20},{28,24},{32,28}... | collective-permute-start | bytes 393224 | tf_op jit(solution)/shard_map/project/ppermute | solution.py:221
  81.2 41.9 %all-to-all-start.2 = ((bf16[128,8,256]{2,1,0:T(8,128)(2,1)}), bf16[128,8,256]{2,1,0:T(8,128)(2,1)S(1)}, u32[]{:S(2)}, u32[]{:S(2)}) async-start(bf16[128,8,256]{2,1,0:T(8,128)(2,1)} %bitcast.11), calls=%async_computation.2 | async-start | bytes 1048576 | tf_op jit(solution)/shard_map/near/all_to_all | solution.py:216
  94.8 7.8 %collective-permute-start.4 = (f32[4,1024]{1,0:T(4,128)S(1)}, f32[4,1024]{1,0:T(4,128)S(1)}, u32[]{:S(2)}, u32[]{:S(2)}) collective-permute-start(f32[4,1024]{1,0:T(4,128)S(1)} %slice_add_fusion.1), channel_id=1, source_target_pairs={{0,1},{1,0},{2,3},{3,2},{4,5},{5,4},{6,7},{7,6},{8,9},{9,8},{10,11... | collective-permute-start | bytes 49160 | tf_op jit(solution)/shard_map/virtual/ppermute | solution.py:225
  99.2 26.9 %collective-permute-start.9 = (bf16[512,128]{1,0:T(8,128)(2,1)S(1)}, bf16[512,128]{1,0:T(8,128)(2,1)S(1)}, u32[]{:S(2)}, u32[]{:S(2)}) collective-permute-start(bf16[512,128]{1,0:T(8,128)(2,1)S(1)} %slice.67), channel_id=1, source_target_pairs={{0,4},{4,0},{1,5},{5,1},{2,6},{6,2},{3,7},{7,3},{8,12},{12,8},{9,1... | collective-permute-start | bytes 393224 | tf_op jit(solution)/shard_map/select/ppermute | solution.py:225
  102.6 12.5 %collective-permute-start.5 = (f32[4,1024]{1,0:T(4,128)S(1)}, f32[4,1024]{1,0:T(4,128)S(1)}, u32[]{:S(2)}, u32[]{:S(2)}) collective-permute-start(f32[4,1024]{1,0:T(4,128)S(1)} %fusion.49), channel_id=1, source_target_pairs={{0,2},{1,3},{2,0},{3,1},{4,6},{5,7},{6,4},{7,5},{8,10},{9,11},{10,... | collective-permute-start | bytes 49160 | tf_op jit(solution)/shard_map/virtual/ppermute | solution.py:225
  107.5 10.6 %collective-permute-start.2 = (bf16[128,512]{1,0:T(8,128)(2,1)S(1)}, bf16[128,512]{1,0:T(8,128)(2,1)S(1)}, u32[]{:S(2)}, u32[]{:S(2)}) collective-permute-start(bf16[128,512]{1,0:T(8,128)(2,1)S(1)} %get-tuple-element.16), channel_id=1, source_target_pairs={{0,4},{4,8},{8,12},{12,16},{16,20},{20,24},{24,28},{28,32},{32,36}... | collective-permute-start | bytes 393224 | tf_op jit(solution)/shard_map/back/ppermute | solution.py:221
  109.6 8.5 %collective-permute-start.3 = (bf16[128,512]{1,0:T(8,128)(2,1)S(1)}, bf16[128,512]{1,0:T(8,128)(2,1)S(1)}, u32[]{:S(2)}, u32[]{:S(2)}) collective-permute-start(bf16[128,512]{1,0:T(8,128)(2,1)S(1)} %get-tuple-element.17), channel_id=1, source_target_pairs={{0,508},{4,0},{8,4},{12,8},{16,12},{20,16},{24,20},{28,24},{32,28}... | collective-permute-start | bytes 393224 | tf_op jit(solution)/shard_map/back/ppermute | solution.py:221
  123.4 3.7 %collective-permute-start.10 = (bf16[160,768]{1,0:T(8,128)(2,1)S(1)}, bf16[160,768]{1,0:T(8,128)(2,1)S(1)}, u32[]{:S(2)}, u32[]{:S(2)}) collective-permute-start(bf16[160,768]{1,0:T(8,128)(2,1)S(1)} %total.1.own_ref), channel_id=1, source_target_pairs={{0,4},{4,0},{1,5},{5,1},{2,6},{6,2},{3,7},{7,3},{8,12},{12,8},{9,1... | collective-permute-start | bytes 737288 | tf_op jit(solution)/shard_map/total/ppermute | solution.py:225
  144.3 10.2 %copy-start.2 = (bf16[1024,3,256]{0,2,1:T(8,128)(2,1)S(1)}, bf16[1024,3,256]{0,2,1:T(8,128)(2,1)}, u32[]{:S(2)}) copy-start(bf16[1024,3,256]{0,2,1:T(8,128)(2,1)} %copy-done.1) | copy-start | bytes 4718596
  145.2 29.6 %all-to-all-start.4 = ((bf16[16,8,1280]{2,1,0:T(8,128)(2,1)}), bf16[16,8,1280]{2,1,0:T(8,128)(2,1)S(1)}, u32[]{:S(2)}, u32[]{:S(2)}) async-start(bf16[16,8,1280]{2,1,0:T(8,128)(2,1)} %pad_maximum_fusion), calls=%async_computation.4 | async-start | bytes 655360 | tf_op jit(solution)/shard_map/weight/all_to_all | solution.py:216
  154.9 8.0 %collective-permute-start.8 = (bf16[128,256]{1,0:T(8,128)(2,1)S(1)}, bf16[128,256]{1,0:T(8,128)(2,1)S(1)}, u32[]{:S(2)}, u32[]{:S(2)}) collective-permute-start(bf16[128,256]{1,0:T(8,128)(2,1)S(1)} %get-tuple-element.24), channel_id=1, source_target_pairs={{0,3},{1,0},{2,1},{3,2},{4,7},{5,4},{6,5},{7,6},{8,11},{9,8},{10,9... | collective-permute-start | bytes 196616 | tf_op jit(solution)/shard_map/feature/ppermute | solution.py:221
  157.1 7.7 %collective-permute-start.7 = (bf16[128,256]{1,0:T(8,128)(2,1)S(1)}, bf16[128,256]{1,0:T(8,128)(2,1)S(1)}, u32[]{:S(2)}, u32[]{:S(2)}) collective-permute-start(bf16[128,256]{1,0:T(8,128)(2,1)S(1)} %get-tuple-element.25), channel_id=1, source_target_pairs={{0,2},{1,3},{2,0},{3,1},{4,6},{5,7},{6,4},{7,5},{8,10},{9,11},{10,... | collective-permute-start | bytes 196616 | tf_op jit(solution)/shard_map/feature/ppermute | solution.py:221
  161.0 7.4 %collective-permute-start.6 = (bf16[128,256]{1,0:T(8,128)(2,1)S(1)}, bf16[128,256]{1,0:T(8,128)(2,1)S(1)}, u32[]{:S(2)}, u32[]{:S(2)}) collective-permute-start(bf16[128,256]{1,0:T(8,128)(2,1)S(1)} %get-tuple-element.23), channel_id=1, source_target_pairs={{0,1},{1,2},{2,3},{3,0},{4,5},{5,6},{6,7},{7,4},{8,9},{9,10},{10,1... | collective-permute-start | bytes 196616 | tf_op jit(solution)/shard_map/feature/ppermute | solution.py:221

commit v3 on v2

--- a/solution.py
+++ b/solution.py
@@ -55,17 +55,52 @@
     return jnp.where(condition, 1.0, 0.0).astype(BF16)
 
 
-def serve_kernel(asked_ref, kv_ref, out_ref):
-    asked = asked_ref[:, 0, :].astype(F32).astype(BF16)
-    place = lax.broadcasted_iota(jnp.int32, (SHARDS * SLOTS, SHARDS), 0)
-    shard = lax.broadcasted_iota(jnp.int32, (SHARDS * SLOTS, SHARDS), 1)
-    spread = mul(ones_where(place // SLOTS == shard), asked, NN)
-    own_slot = lax.broadcasted_iota(jnp.int32, spread.shape, 0) % SLOTS
-    slot = lax.broadcasted_iota(jnp.int32, spread.shape, 1)
-    row = jnp.sum(jnp.where(slot == own_slot, spread, 0.0), axis=1, keepdims=True).astype(jnp.int32)
-    hits = ones_where(lax.broadcasted_iota(jnp.int32, (SHARDS * SLOTS, 2 * ROWS), 1) == row)
-    rows = jnp.concatenate([kv_ref[:, :COLS], kv_ref[:, COLS:]], axis=0)
-    out_ref[...] = mul(hits, rows, NN).astype(BF16)
+def shard_of(column):
+    return lax.shift_right_logical(column, 7)
+
+
+def ask_kernel(neighbours_ref, out_ref):
+    shard = lax.broadcasted_iota(jnp.int32, (SHARDS, ROWS), 0)
+    columns = []
+    for perm in range(DEGREE):
+        target = neighbours_ref[perm : perm + 1, :]
+        rows = jnp.where(shard == shard_of(target), target & (ROWS - 1), 0)
+        columns.append(jnp.sum(rows.astype(F32), axis=1, keepdims=True))
+    out_ref[:, 0, :] = jnp.concatenate(columns, axis=1).astype(jnp.int32)
+
+
+def slot(perm, part):
+    return pl.ds(2 * perm + part, SHARDS, stride=SLOTS)
+
+
+def take_slots(work_ref, perm):
+    pieces = [work_ref[half, slot(perm, part), :] for part in range(2) for half in range(2)]
+    return jnp.concatenate(pieces, axis=1).astype(BF16)
+
+
+def put_slots(work_ref, perm, rows):
+    for part in range(2):
+        for half in range(2):
+            at = part * COLS + half * HEAD
+            work_ref[half, slot(perm, part), :] = rows[:, at : at + HEAD]
+
+
+def open_slots(work_ref, rows_ref):
+    for half in range(2):
+        work_ref[half] = rows_ref[:, half * HEAD : (half + 1) * HEAD].astype(F32)
+
+
+def close_slots(work_ref, rows_ref):
+    for half in range(2):
+        rows_ref[:, half * HEAD : (half + 1) * HEAD] = work_ref[half].astype(BF16)
+
+
+def serve_kernel(asked_ref, kv_ref, out_ref, work_ref):
+    row = lax.broadcasted_iota(jnp.int32, (SHARDS, ROWS), 1)
+    asked, kv = asked_ref[:, 0, :], kv_ref[...]
+    for perm in range(DEGREE):
+        put_slots(work_ref, perm, mul(ones_where(row == asked[:, perm : perm + 1]), kv, NN))
+    close_slots(work_ref, out_ref)
 
 
 def virtual_weights(bias_ref, head, unit_q, virtual_ref, member_ref):
@@ -74,7 +109,12 @@
     return jnp.exp(scores) * member_ref[...].astype(F32), unit_v, inv_v
 
 
-def local_kernel(bias_ref, query_ref, left_ref, own_ref, right_ref, grad_ref, virtual_ref, member_ref, out_ref):
+def turned(columns):
+    wide = jnp.concatenate(columns + [jnp.zeros((ROWS, HEAD - len(columns)), F32)], axis=1)
+    return wide.T[: len(columns)]
+
+
+def local_kernel(bias_ref, query_ref, left_ref, own_ref, right_ref, grad_ref, virtual_ref, member_ref, sums_ref, query_out_ref, grad_out_ref):
     columns = []
     for head in range(HEADS_DEV):
         unit_q, _ = unit(head_of(query_ref, head))
@@ -93,62 +133,65 @@
         total += jnp.sum(weights, axis=1, keepdims=True)
         mixed += jnp.sum(weights * grads, axis=1, keepdims=True)
         columns += [total, mixed]
-    out_ref[...] = jnp.concatenate(columns, axis=1)
-
-
-def near_kernel(bias_ref, columns_ref, codes_ref, query_ref, near_ref, grad_ref, sums_ref, send_ref, stats_ref, dquery_ref, pieces):
-    totals = [sums_ref[:, 2 * head : 2 * head + 1] for head in range(HEADS_DEV)]
-    mixed = [sums_ref[:, 2 * head + 1 : 2 * head + 2] for head in range(HEADS_DEV)]
-    place = lax.broadcasted_iota(jnp.int32, (ROWS, SHARDS * SLOTS), 1)
-    received = near_ref[...]
-    unit_q = [unit(head_of(query_ref, head))[0] for head in range(HEADS_DEV)]
-    grad = [head_of(grad_ref, head).astype(F32) for head in range(HEADS_DEV)]
+        at = slice(head * HEAD, (head + 1) * HEAD)
+        query_out_ref[at, :] = unit_q.T
+        grad_out_ref[at, :] = grad.astype(F32).T
+    sums_ref[...] = turned(columns)
+
+
+def near_kernel(bias_ref, neighbours_ref, query_ref, near_ref, grad_ref, sums_ref, send_ref, stats_ref, dquery_ref, work_ref):
+    totals = [sums_ref[2 * head : 2 * head + 1, :] for head in range(HEADS_DEV)]
+    mixed = [sums_ref[2 * head + 1 : 2 * head + 2, :] for head in range(HEADS_DEV)]
+    shard = lax.broadcasted_iota(jnp.int32, (SHARDS, ROWS), 0)
+    hits = [ones_where(shard == shard_of(neighbours_ref[perm : perm + 1, :])) for perm in range(DEGREE)]
+    unit_q = [query_ref[head * HEAD : (head + 1) * HEAD, :] for head in range(HEADS_DEV)]
+    grad = [grad_ref[head * HEAD : (head + 1) * HEAD, :] for head in range(HEADS_DEV)]
+    open_slots(work_ref, near_ref)
     saved = {}
     for perm in range(DEGREE):
-        key_rows = mul(ones_where(place == columns_ref[:, 2 * perm : 2 * perm + 1]), received, NN)
-        value_rows = mul(ones_where(place == columns_ref[:, 2 * perm + 1 : 2 * perm + 2]), received, NN)
+        rows = mul(take_slots(work_ref, perm), hits[perm], TN)
         for head in range(HEADS_DEV):
-            unit_k, inv_k = unit(key_rows[:, head * HEAD : (head + 1) * HEAD])
-            values = value_rows[:, head * HEAD : (head + 1) * HEAD]
-            scores = SCALE * jnp.sum(unit_q[head] * unit_k, axis=1, keepdims=True)
-            weights = jnp.exp(scores + bias_ref[1, head] + BOOST)
-            grads = jnp.sum(grad[head] * values, axis=1, keepdims=True)
+            keys = rows[head * HEAD : (head + 1) * HEAD]
+            values = rows[COLS + head * HEAD : COLS + (head + 1) * HEAD]
+            inv_k = lax.rsqrt(jnp.mean(keys * keys, axis=0, keepdims=True) + EPSILON)
+            unit_k = keys * inv_k
+            product = jnp.sum(unit_q[head] * unit_k, axis=0, keepdims=True)
+            weights = jnp.exp(SCALE * product + bias_ref[1, head] + BOOST)
+            grads = jnp.sum(grad[head] * values, axis=0, keepdims=True)
             totals[head] = totals[head] + weights
             mixed[head] = mixed[head] + weights * grads
-            saved[perm, head] = (unit_k, inv_k, weights, grads)
+            saved[perm, head] = (unit_k, inv_k, product, weights, grads)
     inverse = [1.0 / total for total in totals]
     delta = [mixed[head] * inverse[head] for head in range(HEADS_DEV)]
-    dquery = [jnp.zeros((ROWS, HEAD), F32) for _ in range(HEADS_DEV)]
-    for perm in range(DEGREE):
+    dquery = [jnp.zeros((HEAD, ROWS), F32) for _ in range(HEADS_DEV)]
+    for perm in range(DEGREE):
+        dkeys, dvalues = [], []
         for head in range(HEADS_DEV):
-            unit_k, inv_k, weights, grads = saved[perm, head]
+            unit_k, inv_k, product, weights, grads = saved[perm, head]
             probs = weights * inverse[head]
             dscores = probs * (grads - delta[head]) * SCALE
             dquery[head] = dquery[head] + dscores * unit_k
-            at = slice(head * HEAD, (head + 1) * HEAD)
-            keys_at = slice(2 * perm * ROWS, (2 * perm + 1) * ROWS)
-            values_at = slice((2 * perm + 1) * ROWS, (2 * perm + 2) * ROWS)
-            pieces[keys_at, at] = unit_back(unit_k, inv_k, dscores * unit_q[head]).astype(BF16)
-            pieces[values_at, at] = (probs * grad[head]).astype(BF16)
-    returned = pieces[...]
-    for block in range(SLOTS):
-        place = lax.broadcasted_iota(jnp.int32, (ROWS, SLOTS * ROWS), 0) + block * ROWS
-        send_ref[block * ROWS : (block + 1) * ROWS, :] = mul(ones_where(place == codes_ref[...]), returned, NN).astype(BF16)
-    stats_ref[...] = jnp.concatenate([inverse[0], delta[0], inverse[1], delta[1]], axis=1)
-    dquery_ref[...] = jnp.concatenate(dquery, axis=1)
+            factor = dscores * inv_k
+            dkeys.append((factor * unit_q[head] - (factor * product * (1.0 / HEAD)) * unit_k).astype(BF16))
+            dvalues.append((probs * grad[head]).astype(BF16))
+        put_slots(work_ref, perm, mul(hits[perm], jnp.concatenate(dkeys + dvalues, axis=0), NT))
+    close_slots(work_ref, send_ref)
+    stats_ref[...] = jnp.concatenate([inverse[0], delta[0], inverse[1], delta[1]], axis=0)
+    dquery_ref[...] = jnp.concatenate(dquery, axis=0)
 
 
 def back_kernel(
     bias_ref, query_ref, left_ref, own_ref, right_ref, grad_ref, virtual_ref, member_ref, stats_ref, dnear_ref,
     dquery_ref, dleft_ref, down_ref, dright_ref, dvirtual_ref,
 ):
+    stats = jnp.concatenate([stats_ref[...], jnp.zeros((HEAD - 2 * HEADS_DEV, ROWS), F32)], axis=0).T
     for head in range(HEADS_DEV):
         unit_q, inv_q = unit(head_of(query_ref, head))
         query = unit_q.astype(BF16)
         grad = head_of(grad_ref, head)
-        inverse = stats_ref[:, 2 * head : 2 * head + 1]
-        delta = stats_ref[:, 2 * head + 1 : 2 * head + 2]
-        dquery = head_of(dnear_ref, head)
+        inverse = stats[:, 2 * head : 2 * head + 1]
+        delta = stats[:, 2 * head + 1 : 2 * head + 2]
+        dquery = dnear_ref[head * HEAD : (head + 1) * HEAD, :].T
         keys_at = slice(head * HEAD, (head + 1) * HEAD)
         values_at = slice(COLS + head * HEAD, COLS + (head + 1) * HEAD)
         for block, out in ((left_ref, dleft_ref), (own_ref, down_ref), (right_ref, dright_ref)):
@@ -171,14 +214,15 @@
         dquery_ref[:, keys_at] = unit_back(unit_q, inv_q, dquery).astype(BF16)
 
 
-def total_kernel(asked_ref, back_ref, dquery_ref, down_ref, from_left_ref, from_right_ref, tail_ref, out_ref):
-    place = lax.broadcasted_iota(jnp.int32, (2 * ROWS, SHARDS * SLOTS), 0)
-    near = mul(ones_where(place == asked_ref[...]), back_ref[...], NN)
+def total_kernel(asked_ref, back_ref, dquery_ref, down_ref, from_left_ref, from_right_ref, tail_ref, out_ref, work_ref):
+    place = lax.broadcasted_iota(jnp.int32, (ROWS, SHARDS), 0)
+    open_slots(work_ref, back_ref)
     rim = from_left_ref[...].astype(F32) + from_right_ref[...].astype(F32)
     total = down_ref[...] + rim
+    for perm in range(DEGREE):
+        total += mul(ones_where(place == asked_ref[perm : perm + 1, :]), take_slots(work_ref, perm), NN)
     out_ref[:ROWS, :COLS] = dquery_ref[...]
-    out_ref[:ROWS, COLS : 2 * COLS] = (total[:, :COLS] + near[:ROWS]).astype(BF16)
-    out_ref[:ROWS, 2 * COLS :] = (total[:, COLS:] + near[ROWS:]).astype(BF16)
+    out_ref[:ROWS, COLS:] = total.astype(BF16)
     out_ref[ROWS:, :] = tail_ref[...]
 
 
@@ -194,8 +238,21 @@
         out_ref[part, 128:, :] = tail
 
 
+def finish_kernel(parts_ref, weight_ref, vnode_ref):
+    out_scale = 1.0 / math.sqrt(ROWS * SHARDS)
+    total = parts_ref[0].astype(F32)
+    for part in range(1, SIZES["z"]):
+        total += parts_ref[part].astype(F32)
+    total *= out_scale
+    for kind in range(3):
+        weight_ref[kind] = total[:, kind * COLS : (kind + 1) * COLS]
+    vnode_ref[:, :512] = total[:VIRTUAL, 3 * COLS :]
+    vnode_ref[:, 512:] = total[VIRTUAL:, 3 * COLS :]
+
+
 VMEM = pl.BlockSpec(memory_space=pltpu.VMEM)
 SMEM = pl.BlockSpec(memory_space=pltpu.SMEM)
+WORK = (pltpu.VMEM((2, SHARDS * SLOTS, HEAD), F32),)
 
 
 def call(kernel, outs, *args, scalars=0, scratch=(), flops=10**8):
@@ -233,12 +290,8 @@
 def body(features, qkv_weight, vnode_emb, edge_bias, out_grad, neighbours, member, tile_list, tile_count):
     width_in = qkv_weight.shape[0]
     with jax.named_scope("ask"):
-        owners = neighbours // ROWS
-        hit = owners[:, None, :] == jnp.arange(SHARDS, dtype=jnp.int32)[None, :, None]
-        wanted = jnp.sum(jnp.where(hit, (neighbours % ROWS)[:, None, :], 0), axis=2)
-        wanted = jnp.stack([wanted, wanted + ROWS], axis=1).reshape(SLOTS, SHARDS)
-        asked = exchange(wanted.T.reshape(SHARDS, 1, SLOTS), NODES)
-        codes = jnp.repeat(owners, 2, axis=0) * SLOTS + jnp.arange(SLOTS, dtype=jnp.int32)[:, None]
+        wanted, = call(ask_kernel, [((SHARDS, 1, DEGREE), jnp.int32)], neighbours)
+        asked = exchange(wanted, NODES)
     with jax.named_scope("project"):
         flat_weight = qkv_weight.reshape(width_in, 3 * COLS)
         projected = jnp.dot(features, flat_weight, preferred_element_type=F32)
@@ -258,18 +311,17 @@
         in_own = sorted_in[:512]
         in_other = jnp.concatenate([swap(sorted_in[512:, :ROWS], "c", 1), in_own[:, ROWS:]], axis=1)
     with jax.named_scope("serve"):
-        served, = call(serve_kernel, [((SHARDS * SLOTS, COLS), BF16)], asked, kv)
+        served, = call(serve_kernel, [((SHARDS * SLOTS, COLS), BF16)], asked, kv, scratch=WORK)
         near = exchange(served.reshape(SHARDS, SLOTS, COLS), NODES).reshape(SHARDS * SLOTS, COLS)
     with jax.named_scope("local"):
-        sums, = call(
-            local_kernel, [((ROWS, 4), F32)],
+        sums, query_turned, grad_turned = call(
+            local_kernel, [((2 * HEADS_DEV, ROWS), F32), ((COLS, ROWS), F32), ((COLS, ROWS), F32)],
             edge_bias, query, from_left, kv, from_right, out_grad, virtual_kv, member, scalars=1,
         )
     with jax.named_scope("near"):
         send, stats, dnear = call(
-            near_kernel, [((SHARDS * SLOTS, COLS), BF16), ((ROWS, 4), F32), ((ROWS, COLS), F32)],
-            edge_bias, codes.T, codes.reshape(1, SLOTS * ROWS), query, near, out_grad, sums, scalars=1,
-            scratch=[pltpu.VMEM((SLOTS * ROWS, COLS), BF16)],
+            near_kernel, [((SHARDS * SLOTS, COLS), BF16), ((2 * HEADS_DEV, ROWS), F32), ((COLS, ROWS), F32)],
+            edge_bias, neighbours, query_turned, near, grad_turned, sums, scalars=1, scratch=WORK,
         )
         back = exchange(send.reshape(SHARDS, SLOTS, COLS), NODES).reshape(SHARDS * SLOTS, COLS)
     with jax.named_scope("back"):
@@ -286,12 +338,12 @@
         vnode = vnode[:VIRTUAL] + vnode[VIRTUAL:]
         for bit in (1, 2):
             vnode = vnode + swap(vnode, "mp", bit)
-        vnode = jnp.concatenate(two_terms(vnode.reshape(8, 512)), axis=0)
+        vnode = jnp.concatenate(two_terms(jnp.concatenate([vnode[:, :512], vnode[:, 512:]], axis=0)), axis=0)
         tail = jnp.concatenate([jnp.pad(split, ((0, 8), (COLS, 0))), jnp.pad(vnode, ((0, 0), (0, COLS)))], axis=0)
     with jax.named_scope("total"):
         own, = call(
             total_kernel, [((ROWS + 32, 3 * COLS), BF16)],
-            asked.reshape(1, SHARDS * SLOTS), back, dquery, down, back_left, back_right, tail,
+            asked.reshape(SHARDS, DEGREE).T, back, dquery, down, back_left, back_right, tail, scratch=WORK,
         )
         other = swap(own, "c", 1)
     with jax.named_scope("feature"):
@@ -308,10 +360,10 @@
         vnode = term[128:136, :512] + term[136:, :512]
         tail = jnp.broadcast_to(vnode[None], (16, 8, 512))
         term = jnp.concatenate([term[:128].reshape(16, 8, 3 * COLS), tail], axis=2).astype(BF16)
-        term = jnp.sum(exchange(term, "z").astype(F32), axis=0)
-        out_scale = 1.0 / math.sqrt(ROWS * SHARDS)
-        weight_grad = (term[:, : 3 * COLS] * out_scale).reshape(8, 3, COLS)
-        vnode_grad = (term[:, 3 * COLS :] * out_scale).reshape(VIRTUAL, width_in)
+        weight_grad, vnode_grad = call(
+            finish_kernel, [((3, 8, COLS), F32), ((VIRTUAL, width_in), F32)], exchange(term, "z"),
+        )
+        weight_grad = weight_grad.transpose(1, 0, 2)
     return feature_grad, weight_grad, vnode_grad
 
 

time: 177 us -> 173 us (0.977)
    pallas_call x6 -> x8, Pallas kernels: 11.7 us -> 10.7 us  [call(): pl.pallas_call(kernel, out_shape=shapes, in_specs=[SMEM] * scalars + [VME...]
where the time goes in v3:
time: 173 us; the launch traced here: 172 us
  starting transfers between devices  79.2 us (46%)
  waiting for transfers between devices  54.1 us (31%)
  blocking collectives  16.6 us (10%)
  Pallas kernels  10.7 us (6%)
  local copies, waits for them, and re-layouts  4.65 us (3%)
  matrix products  3.55 us (2%)
  other arithmetic  2.59 us (1%)
    all_to_all x4, starting transfers between devices, exchange(): return lax.all_to_all(values, axis, split_axis=0, concat_axis=0, tiled=True)  42.9 us
    all_to_all x4, waiting for transfers between devices, exchange(): return lax.all_to_all(values, axis, split_axis=0, concat_axis=0, tiled=True)  30.9 us
    ppermute x7, starting transfers between devices, shift(): lax.ppermute(values, axis, [(i, (i + step) % count) for i in range(count)])  23.3 us
    ppermute x7, waiting for transfers between devices, shift(): lax.ppermute(values, axis, [(i, (i + step) % count) for i in range(count)])  23.1 us
    all_to_all x1, blocking collectives, exchange(): return lax.all_to_all(values, axis, split_axis=0, concat_axis=0, tiled=True)  16.6 us
    ppermute x4, starting transfers between devices, swap(): lax.ppermute(values, axis, [(i, i ^ bit) for i in range(SIZES[axis])])  13 us
    pallas_call x8, Pallas kernels, call(): pl.pallas_call(kernel, out_shape=shapes, in_specs=[SMEM] * scalars + [VME...  10.7 us
    unnamed x23, local copies, waits for them, and re-layouts  3.46 us
  transfers between devices with their start and end apart: 15, of which 9 were waited for; matrix products, arithmetic and copies ran while one was open for 5% of the time, Pallas kernels for 3%

profile of v3, /device:TPU:32, one launch (start us, length us, event | category | flops | bytes accessed | tf_op | source)
XLA Modules:
  0.0 172.4 jit_solution(17677003826272822778)
XLA Ops:
  2.1 19.0 %all-to-all-start = ((s32[128,1,4]{2,1,0:T(1,128)}), s32[128,1,4]{2,1,0:T(1,128)S(1)}, u32[]{:S(2)}, u32[]{:S(2)}) async-start(s32[128,1,4]{2,1,0:T(1,128)} %ask.1), calls=%async_computation | async-start | bytes 131072 | tf_op jit(solution)/shard_map/ask/all_to_all | solution.py:273
  21.1 1.8 %copy.28 = bf16[1024,3,256]{0,2,1:T(8,128)(2,1)S(1)} copy(bf16[1024,3,256]{2,0,1:T(8,128)(2,1)} %param.10) | data formatting | bytes 3145728 | tf_op args[1]
  23.6 11.8 %all-to-all-done.asked_ref = s32[128,1,4]{2,1,0:T(1,128)S(1)} async-done(((s32[128,1,4]{2,1,0:T(1,128)}), s32[128,1,4]{2,1,0:T(1,128)S(1)}, u32[]{:S(2)}, u32[]{:S(2)}) %all-to-all-start) | async-done | bytes 2080 | tf_op jit(solution)/shard_map/ask/all_to_all | solution.py:273
  35.4 1.6 serve.1
  37.0 6.4 %all-to-all-start.1 = ((bf16[128,8,256]{2,1,0:T(8,128)(2,1)}), bf16[128,8,256]{2,1,0:T(8,128)(2,1)S(1)}, u32[]{:S(2)}, u32[]{:S(2)}) async-start(bf16[128,8,256]{2,1,0:T(8,128)(2,1)} %bitcast.3), calls=%async_computation.1 | async-start | bytes 1048576 | tf_op jit(solution)/shard_map/serve/all_to_all | solution.py:273
  43.4 2.1 %collective-permute-start = (bf16[128,512]{1,0:T(8,128)(2,1)S(1)}, bf16[128,512]{1,0:T(8,128)(2,1)S(1)}, u32[]{:S(2)}, u32[]{:S(2)}) collective-permute-start(bf16[128,512]{1,0:T(8,128)(2,1)S(1)} %slice.90.own_ref.kv_ref), channel_id=1, source_target_pairs={{0,4},{4,8},{8,12},{12,16},{16,20},{20,24},{24,28},{28,32},{32,36}... | collective-permute-start | bytes 393224 | tf_op jit(solution)/shard_map/project/ppermute | solution.py:278
  45.4 5.6 %collective-permute-start.1 = (bf16[128,512]{1,0:T(8,128)(2,1)S(1)}, bf16[128,512]{1,0:T(8,128)(2,1)S(1)}, u32[]{:S(2)}, u32[]{:S(2)}) collective-permute-start(bf16[128,512]{1,0:T(8,128)(2,1)S(1)} %slice.90.own_ref.kv_ref), channel_id=1, source_target_pairs={{0,508},{4,0},{8,4},{12,8},{16,12},{20,16},{24,20},{28,24},{32,28}... | collective-permute-start | bytes 393224 | tf_op jit(solution)/shard_map/project/ppermute | solution.py:278
  51.0 0.9 slice.60.query_ref
  52.6 14.3 %collective-permute-done.left_ref = bf16[128,512]{1,0:T(8,128)(2,1)S(1)} collective-permute-done((bf16[128,512]{1,0:T(8,128)(2,1)S(1)}, bf16[128,512]{1,0:T(8,128)(2,1)S(1)}, u32[]{:S(2)}, u32[]{:S(2)}) %collective-permute-start) | collective-permute-done | bytes 131104 | tf_op jit(solution)/shard_map/project/ppermute | solution.py:278
  66.9 1.4 local.1
  68.3 8.1 %all-to-all-done.1 = bf16[128,8,256]{2,1,0:T(8,128)(2,1)S(1)} async-done(((bf16[128,8,256]{2,1,0:T(8,128)(2,1)}), bf16[128,8,256]{2,1,0:T(8,128)(2,1)S(1)}, u32[]{:S(2)}, u32[]{:S(2)}) %all-to-all-start.1) | async-done | bytes 524320 | tf_op jit(solution)/shard_map/serve/all_to_all | solution.py:273
  76.4 2.3 %near.1 = (bf16[1024,256]{1,0:T(8,128)(2,1)}, f32[4,128]{1,0:T(4,128)S(1)}, f32[256,128]{1,0:T(8,128)S(1)}) custom-call(f32[3,2]{1,0:T(4,128)S(1)} %copy.31.bias_ref, s32[4,128]{1,0:T(4,128)S(1)} %copy-done.2, f32[256,128]{1,0:T(8,128)S(1)} %get-tuple-element.16.query_ref, bf16[1024,256]{1,0:T(8,128)(2,1)S(1)} %bitcast.16, ...), custom_call_target="tpu_custom_call" | custom-call | flops 100000000 | bytes 1447960 | tf_op jit(solution)/shard_map/near/pallas_call | solution.py:261
  78.7 8.9 %all-to-all-start.2 = ((bf16[128,8,256]{2,1,0:T(8,128)(2,1)}), bf16[128,8,256]{2,1,0:T(8,128)(2,1)S(1)}, u32[]{:S(2)}, u32[]{:S(2)}) async-start(bf16[128,8,256]{2,1,0:T(8,128)(2,1)} %bitcast.5), calls=%async_computation.2 | async-start | bytes 1048576 | tf_op jit(solution)/shard_map/near/all_to_all | solution.py:273
  87.7 3.1 %back.1 = (bf16[128,256]{1,0:T(8,128)(2,1)S(1)}, bf16[128,512]{1,0:T(8,128)(2,1)S(1)}, f32[128,512]{1,0:T(8,128)S(1)}, bf16[128,512]{1,0:T(8,128)(2,1)S(1)}, f32[4,512]{1,0:T(4,128)S(1)}) custom-call(f32[3,2]{1,0:T(4,128)S(1)} %copy.31.bias_ref, f32[128,256]{1,0:T(8,128)S(1)} %slice.60.query_ref, bf16[128,512]{1,0:T(8,128)(2,1)S(1)} %collective-permute-done.left_ref, ...), custom_call_target="tpu_custom_call" | custom-call | flops 100000000 | bytes 1331224 | tf_op jit(solution)/shard_map/back/pallas_call | solution.py:261
  91.1 3.7 %collective-permute-start.4 = (f32[4,1024]{1,0:T(4,128)S(1)}, f32[4,1024]{1,0:T(4,128)S(1)}, u32[]{:S(2)}, u32[]{:S(2)}) collective-permute-start(f32[4,1024]{1,0:T(4,128)S(1)} %slice_add_fusion.1), channel_id=1, source_target_pairs={{0,1},{1,0},{2,3},{3,2},{4,5},{5,4},{6,7},{7,6},{8,9},{9,8},{10,11... | collective-permute-start | bytes 49160 | tf_op jit(solution)/shard_map/virtual/ppermute | solution.py:282
  94.8 1.9 %fusion.2 = bf16[1024,160]{1,0:T(8,128)(2,1)S(1)} fusion(s32[1024]{0:T(1024)S(1)} %fusion.27, bf16[4,1024]{1,0:T(4,128)(2,1)} %param.11, bf16[128,1024]{1,0:T(8,128)(2,1)} %param.9, bf16[160]{0:T(256)(128)(2,1)S(1)} %pad.17.clone), kind=kOutput, calls=%fused_computation.4 | convolution fusion | flops 338067456 | bytes 602432 | tf_op jit(solution)/shard_map/select/dot_general | solution.py:37
  97.5 1.9 %collective-permute-start.9 = (bf16[512,128]{1,0:T(8,128)(2,1)S(1)}, bf16[512,128]{1,0:T(8,128)(2,1)}, u32[]{:S(2)}, u32[]{:S(2)}) collective-permute-start(bf16[512,128]{1,0:T(8,128)(2,1)S(1)} %slice.69), channel_id=1, source_target_pairs={{0,4},{4,0},{1,5},{5,1},{2,6},{6,2},{3,7},{7,3},{8,12},{12,8},{9,1... | collective-permute-start | bytes 393224 | tf_op jit(solution)/shard_map/select/ppermute | solution.py:282
  99.5 4.8 %collective-permute-start.5 = (f32[4,1024]{1,0:T(4,128)S(1)}, f32[4,1024]{1,0:T(4,128)S(1)}, u32[]{:S(2)}, u32[]{:S(2)}) collective-permute-start(f32[4,1024]{1,0:T(4,128)S(1)} %fusion.50), channel_id=1, source_target_pairs={{0,2},{1,3},{2,0},{3,1},{4,6},{5,7},{6,4},{7,5},{8,10},{9,11},{10,... | collective-permute-start | bytes 49160 | tf_op jit(solution)/shard_map/virtual/ppermute | solution.py:282
  104.3 2.1 %collective-permute-start.2 = (bf16[128,512]{1,0:T(8,128)(2,1)S(1)}, bf16[128,512]{1,0:T(8,128)(2,1)S(1)}, u32[]{:S(2)}, u32[]{:S(2)}) collective-permute-start(bf16[128,512]{1,0:T(8,128)(2,1)S(1)} %get-tuple-element.24), channel_id=1, source_target_pairs={{0,4},{4,8},{8,12},{12,16},{16,20},{20,24},{24,28},{28,32},{32,36}... | collective-permute-start | bytes 393224 | tf_op jit(solution)/shard_map/back/ppermute | solution.py:278
  106.5 5.5 %collective-permute-start.3 = (bf16[128,512]{1,0:T(8,128)(2,1)S(1)}, bf16[128,512]{1,0:T(8,128)(2,1)S(1)}, u32[]{:S(2)}, u32[]{:S(2)}) collective-permute-start(bf16[128,512]{1,0:T(8,128)(2,1)S(1)} %get-tuple-element.25), channel_id=1, source_target_pairs={{0,508},{4,0},{8,4},{12,8},{16,12},{20,16},{24,20},{28,24},{32,28}... | collective-permute-start | bytes 393224 | tf_op jit(solution)/shard_map/back/ppermute | solution.py:278
  112.1 3.3 %collective-permute-done.2.from_left_ref = bf16[128,512]{1,0:T(8,128)(2,1)S(1)} collective-permute-done((bf16[128,512]{1,0:T(8,128)(2,1)S(1)}, bf16[128,512]{1,0:T(8,128)(2,1)S(1)}, u32[]{:S(2)}, u32[]{:S(2)}) %collective-permute-start.2) | collective-permute-done | bytes 131104 | tf_op jit(solution)/shard_map/back/ppermute | solution.py:278
  115.5 5.2 %all-to-all-done.2 = bf16[128,8,256]{2,1,0:T(8,128)(2,1)S(1)} async-done(((bf16[128,8,256]{2,1,0:T(8,128)(2,1)}), bf16[128,8,256]{2,1,0:T(8,128)(2,1)S(1)}, u32[]{:S(2)}, u32[]{:S(2)}) %all-to-all-start.2) | async-done | bytes 524320 | tf_op jit(solution)/shard_map/near/all_to_all | solution.py:273
  121.0 2.6 %collective-permute-start.10 = (bf16[160,768]{1,0:T(8,128)(2,1)S(1)}, bf16[160,768]{1,0:T(8,128)(2,1)S(1)}, u32[]{:S(2)}, u32[]{:S(2)}) collective-permute-start(bf16[160,768]{1,0:T(8,128)(2,1)S(1)} %total.1.own_ref), channel_id=1, source_target_pairs={{0,4},{4,0},{1,5},{5,1},{2,6},{6,2},{3,7},{7,3},{8,12},{12,8},{9,1... | collective-permute-start | bytes 737288 | tf_op jit(solution)/shard_map/total/ppermute | solution.py:282
  123.7 1.0 pad_maximum_fusion.1.in_other_ref
  125.3 16.6 %all_to_all.25 = bf16[4,144,768]{2,1,0:T(8,128)(2,1)S(1)} all-to-all(bf16[4,144,768]{2,1,0:T(8,128)(2,1)S(1)} %weight.2), channel_id=1, replica_groups=mesh['z'=16,'x'=4,'c'=2,'mp'=4] {'x'}, dimensions={0} | all-to-all | bytes 1769472 | tf_op jit(solution)/shard_map/weight/all_to_all | solution.py:273
  142.8 8.6 %all-to-all-start.4 = ((bf16[16,8,1280]{2,1,0:T(8,128)(2,1)}), bf16[16,8,1280]{2,1,0:T(8,128)(2,1)S(1)}, u32[]{:S(2)}, u32[]{:S(2)}) async-start(bf16[16,8,1280]{2,1,0:T(8,128)(2,1)} %pad_maximum_fusion), calls=%async_computation.4 | async-start | bytes 655360 | tf_op jit(solution)/shard_map/weight/all_to_all | solution.py:273
  151.9 2.1 %collective-permute-start.8 = (bf16[128,256]{1,0:T(8,128)(2,1)S(1)}, bf16[128,256]{1,0:T(8,128)(2,1)S(1)}, u32[]{:S(2)}, u32[]{:S(2)}) collective-permute-start(bf16[128,256]{1,0:T(8,128)(2,1)S(1)} %get-tuple-element.30), channel_id=1, source_target_pairs={{0,3},{1,0},{2,1},{3,2},{4,7},{5,4},{6,5},{7,6},{8,11},{9,8},{10,9... | collective-permute-start | bytes 196616 | tf_op jit(solution)/shard_map/feature/ppermute | solution.py:278
  154.0 3.9 %collective-permute-start.7 = (bf16[128,256]{1,0:T(8,128)(2,1)S(1)}, bf16[128,256]{1,0:T(8,128)(2,1)S(1)}, u32[]{:S(2)}, u32[]{:S(2)}) collective-permute-start(bf16[128,256]{1,0:T(8,128)(2,1)S(1)} %get-tuple-element.31), channel_id=1, source_target_pairs={{0,2},{1,3},{2,0},{3,1},{4,6},{5,7},{6,4},{7,5},{8,10},{9,11},{10,... | collective-permute-start | bytes 196616 | tf_op jit(solution)/shard_map/feature/ppermute | solution.py:278
  157.9 1.9 %collective-permute-start.6 = (bf16[128,256]{1,0:T(8,128)(2,1)S(1)}, bf16[128,256]{1,0:T(8,128)(2,1)S(1)}, u32[]{:S(2)}, u32[]{:S(2)}) collective-permute-start(bf16[128,256]{1,0:T(8,128)(2,1)S(1)} %get-tuple-element.29), channel_id=1, source_target_pairs={{0,1},{1,2},{2,3},{3,0},{4,5},{5,6},{6,7},{7,4},{8,9},{9,10},{10,1... | collective-permute-start | bytes 196616 | tf_op jit(solution)/shard_map/feature/ppermute | solution.py:278
  159.8 1.8 %collective-permute-done.7 = bf16[128,256]{1,0:T(8,128)(2,1)S(1)} collective-permute-done((bf16[128,256]{1,0:T(8,128)(2,1)S(1)}, bf16[128,256]{1,0:T(8,128)(2,1)S(1)}, u32[]{:S(2)}, u32[]{:S(2)}) %collective-permute-start.7) | collective-permute-done | bytes 65568 | tf_op jit(solution)/shard_map/feature/ppermute | solution.py:278
  161.7 3.6 %collective-permute-done.6 = bf16[128,256]{1,0:T(8,128)(2,1)S(1)} collective-permute-done((bf16[128,256]{1,0:T(8,128)(2,1)S(1)}, bf16[128,256]{1,0:T(8,128)(2,1)S(1)}, u32[]{:S(2)}, u32[]{:S(2)}) %collective-permute-start.6) | collective-permute-done | bytes 65568 | tf_op jit(solution)/shard_map/feature/ppermute | solution.py:278
  165.9 5.8 %all-to-all-done.4.parts_ref = bf16[16,8,1280]{2,1,0:T(8,128)(2,1)S(1)} async-done(((bf16[16,8,1280]{2,1,0:T(8,128)(2,1)}), bf16[16,8,1280]{2,1,0:T(8,128)(2,1)S(1)}, u32[]{:S(2)}, u32[]{:S(2)}) %all-to-all-start.4) | async-done | bytes 327712 | tf_op jit(solution)/shard_map/weight/all_to_all | solution.py:273
  (62 shorter events, 7.8 us)
Async XLA Ops:
  0.6 0.7 copy-start.1
  2.1 33.3 %all-to-all-start = ((s32[128,1,4]{2,1,0:T(1,128)}), s32[128,1,4]{2,1,0:T(1,128)S(1)}, u32[]{:S(2)}, u32[]{:S(2)}) async-start(s32[128,1,4]{2,1,0:T(1,128)} %ask.1), calls=%async_computation | async-start | bytes 131072 | tf_op jit(solution)/shard_map/ask/all_to_all | solution.py:273
  21.1 1.8 %copy-start.6 = (bf16[128,1024]{1,0:T(8,128)(2,1)S(1)}, bf16[128,1024]{1,0:T(8,128)(2,1)}, u32[]{:S(2)}) copy-start(bf16[128,1024]{1,0:T(8,128)(2,1)} %param.9) | copy-start | bytes 786436
  23.6 13.4 %copy-start.3 = (f32[128,768]{1,0:T(8,128)}, f32[128,768]{1,0:T(8,128)S(1)}, u32[]{:S(2)}) copy-start(f32[128,768]{1,0:T(8,128)S(1)} %fusion.45) | copy-start | bytes 1179652
  23.6 28.4 %copy-start.9 = (f32[3,2]{0,1:T(2,128)S(1)}, f32[3,2]{0,1:T(2,128)}, u32[]{:S(2)}) copy-start(f32[3,2]{0,1:T(2,128)} %param.12) | copy-start | bytes 76
  23.6 28.5 %copy-start.8 = (s32[128,4]{0,1:T(4,128)S(1)}, s32[128,4]{0,1:T(4,128)}, u32[]{:S(2)}) copy-start(s32[128,4]{0,1:T(4,128)} %param.15) | copy-start | bytes 6148
  23.6 28.6 %copy-start.7 = (bf16[4,1024]{1,0:T(4,128)(2,1)S(1)}, bf16[4,1024]{1,0:T(4,128)(2,1)}, u32[]{:S(2)}) copy-start(bf16[4,1024]{1,0:T(4,128)(2,1)} %param.11) | copy-start | bytes 24580
  23.6 43.3 %copy-start = (bf16[128,256]{1,0:T(8,128)(2,1)S(1)}, bf16[128,256]{1,0:T(8,128)(2,1)}, u32[]{:S(2)}) copy-start(bf16[128,256]{1,0:T(8,128)(2,1)} %grad_ref.3) | copy-start | bytes 196612
  37.0 39.4 %copy-start.2 = (s32[4,128]{1,0:T(4,128)S(1)}, s32[4,128]{1,0:T(4,128)}, u32[]{:S(2)}) copy-start(s32[4,128]{1,0:T(4,128)} %neighbours_ref.3) | copy-start | bytes 6148
  37.0 39.4 %all-to-all-start.1 = ((bf16[128,8,256]{2,1,0:T(8,128)(2,1)}), bf16[128,8,256]{2,1,0:T(8,128)(2,1)S(1)}, u32[]{:S(2)}, u32[]{:S(2)}) async-start(bf16[128,8,256]{2,1,0:T(8,128)(2,1)} %bitcast.3), calls=%async_computation.1 | async-start | bytes 1048576 | tf_op jit(solution)/shard_map/serve/all_to_all | solution.py:273
  43.4 23.5 %collective-permute-start = (bf16[128,512]{1,0:T(8,128)(2,1)S(1)}, bf16[128,512]{1,0:T(8,128)(2,1)S(1)}, u32[]{:S(2)}, u32[]{:S(2)}) collective-permute-start(bf16[128,512]{1,0:T(8,128)(2,1)S(1)} %slice.90.own_ref.kv_ref), channel_id=1, source_target_pairs={{0,4},{4,8},{8,12},{12,16},{16,20},{20,24},{24,28},{28,32},{32,36}... | collective-permute-start | bytes 393224 | tf_op jit(solution)/shard_map/project/ppermute | solution.py:278
  45.4 21.5 %collective-permute-start.1 = (bf16[128,512]{1,0:T(8,128)(2,1)S(1)}, bf16[128,512]{1,0:T(8,128)(2,1)S(1)}, u32[]{:S(2)}, u32[]{:S(2)}) collective-permute-start(bf16[128,512]{1,0:T(8,128)(2,1)S(1)} %slice.90.own_ref.kv_ref), channel_id=1, source_target_pairs={{0,508},{4,0},{8,4},{12,8},{16,12},{20,16},{24,20},{28,24},{32,28}... | collective-permute-start | bytes 393224 | tf_op jit(solution)/shard_map/project/ppermute | solution.py:278
  78.7 41.9 %all-to-all-start.2 = ((bf16[128,8,256]{2,1,0:T(8,128)(2,1)}), bf16[128,8,256]{2,1,0:T(8,128)(2,1)S(1)}, u32[]{:S(2)}, u32[]{:S(2)}) async-start(bf16[128,8,256]{2,1,0:T(8,128)(2,1)} %bitcast.5), calls=%async_computation.2 | async-start | bytes 1048576 | tf_op jit(solution)/shard_map/near/all_to_all | solution.py:273
  91.1 8.4 %collective-permute-start.4 = (f32[4,1024]{1,0:T(4,128)S(1)}, f32[4,1024]{1,0:T(4,128)S(1)}, u32[]{:S(2)}, u32[]{:S(2)}) collective-permute-start(f32[4,1024]{1,0:T(4,128)S(1)} %slice_add_fusion.1), channel_id=1, source_target_pairs={{0,1},{1,0},{2,3},{3,2},{4,5},{5,4},{6,7},{7,6},{8,9},{9,8},{10,11... | collective-permute-start | bytes 49160 | tf_op jit(solution)/shard_map/virtual/ppermute | solution.py:282
  96.7 0.8 copy-start.4
  97.5 26.2 %collective-permute-start.9 = (bf16[512,128]{1,0:T(8,128)(2,1)S(1)}, bf16[512,128]{1,0:T(8,128)(2,1)}, u32[]{:S(2)}, u32[]{:S(2)}) collective-permute-start(bf16[512,128]{1,0:T(8,128)(2,1)S(1)} %slice.69), channel_id=1, source_target_pairs={{0,4},{4,0},{1,5},{5,1},{2,6},{6,2},{3,7},{7,3},{8,12},{12,8},{9,1... | collective-permute-start | bytes 393224 | tf_op jit(solution)/shard_map/select/ppermute | solution.py:282
  99.5 12.5 %collective-permute-start.5 = (f32[4,1024]{1,0:T(4,128)S(1)}, f32[4,1024]{1,0:T(4,128)S(1)}, u32[]{:S(2)}, u32[]{:S(2)}) collective-permute-start(f32[4,1024]{1,0:T(4,128)S(1)} %fusion.50), channel_id=1, source_target_pairs={{0,2},{1,3},{2,0},{3,1},{4,6},{5,7},{6,4},{7,5},{8,10},{9,11},{10,... | collective-permute-start | bytes 49160 | tf_op jit(solution)/shard_map/virtual/ppermute | solution.py:282
  104.3 11.1 %collective-permute-start.2 = (bf16[128,512]{1,0:T(8,128)(2,1)S(1)}, bf16[128,512]{1,0:T(8,128)(2,1)S(1)}, u32[]{:S(2)}, u32[]{:S(2)}) collective-permute-start(bf16[128,512]{1,0:T(8,128)(2,1)S(1)} %get-tuple-element.24), channel_id=1, source_target_pairs={{0,4},{4,8},{8,12},{12,16},{16,20},{20,24},{24,28},{28,32},{32,36}... | collective-permute-start | bytes 393224 | tf_op jit(solution)/shard_map/back/ppermute | solution.py:278
  106.5 9.0 %collective-permute-start.3 = (bf16[128,512]{1,0:T(8,128)(2,1)S(1)}, bf16[128,512]{1,0:T(8,128)(2,1)S(1)}, u32[]{:S(2)}, u32[]{:S(2)}) collective-permute-start(bf16[128,512]{1,0:T(8,128)(2,1)S(1)} %get-tuple-element.25), channel_id=1, source_target_pairs={{0,508},{4,0},{8,4},{12,8},{16,12},{20,16},{24,20},{28,24},{32,28}... | collective-permute-start | bytes 393224 | tf_op jit(solution)/shard_map/back/ppermute | solution.py:278
  120.6 3.0 %copy-start.5 = (bf16[1024,160]{1,0:T(8,128)(2,1)S(1)}, bf16[1024,160]{1,0:T(8,128)(2,1)}, u32[]{:S(2)}) copy-start(bf16[1024,160]{1,0:T(8,128)(2,1)} %copy-done.4) | copy-start | bytes 983044
  121.0 3.7 %collective-permute-start.10 = (bf16[160,768]{1,0:T(8,128)(2,1)S(1)}, bf16[160,768]{1,0:T(8,128)(2,1)S(1)}, u32[]{:S(2)}, u32[]{:S(2)}) collective-permute-start(bf16[160,768]{1,0:T(8,128)(2,1)S(1)} %total.1.own_ref), channel_id=1, source_target_pairs={{0,4},{4,0},{1,5},{5,1},{2,6},{6,2},{3,7},{7,3},{8,12},{12,8},{9,1... | collective-permute-start | bytes 737288 | tf_op jit(solution)/shard_map/total/ppermute | solution.py:282
  142.8 29.0 %all-to-all-start.4 = ((bf16[16,8,1280]{2,1,0:T(8,128)(2,1)}), bf16[16,8,1280]{2,1,0:T(8,128)(2,1)S(1)}, u32[]{:S(2)}, u32[]{:S(2)}) async-start(bf16[16,8,1280]{2,1,0:T(8,128)(2,1)} %pad_maximum_fusion), calls=%async_computation.4 | async-start | bytes 655360 | tf_op jit(solution)/shard_map/weight/all_to_all | solution.py:273
  151.9 8.0 %collective-permute-start.8 = (bf16[128,256]{1,0:T(8,128)(2,1)S(1)}, bf16[128,256]{1,0:T(8,128)(2,1)S(1)}, u32[]{:S(2)}, u32[]{:S(2)}) collective-permute-start(bf16[128,256]{1,0:T(8,128)(2,1)S(1)} %get-tuple-element.30), channel_id=1, source_target_pairs={{0,3},{1,0},{2,1},{3,2},{4,7},{5,4},{6,5},{7,6},{8,11},{9,8},{10,9... | collective-permute-start | bytes 196616 | tf_op jit(solution)/shard_map/feature/ppermute | solution.py:278
  154.0 7.7 %collective-permute-start.7 = (bf16[128,256]{1,0:T(8,128)(2,1)S(1)}, bf16[128,256]{1,0:T(8,128)(2,1)S(1)}, u32[]{:S(2)}, u32[]{:S(2)}) collective-permute-start(bf16[128,256]{1,0:T(8,128)(2,1)S(1)} %get-tuple-element.31), channel_id=1, source_target_pairs={{0,2},{1,3},{2,0},{3,1},{4,6},{5,7},{6,4},{7,5},{8,10},{9,11},{10,... | collective-permute-start | bytes 196616 | tf_op jit(solution)/shard_map/feature/ppermute | solution.py:278
  157.9 7.4 %collective-permute-start.6 = (bf16[128,256]{1,0:T(8,128)(2,1)S(1)}, bf16[128,256]{1,0:T(8,128)(2,1)S(1)}, u32[]{:S(2)}, u32[]{:S(2)}) collective-permute-start(bf16[128,256]{1,0:T(8,128)(2,1)S(1)} %get-tuple-element.29), channel_id=1, source_target_pairs={{0,1},{1,2},{2,3},{3,0},{4,5},{5,6},{6,7},{7,4},{8,9},{9,10},{10,1... | collective-permute-start | bytes 196616 | tf_op jit(solution)/shard_map/feature/ppermute | solution.py:278

commit v4 on v3

--- a/solution.py
+++ b/solution.py
@@ -229,13 +229,11 @@
 def weight_kernel(in_own_ref, in_other_ref, own_ref, other_ref, out_ref):
     own, other = own_ref[...], other_ref[...]
     vnode = own[ROWS + 16 :].astype(F32) + other[ROWS + 16 :].astype(F32)
-    high, low = two_terms(vnode[:8] + vnode[8:])
-    tail = jnp.concatenate([high.astype(F32), low.astype(F32)], axis=0).astype(BF16)
+    vnode = vnode[:8] + vnode[8:]
     for part in range(4):
         at = slice(part * 128, (part + 1) * 128)
         term = mul(in_own_ref[at, :], own, NN) + mul(in_other_ref[at, :], other, NN)
-        out_ref[part, :128, :] = term.astype(BF16)
-        out_ref[part, 128:, :] = tail
+        out_ref[part] = jnp.concatenate([term, vnode], axis=0).astype(BF16)
 
 
 def finish_kernel(parts_ref, weight_ref, vnode_ref):
@@ -280,6 +278,11 @@
 
 def swap(values, axis, bit):
     return lax.ppermute(values, axis, [(i, i ^ bit) for i in range(SIZES[axis])])
+
+
+def sum_of_four(values, axis):
+    near, far, both = (swap(values, axis, bit) for bit in (1, 2, 3))
+    return (values + near) + (far + both)
 
 
 def two_terms(values):
@@ -310,6 +313,7 @@
         sorted_in = mul(chosen, rows_in, NT).astype(BF16)
         in_own = sorted_in[:512]
         in_other = jnp.concatenate([swap(sorted_in[512:, :ROWS], "c", 1), in_own[:, ROWS:]], axis=1)
+        from_left, from_right, in_own, in_other = lax.optimization_barrier((from_left, from_right, in_own, in_other))
     with jax.named_scope("serve"):
         served, = call(serve_kernel, [((SHARDS * SLOTS, COLS), BF16)], asked, kv, scratch=WORK)
         near = exchange(served.reshape(SHARDS, SLOTS, COLS), NODES).reshape(SHARDS * SLOTS, COLS)
@@ -336,8 +340,7 @@
         split = jnp.concatenate(two_terms(dvirtual), axis=0)
         vnode = mul(split, flat_weight[:, COLS:], NT)
         vnode = vnode[:VIRTUAL] + vnode[VIRTUAL:]
-        for bit in (1, 2):
-            vnode = vnode + swap(vnode, "mp", bit)
+        vnode = sum_of_four(vnode, "mp")
         vnode = jnp.concatenate(two_terms(jnp.concatenate([vnode[:, :512], vnode[:, 512:]], axis=0)), axis=0)
         tail = jnp.concatenate([jnp.pad(split, ((0, 8), (COLS, 0))), jnp.pad(vnode, ((0, 0), (0, COLS)))], axis=0)
     with jax.named_scope("total"):
@@ -355,9 +358,9 @@
             summed = summed + shift(piece, "mp", step).astype(F32)
         feature_grad = summed.astype(BF16)
     with jax.named_scope("weight"):
-        term, = call(weight_kernel, [((4, 144, 3 * COLS), BF16)], in_own, in_other, own, other, flops=3 * 10**8)
+        term, = call(weight_kernel, [((4, 136, 3 * COLS), BF16)], in_own, in_other, own, other, flops=3 * 10**8)
         term = jnp.sum(exchange(term, "x").astype(F32), axis=0)
-        vnode = term[128:136, :512] + term[136:, :512]
+        vnode = term[128:, :512]
         tail = jnp.broadcast_to(vnode[None], (16, 8, 512))
         term = jnp.concatenate([term[:128].reshape(16, 8, 3 * COLS), tail], axis=2).astype(BF16)
         weight_grad, vnode_grad = call(

time: 173 us -> 171 us (0.988)
  the two profiles are of different devices: /device:TPU:32 before, /device:TPU:16 now
where the time goes in v4:
time: 171 us; the launch traced here: 170 us
  starting transfers between devices  82.4 us (48%)
  waiting for transfers between devices  48.6 us (28%)
  blocking collectives  17.2 us (10%)
  Pallas kernels  10.7 us (6%)
  local copies, waits for them, and re-layouts  4.62 us (3%)
  matrix products  3.81 us (2%)
    all_to_all x4, starting transfers between devices, exchange(): return lax.all_to_all(values, axis, split_axis=0, concat_axis=0, tiled=True)  42 us
    ppermute x7, starting transfers between devices, shift(): lax.ppermute(values, axis, [(i, (i + step) % count) for i in range(count)])  26 us
    all_to_all x4, waiting for transfers between devices, exchange(): return lax.all_to_all(values, axis, split_axis=0, concat_axis=0, tiled=True)  23.7 us
    ppermute x7, waiting for transfers between devices, shift(): lax.ppermute(values, axis, [(i, (i + step) % count) for i in range(count)])  23.4 us
    all_to_all x1, blocking collectives, exchange(): return lax.all_to_all(values, axis, split_axis=0, concat_axis=0, tiled=True)  17.2 us
    ppermute x5, starting transfers between devices, swap(): lax.ppermute(values, axis, [(i, i ^ bit) for i in range(SIZES[axis])])  14.4 us
    pallas_call x8, Pallas kernels, call(): pl.pallas_call(kernel, out_shape=shapes, in_specs=[SMEM] * scalars + [VME...  10.7 us
    unnamed x23, local copies, waits for them, and re-layouts  3.43 us
  transfers between devices with their start and end apart: 16, of which 9 were waited for; matrix products, arithmetic and copies ran while one was open for 5% of the time, Pallas kernels for 3%

profile of v4, /device:TPU:16, one launch (start us, length us, event | category | flops | bytes accessed | tf_op | source)
XLA Modules:
  0.0 170.2 jit_solution(15663136072141932424)
XLA Ops:
  2.1 19.8 %all-to-all-start = ((s32[128,1,4]{2,1,0:T(1,128)}), s32[128,1,4]{2,1,0:T(1,128)S(1)}, u32[]{:S(2)}, u32[]{:S(2)}) async-start(s32[128,1,4]{2,1,0:T(1,128)} %ask.1), calls=%async_computation | async-start | bytes 131072 | tf_op jit(solution)/shard_map/ask/all_to_all | solution.py:271
  21.9 1.8 %copy.28 = bf16[1024,3,256]{0,2,1:T(8,128)(2,1)S(1)} copy(bf16[1024,3,256]{2,0,1:T(8,128)(2,1)} %param.10) | data formatting | bytes 3145728 | tf_op args[1]
  25.1 11.2 %all-to-all-done.asked_ref = s32[128,1,4]{2,1,0:T(1,128)S(1)} async-done(((s32[128,1,4]{2,1,0:T(1,128)}), s32[128,1,4]{2,1,0:T(1,128)S(1)}, u32[]{:S(2)}, u32[]{:S(2)}) %all-to-all-start) | async-done | bytes 2080 | tf_op jit(solution)/shard_map/ask/all_to_all | solution.py:271
  36.3 1.5 serve.1
  37.9 6.2 %all-to-all-start.1 = ((bf16[128,8,256]{2,1,0:T(8,128)(2,1)}), bf16[128,8,256]{2,1,0:T(8,128)(2,1)S(1)}, u32[]{:S(2)}, u32[]{:S(2)}) async-start(bf16[128,8,256]{2,1,0:T(8,128)(2,1)} %bitcast.3), calls=%async_computation.1 | async-start | bytes 1048576 | tf_op jit(solution)/shard_map/serve/all_to_all | solution.py:271
  44.1 1.9 %collective-permute-start = (bf16[128,512]{1,0:T(8,128)(2,1)S(1)}, bf16[128,512]{1,0:T(8,128)(2,1)S(1)}, u32[]{:S(2)}, u32[]{:S(2)}) collective-permute-start(bf16[128,512]{1,0:T(8,128)(2,1)S(1)} %slice.82.own_ref.kv_ref), channel_id=1, source_target_pairs={{0,4},{4,8},{8,12},{12,16},{16,20},{20,24},{24,28},{28,32},{32,36}... | collective-permute-start | bytes 393224 | tf_op jit(solution)/shard_map/project/ppermute | solution.py:276
  46.0 7.0 %collective-permute-start.1 = (bf16[128,512]{1,0:T(8,128)(2,1)S(1)}, bf16[128,512]{1,0:T(8,128)(2,1)S(1)}, u32[]{:S(2)}, u32[]{:S(2)}) collective-permute-start(bf16[128,512]{1,0:T(8,128)(2,1)S(1)} %slice.82.own_ref.kv_ref), channel_id=1, source_target_pairs={{0,508},{4,0},{8,4},{12,8},{16,12},{20,16},{24,20},{28,24},{32,28}... | collective-permute-start | bytes 393224 | tf_op jit(solution)/shard_map/project/ppermute | solution.py:276
  54.1 2.1 %collective-permute-start.2 = (bf16[512,128]{1,0:T(8,128)(2,1)S(1)}, bf16[512,128]{1,0:T(8,128)(2,1)S(1)}, u32[]{:S(2)}, u32[]{:S(2)}) collective-permute-start(bf16[512,128]{1,0:T(8,128)(2,1)S(1)} %slice.59), channel_id=1, source_target_pairs={{0,4},{4,0},{1,5},{5,1},{2,6},{6,2},{3,7},{7,3},{8,12},{12,8},{9,1... | collective-permute-start | bytes 393224 | tf_op jit(solution)/shard_map/select/ppermute | solution.py:280
  57.8 15.1 %collective-permute-done.left_ref = bf16[128,512]{1,0:T(8,128)(2,1)S(1)} collective-permute-done((bf16[128,512]{1,0:T(8,128)(2,1)S(1)}, bf16[128,512]{1,0:T(8,128)(2,1)S(1)}, u32[]{:S(2)}, u32[]{:S(2)}) %collective-permute-start) | collective-permute-done | bytes 131104 | tf_op jit(solution)/shard_map/project/ppermute | solution.py:276
  72.9 1.4 local.1
  74.3 2.0 %all-to-all-done.1 = bf16[128,8,256]{2,1,0:T(8,128)(2,1)S(1)} async-done(((bf16[128,8,256]{2,1,0:T(8,128)(2,1)}), bf16[128,8,256]{2,1,0:T(8,128)(2,1)S(1)}, u32[]{:S(2)}, u32[]{:S(2)}) %all-to-all-start.1) | async-done | bytes 524320 | tf_op jit(solution)/shard_map/serve/all_to_all | solution.py:271
  76.3 2.2 %near.1 = (bf16[1024,256]{1,0:T(8,128)(2,1)}, f32[4,128]{1,0:T(4,128)S(1)}, f32[256,128]{1,0:T(8,128)S(1)}) custom-call(f32[3,2]{1,0:T(4,128)S(1)} %copy.32.bias_ref, s32[4,128]{1,0:T(4,128)S(1)} %copy-done.2, f32[256,128]{1,0:T(8,128)S(1)} %get-tuple-element.22.query_ref, bf16[1024,256]{1,0:T(8,128)(2,1)S(1)} %bitcast.16, ...), custom_call_target="tpu_custom_call" | custom-call | flops 100000000 | bytes 1447960 | tf_op jit(solution)/shard_map/near/pallas_call | solution.py:259
  78.5 9.9 %all-to-all-start.2 = ((bf16[128,8,256]{2,1,0:T(8,128)(2,1)}), bf16[128,8,256]{2,1,0:T(8,128)(2,1)S(1)}, u32[]{:S(2)}, u32[]{:S(2)}) async-start(bf16[128,8,256]{2,1,0:T(8,128)(2,1)} %bitcast.5), calls=%async_computation.2 | async-start | bytes 1048576 | tf_op jit(solution)/shard_map/near/all_to_all | solution.py:271
  88.4 3.2 %back.1 = (bf16[128,256]{1,0:T(8,128)(2,1)S(1)}, bf16[128,512]{1,0:T(8,128)(2,1)S(1)}, f32[128,512]{1,0:T(8,128)S(1)}, bf16[128,512]{1,0:T(8,128)(2,1)S(1)}, f32[4,512]{1,0:T(4,128)S(1)}) custom-call(f32[3,2]{1,0:T(4,128)S(1)} %copy.32.bias_ref, f32[128,256]{1,0:T(8,128)S(1)} %slice.56.query_ref, bf16[128,512]{1,0:T(8,128)(2,1)S(1)} %collective-permute-done.left_ref, ...), custom_call_target="tpu_custom_call" | custom-call | flops 100000000 | bytes 1331224 | tf_op jit(solution)/shard_map/back/pallas_call | solution.py:259
  91.6 1.5 fusion.3
  93.1 2.2 %collective-permute-start.6 = (f32[4,1024]{1,0:T(4,128)S(1)}, f32[4,1024]{1,0:T(4,128)S(1)}, u32[]{:S(2)}, u32[]{:S(2)}) collective-permute-start(f32[4,1024]{1,0:T(4,128)S(1)} %slice_add_fusion), channel_id=1, source_target_pairs={{0,2},{1,3},{2,0},{3,1},{4,6},{5,7},{6,4},{7,5},{8,10},{9,11},{10,... | collective-permute-start | bytes 49160 | tf_op jit(solution)/shard_map/virtual/ppermute | solution.py:280
  95.4 4.3 %collective-permute-start.7 = (f32[4,1024]{1,0:T(4,128)S(1)}, f32[4,1024]{1,0:T(4,128)S(1)}, u32[]{:S(2)}, u32[]{:S(2)}) collective-permute-start(f32[4,1024]{1,0:T(4,128)S(1)} %slice_add_fusion), channel_id=1, source_target_pairs={{0,3},{1,2},{2,1},{3,0},{4,7},{5,6},{6,5},{7,4},{8,11},{9,10},{10,... | collective-permute-start | bytes 49160 | tf_op jit(solution)/shard_map/virtual/ppermute | solution.py:280
  99.7 3.9 %collective-permute-start.5 = (f32[4,1024]{1,0:T(4,128)S(1)}, f32[4,1024]{1,0:T(4,128)S(1)}, u32[]{:S(2)}, u32[]{:S(2)}) collective-permute-start(f32[4,1024]{1,0:T(4,128)S(1)} %slice_add_fusion), channel_id=1, source_target_pairs={{0,1},{1,0},{2,3},{3,2},{4,5},{5,4},{6,7},{7,6},{8,9},{9,8},{10,11... | collective-permute-start | bytes 49160 | tf_op jit(solution)/shard_map/virtual/ppermute | solution.py:280
  103.6 1.9 %collective-permute-start.3 = (bf16[128,512]{1,0:T(8,128)(2,1)S(1)}, bf16[128,512]{1,0:T(8,128)(2,1)S(1)}, u32[]{:S(2)}, u32[]{:S(2)}) collective-permute-start(bf16[128,512]{1,0:T(8,128)(2,1)S(1)} %get-tuple-element.30), channel_id=1, source_target_pairs={{0,4},{4,8},{8,12},{12,16},{16,20},{20,24},{24,28},{28,32},{32,36}... | collective-permute-start | bytes 393224 | tf_op jit(solution)/shard_map/back/ppermute | solution.py:276
  105.5 7.0 %collective-permute-start.4 = (bf16[128,512]{1,0:T(8,128)(2,1)S(1)}, bf16[128,512]{1,0:T(8,128)(2,1)S(1)}, u32[]{:S(2)}, u32[]{:S(2)}) collective-permute-start(bf16[128,512]{1,0:T(8,128)(2,1)S(1)} %get-tuple-element.31), channel_id=1, source_target_pairs={{0,508},{4,0},{8,4},{12,8},{16,12},{20,16},{24,20},{28,24},{32,28}... | collective-permute-start | bytes 393224 | tf_op jit(solution)/shard_map/back/ppermute | solution.py:276
  112.6 4.5 %collective-permute-done.3.from_left_ref = bf16[128,512]{1,0:T(8,128)(2,1)S(1)} collective-permute-done((bf16[128,512]{1,0:T(8,128)(2,1)S(1)}, bf16[128,512]{1,0:T(8,128)(2,1)S(1)}, u32[]{:S(2)}, u32[]{:S(2)}) %collective-permute-start.3) | collective-permute-done | bytes 131104 | tf_op jit(solution)/shard_map/back/ppermute | solution.py:276
  117.0 3.5 %all-to-all-done.2 = bf16[128,8,256]{2,1,0:T(8,128)(2,1)S(1)} async-done(((bf16[128,8,256]{2,1,0:T(8,128)(2,1)}), bf16[128,8,256]{2,1,0:T(8,128)(2,1)S(1)}, u32[]{:S(2)}, u32[]{:S(2)}) %all-to-all-start.2) | async-done | bytes 524320 | tf_op jit(solution)/shard_map/near/all_to_all | solution.py:271
  120.9 1.9 %collective-permute-start.11 = (bf16[160,768]{1,0:T(8,128)(2,1)S(1)}, bf16[160,768]{1,0:T(8,128)(2,1)S(1)}, u32[]{:S(2)}, u32[]{:S(2)}) collective-permute-start(bf16[160,768]{1,0:T(8,128)(2,1)S(1)} %total.1.own_ref), channel_id=1, source_target_pairs={{0,4},{4,0},{1,5},{5,1},{2,6},{6,2},{3,7},{7,3},{8,12},{12,8},{9,1... | collective-permute-start | bytes 737288 | tf_op jit(solution)/shard_map/total/ppermute | solution.py:280
  122.8 1.5 collective-permute-done.11.other_ref
  124.9 17.2 %all_to_all.25 = bf16[4,136,768]{2,1,0:T(8,128)(2,1)S(1)} all-to-all(bf16[4,136,768]{2,1,0:T(8,128)(2,1)S(1)} %weight.2), channel_id=1, replica_groups=mesh['z'=16,'x'=4,'c'=2,'mp'=4] {'x'}, dimensions={0} | all-to-all | bytes 1671168 | tf_op jit(solution)/shard_map/weight/all_to_all | solution.py:271
  143.0 6.2 %all-to-all-start.4 = ((bf16[16,8,1280]{2,1,0:T(8,128)(2,1)}), bf16[16,8,1280]{2,1,0:T(8,128)(2,1)S(1)}, u32[]{:S(2)}, u32[]{:S(2)}) async-start(bf16[16,8,1280]{2,1,0:T(8,128)(2,1)} %pad_maximum_fusion), calls=%async_computation.4 | async-start | bytes 655360 | tf_op jit(solution)/shard_map/weight/all_to_all | solution.py:271
  149.7 2.4 %collective-permute-start.10 = (bf16[128,256]{1,0:T(8,128)(2,1)S(1)}, bf16[128,256]{1,0:T(8,128)(2,1)S(1)}, u32[]{:S(2)}, u32[]{:S(2)}) collective-permute-start(bf16[128,256]{1,0:T(8,128)(2,1)S(1)} %get-tuple-element.38), channel_id=1, source_target_pairs={{0,3},{1,0},{2,1},{3,2},{4,7},{5,4},{6,5},{7,6},{8,11},{9,8},{10,9... | collective-permute-start | bytes 196616 | tf_op jit(solution)/shard_map/feature/ppermute | solution.py:276
  152.0 3.6 %collective-permute-start.9 = (bf16[128,256]{1,0:T(8,128)(2,1)S(1)}, bf16[128,256]{1,0:T(8,128)(2,1)S(1)}, u32[]{:S(2)}, u32[]{:S(2)}) collective-permute-start(bf16[128,256]{1,0:T(8,128)(2,1)S(1)} %get-tuple-element.39), channel_id=1, source_target_pairs={{0,2},{1,3},{2,0},{3,1},{4,6},{5,7},{6,4},{7,5},{8,10},{9,11},{10,... | collective-permute-start | bytes 196616 | tf_op jit(solution)/shard_map/feature/ppermute | solution.py:276
  155.6 2.3 %collective-permute-start.8 = (bf16[128,256]{1,0:T(8,128)(2,1)S(1)}, bf16[128,256]{1,0:T(8,128)(2,1)S(1)}, u32[]{:S(2)}, u32[]{:S(2)}) collective-permute-start(bf16[128,256]{1,0:T(8,128)(2,1)S(1)} %get-tuple-element.37), channel_id=1, source_target_pairs={{0,1},{1,2},{2,3},{3,0},{4,5},{5,6},{6,7},{7,4},{8,9},{9,10},{10,1... | collective-permute-start | bytes 196616 | tf_op jit(solution)/shard_map/feature/ppermute | solution.py:276
  158.0 2.3 %collective-permute-done.9 = bf16[128,256]{1,0:T(8,128)(2,1)S(1)} collective-permute-done((bf16[128,256]{1,0:T(8,128)(2,1)S(1)}, bf16[128,256]{1,0:T(8,128)(2,1)S(1)}, u32[]{:S(2)}, u32[]{:S(2)}) %collective-permute-start.9) | collective-permute-done | bytes 65568 | tf_op jit(solution)/shard_map/feature/ppermute | solution.py:276
  160.3 1.5 collective-permute-done.8
  162.5 7.1 %all-to-all-done.4.parts_ref = bf16[16,8,1280]{2,1,0:T(8,128)(2,1)S(1)} async-done(((bf16[16,8,1280]{2,1,0:T(8,128)(2,1)}), bf16[16,8,1280]{2,1,0:T(8,128)(2,1)S(1)}, u32[]{:S(2)}, u32[]{:S(2)}) %all-to-all-start.4) | async-done | bytes 327712 | tf_op jit(solution)/shard_map/weight/all_to_all | solution.py:271
  (63 shorter events, 9.3 us)
Async XLA Ops:
  0.6 0.7 copy-start.1
  2.1 34.2 %all-to-all-start = ((s32[128,1,4]{2,1,0:T(1,128)}), s32[128,1,4]{2,1,0:T(1,128)S(1)}, u32[]{:S(2)}, u32[]{:S(2)}) async-start(s32[128,1,4]{2,1,0:T(1,128)} %ask.1), calls=%async_computation | async-start | bytes 131072 | tf_op jit(solution)/shard_map/ask/all_to_all | solution.py:271
  21.9 1.8 %copy-start.6 = (bf16[128,1024]{1,0:T(8,128)(2,1)S(1)}, bf16[128,1024]{1,0:T(8,128)(2,1)}, u32[]{:S(2)}) copy-start(bf16[128,1024]{1,0:T(8,128)(2,1)} %param.9) | copy-start | bytes 786436
  23.7 32.5 %copy-start.3 = (bf16[1024,3,256]{0,2,1:T(8,128)(2,1)}, bf16[1024,3,256]{0,2,1:T(8,128)(2,1)S(1)}, u32[]{:S(2)}) copy-start(bf16[1024,3,256]{0,2,1:T(8,128)(2,1)S(1)} %copy.28) | copy-start | bytes 4718596
  24.4 0.8 copy-start.5
  25.1 28.0 %copy-start.7 = (bf16[4,1024]{1,0:T(4,128)(2,1)S(1)}, bf16[4,1024]{1,0:T(4,128)(2,1)}, u32[]{:S(2)}) copy-start(bf16[4,1024]{1,0:T(4,128)(2,1)} %param.11) | copy-start | bytes 24580
  37.9 38.4 %all-to-all-start.1 = ((bf16[128,8,256]{2,1,0:T(8,128)(2,1)}), bf16[128,8,256]{2,1,0:T(8,128)(2,1)S(1)}, u32[]{:S(2)}, u32[]{:S(2)}) async-start(bf16[128,8,256]{2,1,0:T(8,128)(2,1)} %bitcast.3), calls=%async_computation.1 | async-start | bytes 1048576 | tf_op jit(solution)/shard_map/serve/all_to_all | solution.py:271
  44.1 28.9 %collective-permute-start = (bf16[128,512]{1,0:T(8,128)(2,1)S(1)}, bf16[128,512]{1,0:T(8,128)(2,1)S(1)}, u32[]{:S(2)}, u32[]{:S(2)}) collective-permute-start(bf16[128,512]{1,0:T(8,128)(2,1)S(1)} %slice.82.own_ref.kv_ref), channel_id=1, source_target_pairs={{0,4},{4,8},{8,12},{12,16},{16,20},{20,24},{24,28},{28,32},{32,36}... | collective-permute-start | bytes 393224 | tf_op jit(solution)/shard_map/project/ppermute | solution.py:276
  46.0 26.9 %collective-permute-start.1 = (bf16[128,512]{1,0:T(8,128)(2,1)S(1)}, bf16[128,512]{1,0:T(8,128)(2,1)S(1)}, u32[]{:S(2)}, u32[]{:S(2)}) collective-permute-start(bf16[128,512]{1,0:T(8,128)(2,1)S(1)} %slice.82.own_ref.kv_ref), channel_id=1, source_target_pairs={{0,508},{4,0},{8,4},{12,8},{16,12},{20,16},{24,20},{28,24},{32,28}... | collective-permute-start | bytes 393224 | tf_op jit(solution)/shard_map/project/ppermute | solution.py:276
  54.0 3.5 %copy-start.9 = (f32[3,2]{0,1:T(2,128)S(1)}, f32[3,2]{0,1:T(2,128)}, u32[]{:S(2)}) copy-start(f32[3,2]{0,1:T(2,128)} %param.12) | copy-start | bytes 76
  54.0 3.6 %copy-start.8 = (s32[128,4]{0,1:T(4,128)S(1)}, s32[128,4]{0,1:T(4,128)}, u32[]{:S(2)}) copy-start(s32[128,4]{0,1:T(4,128)} %param.15) | copy-start | bytes 6148
  54.0 18.9 %copy-start = (bf16[128,256]{1,0:T(8,128)(2,1)S(1)}, bf16[128,256]{1,0:T(8,128)(2,1)}, u32[]{:S(2)}) copy-start(bf16[128,256]{1,0:T(8,128)(2,1)} %grad_ref.3) | copy-start | bytes 196612
  54.1 22.2 %copy-start.2 = (s32[4,128]{1,0:T(4,128)S(1)}, s32[4,128]{1,0:T(4,128)}, u32[]{:S(2)}) copy-start(s32[4,128]{1,0:T(4,128)} %neighbours_ref.3) | copy-start | bytes 6148
  54.1 3.6 %collective-permute-start.2 = (bf16[512,128]{1,0:T(8,128)(2,1)S(1)}, bf16[512,128]{1,0:T(8,128)(2,1)S(1)}, u32[]{:S(2)}, u32[]{:S(2)}) collective-permute-start(bf16[512,128]{1,0:T(8,128)(2,1)S(1)} %slice.59), channel_id=1, source_target_pairs={{0,4},{4,0},{1,5},{5,1},{2,6},{6,2},{3,7},{7,3},{8,12},{12,8},{9,1... | collective-permute-start | bytes 393224 | tf_op jit(solution)/shard_map/select/ppermute | solution.py:280
  78.5 42.0 %all-to-all-start.2 = ((bf16[128,8,256]{2,1,0:T(8,128)(2,1)}), bf16[128,8,256]{2,1,0:T(8,128)(2,1)S(1)}, u32[]{:S(2)}, u32[]{:S(2)}) async-start(bf16[128,8,256]{2,1,0:T(8,128)(2,1)} %bitcast.5), calls=%async_computation.2 | async-start | bytes 1048576 | tf_op jit(solution)/shard_map/near/all_to_all | solution.py:271
  93.1 19.4 %collective-permute-start.6 = (f32[4,1024]{1,0:T(4,128)S(1)}, f32[4,1024]{1,0:T(4,128)S(1)}, u32[]{:S(2)}, u32[]{:S(2)}) collective-permute-start(f32[4,1024]{1,0:T(4,128)S(1)} %slice_add_fusion), channel_id=1, source_target_pairs={{0,2},{1,3},{2,0},{3,1},{4,6},{5,7},{6,4},{7,5},{8,10},{9,11},{10,... | collective-permute-start | bytes 49160 | tf_op jit(solution)/shard_map/virtual/ppermute | solution.py:280
  95.4 17.1 %collective-permute-start.7 = (f32[4,1024]{1,0:T(4,128)S(1)}, f32[4,1024]{1,0:T(4,128)S(1)}, u32[]{:S(2)}, u32[]{:S(2)}) collective-permute-start(f32[4,1024]{1,0:T(4,128)S(1)} %slice_add_fusion), channel_id=1, source_target_pairs={{0,3},{1,2},{2,1},{3,0},{4,7},{5,6},{6,5},{7,4},{8,11},{9,10},{10,... | collective-permute-start | bytes 49160 | tf_op jit(solution)/shard_map/virtual/ppermute | solution.py:280
  99.7 12.8 %collective-permute-start.5 = (f32[4,1024]{1,0:T(4,128)S(1)}, f32[4,1024]{1,0:T(4,128)S(1)}, u32[]{:S(2)}, u32[]{:S(2)}) collective-permute-start(f32[4,1024]{1,0:T(4,128)S(1)} %slice_add_fusion), channel_id=1, source_target_pairs={{0,1},{1,0},{2,3},{3,2},{4,5},{5,4},{6,7},{7,6},{8,9},{9,8},{10,11... | collective-permute-start | bytes 49160 | tf_op jit(solution)/shard_map/virtual/ppermute | solution.py:280
  103.6 13.5 %collective-permute-start.3 = (bf16[128,512]{1,0:T(8,128)(2,1)S(1)}, bf16[128,512]{1,0:T(8,128)(2,1)S(1)}, u32[]{:S(2)}, u32[]{:S(2)}) collective-permute-start(bf16[128,512]{1,0:T(8,128)(2,1)S(1)} %get-tuple-element.30), channel_id=1, source_target_pairs={{0,4},{4,8},{8,12},{12,16},{16,20},{20,24},{24,28},{28,32},{32,36}... | collective-permute-start | bytes 393224 | tf_op jit(solution)/shard_map/back/ppermute | solution.py:276
  105.5 11.5 %collective-permute-start.4 = (bf16[128,512]{1,0:T(8,128)(2,1)S(1)}, bf16[128,512]{1,0:T(8,128)(2,1)S(1)}, u32[]{:S(2)}, u32[]{:S(2)}) collective-permute-start(bf16[128,512]{1,0:T(8,128)(2,1)S(1)} %get-tuple-element.31), channel_id=1, source_target_pairs={{0,508},{4,0},{8,4},{12,8},{16,12},{20,16},{24,20},{28,24},{32,28}... | collective-permute-start | bytes 393224 | tf_op jit(solution)/shard_map/back/ppermute | solution.py:276
  120.9 3.4 %collective-permute-start.11 = (bf16[160,768]{1,0:T(8,128)(2,1)S(1)}, bf16[160,768]{1,0:T(8,128)(2,1)S(1)}, u32[]{:S(2)}, u32[]{:S(2)}) collective-permute-start(bf16[160,768]{1,0:T(8,128)(2,1)S(1)} %total.1.own_ref), channel_id=1, source_target_pairs={{0,4},{4,0},{1,5},{5,1},{2,6},{6,2},{3,7},{7,3},{8,12},{12,8},{9,1... | collective-permute-start | bytes 737288 | tf_op jit(solution)/shard_map/total/ppermute | solution.py:280
  142.1 7.2 %copy-start.4 = (bf16[1024,3,256]{0,2,1:T(8,128)(2,1)S(1)}, bf16[1024,3,256]{0,2,1:T(8,128)(2,1)}, u32[]{:S(2)}) copy-start(bf16[1024,3,256]{0,2,1:T(8,128)(2,1)} %copy-done.3) | copy-start | bytes 4718596
  143.0 26.5 %all-to-all-start.4 = ((bf16[16,8,1280]{2,1,0:T(8,128)(2,1)}), bf16[16,8,1280]{2,1,0:T(8,128)(2,1)S(1)}, u32[]{:S(2)}, u32[]{:S(2)}) async-start(bf16[16,8,1280]{2,1,0:T(8,128)(2,1)} %pad_maximum_fusion), calls=%async_computation.4 | async-start | bytes 655360 | tf_op jit(solution)/shard_map/weight/all_to_all | solution.py:271
  149.7 8.3 %collective-permute-start.10 = (bf16[128,256]{1,0:T(8,128)(2,1)S(1)}, bf16[128,256]{1,0:T(8,128)(2,1)S(1)}, u32[]{:S(2)}, u32[]{:S(2)}) collective-permute-start(bf16[128,256]{1,0:T(8,128)(2,1)S(1)} %get-tuple-element.38), channel_id=1, source_target_pairs={{0,3},{1,0},{2,1},{3,2},{4,7},{5,4},{6,5},{7,6},{8,11},{9,8},{10,9... | collective-permute-start | bytes 196616 | tf_op jit(solution)/shard_map/feature/ppermute | solution.py:276
  152.0 8.2 %collective-permute-start.9 = (bf16[128,256]{1,0:T(8,128)(2,1)S(1)}, bf16[128,256]{1,0:T(8,128)(2,1)S(1)}, u32[]{:S(2)}, u32[]{:S(2)}) collective-permute-start(bf16[128,256]{1,0:T(8,128)(2,1)S(1)} %get-tuple-element.39), channel_id=1, source_target_pairs={{0,2},{1,3},{2,0},{3,1},{4,6},{5,7},{6,4},{7,5},{8,10},{9,11},{10,... | collective-permute-start | bytes 196616 | tf_op jit(solution)/shard_map/feature/ppermute | solution.py:276
  155.6 6.2 %collective-permute-start.8 = (bf16[128,256]{1,0:T(8,128)(2,1)S(1)}, bf16[128,256]{1,0:T(8,128)(2,1)S(1)}, u32[]{:S(2)}, u32[]{:S(2)}) collective-permute-start(bf16[128,256]{1,0:T(8,128)(2,1)S(1)} %get-tuple-element.37), channel_id=1, source_target_pairs={{0,1},{1,2},{2,3},{3,0},{4,5},{5,6},{6,7},{7,4},{8,9},{9,10},{10,1... | collective-permute-start | bytes 196616 | tf_op jit(solution)/shard_map/feature/ppermute | solution.py:276

commit v5 on v3

--- a/solution.py
+++ b/solution.py
@@ -97,9 +97,11 @@
 
 def serve_kernel(asked_ref, kv_ref, out_ref, work_ref):
     row = lax.broadcasted_iota(jnp.int32, (SHARDS, ROWS), 1)
-    asked, kv = asked_ref[:, 0, :], kv_ref[...]
+    asked = asked_ref[:, 0, :]
+    hits = jnp.concatenate([ones_where(row == asked[:, perm : perm + 1]) for perm in range(DEGREE)], axis=0)
+    picked = mul(hits, kv_ref[...], NN)
     for perm in range(DEGREE):
-        put_slots(work_ref, perm, mul(ones_where(row == asked[:, perm : perm + 1]), kv, NN))
+        put_slots(work_ref, perm, picked[perm * SHARDS : (perm + 1) * SHARDS])
     close_slots(work_ref, out_ref)
 
 
@@ -218,9 +220,9 @@
     place = lax.broadcasted_iota(jnp.int32, (ROWS, SHARDS), 0)
     open_slots(work_ref, back_ref)
     rim = from_left_ref[...].astype(F32) + from_right_ref[...].astype(F32)
-    total = down_ref[...] + rim
-    for perm in range(DEGREE):
-        total += mul(ones_where(place == asked_ref[perm : perm + 1, :]), take_slots(work_ref, perm), NN)
+    hits = jnp.concatenate([ones_where(place == asked_ref[perm : perm + 1, :]) for perm in range(DEGREE)], axis=1)
+    rows = jnp.concatenate([take_slots(work_ref, perm) for perm in range(DEGREE)], axis=0)
+    total = down_ref[...] + rim + mul(hits, rows, NN)
     out_ref[:ROWS, :COLS] = dquery_ref[...]
     out_ref[:ROWS, COLS:] = total.astype(BF16)
     out_ref[ROWS:, :] = tail_ref[...]
@@ -280,6 +282,11 @@
 
 def swap(values, axis, bit):
     return lax.ppermute(values, axis, [(i, i ^ bit) for i in range(SIZES[axis])])
+
+
+def sum_of_four(values, axis):
+    near, far, both = (swap(values, axis, bit) for bit in (1, 2, 3))
+    return (values + near) + (far + both)
 
 
 def two_terms(values):
@@ -310,6 +317,7 @@
         sorted_in = mul(chosen, rows_in, NT).astype(BF16)
         in_own = sorted_in[:512]
         in_other = jnp.concatenate([swap(sorted_in[512:, :ROWS], "c", 1), in_own[:, ROWS:]], axis=1)
+        from_left, from_right, in_own, in_other = lax.optimization_barrier((from_left, from_right, in_own, in_other))
     with jax.named_scope("serve"):
         served, = call(serve_kernel, [((SHARDS * SLOTS, COLS), BF16)], asked, kv, scratch=WORK)
         near = exchange(served.reshape(SHARDS, SLOTS, COLS), NODES).reshape(SHARDS * SLOTS, COLS)
@@ -336,8 +344,7 @@
         split = jnp.concatenate(two_terms(dvirtual), axis=0)
         vnode = mul(split, flat_weight[:, COLS:], NT)
         vnode = vnode[:VIRTUAL] + vnode[VIRTUAL:]
-        for bit in (1, 2):
-            vnode = vnode + swap(vnode, "mp", bit)
+        vnode = sum_of_four(vnode, "mp")
         vnode = jnp.concatenate(two_terms(jnp.concatenate([vnode[:, :512], vnode[:, 512:]], axis=0)), axis=0)
         tail = jnp.concatenate([jnp.pad(split, ((0, 8), (COLS, 0))), jnp.pad(vnode, ((0, 0), (0, COLS)))], axis=0)
     with jax.named_scope("total"):

time: 173 us -> 172 us (level)
  the two profiles are of different devices: /device:TPU:32 before, /device:TPU:16 now
where the time goes in v5:
time: 172 us; the launch traced here: 171 us
  starting transfers between devices  82.4 us (48%)
  waiting for transfers between devices  48.5 us (28%)
  blocking collectives  17.7 us (10%)
  Pallas kernels  10.7 us (6%)
  local copies, waits for them, and re-layouts  4.62 us (3%)
  matrix products  3.81 us (2%)
    all_to_all x4, starting transfers between devices, exchange(): return lax.all_to_all(values, axis, split_axis=0, concat_axis=0, tiled=True)  42 us
    ppermute x7, starting transfers between devices, shift(): lax.ppermute(values, axis, [(i, (i + step) % count) for i in range(count)])  26 us
    all_to_all x4, waiting for transfers between devices, exchange(): return lax.all_to_all(values, axis, split_axis=0, concat_axis=0, tiled=True)  23.5 us
    ppermute x7, waiting for transfers between devices, shift(): lax.ppermute(values, axis, [(i, (i + step) % count) for i in range(count)])  23.4 us
    all_to_all x1, blocking collectives, exchange(): return lax.all_to_all(values, axis, split_axis=0, concat_axis=0, tiled=True)  17.7 us
    ppermute x5, starting transfers between devices, swap(): lax.ppermute(values, axis, [(i, i ^ bit) for i in range(SIZES[axis])])  14.4 us
    pallas_call x8, Pallas kernels, call(): pl.pallas_call(kernel, out_shape=shapes, in_specs=[SMEM] * scalars + [VME...  10.7 us
  transfers between devices with their start and end apart: 16, of which 9 were waited for; matrix products, arithmetic and copies ran while one was open for 5% of the time, Pallas kernels for 3%

profile of v5, /device:TPU:16, one launch (start us, length us, event | category | flops | bytes accessed | tf_op | source)
XLA Modules:
  0.0 170.6 jit_solution(4757369135603357348)
XLA Ops:
  2.1 19.8 %all-to-all-start = ((s32[128,1,4]{2,1,0:T(1,128)}), s32[128,1,4]{2,1,0:T(1,128)S(1)}, u32[]{:S(2)}, u32[]{:S(2)}) async-start(s32[128,1,4]{2,1,0:T(1,128)} %ask.1), calls=%async_computation | async-start | bytes 131072 | tf_op jit(solution)/shard_map/ask/all_to_all | solution.py:275
  21.9 1.8 %copy.28 = bf16[1024,3,256]{0,2,1:T(8,128)(2,1)S(1)} copy(bf16[1024,3,256]{2,0,1:T(8,128)(2,1)} %param.10) | data formatting | bytes 3145728 | tf_op args[1]
  25.1 11.2 %all-to-all-done.asked_ref = s32[128,1,4]{2,1,0:T(1,128)S(1)} async-done(((s32[128,1,4]{2,1,0:T(1,128)}), s32[128,1,4]{2,1,0:T(1,128)S(1)}, u32[]{:S(2)}, u32[]{:S(2)}) %all-to-all-start) | async-done | bytes 2080 | tf_op jit(solution)/shard_map/ask/all_to_all | solution.py:275
  36.3 1.5 serve.1
  37.9 6.2 %all-to-all-start.1 = ((bf16[128,8,256]{2,1,0:T(8,128)(2,1)}), bf16[128,8,256]{2,1,0:T(8,128)(2,1)S(1)}, u32[]{:S(2)}, u32[]{:S(2)}) async-start(bf16[128,8,256]{2,1,0:T(8,128)(2,1)} %bitcast.3), calls=%async_computation.1 | async-start | bytes 1048576 | tf_op jit(solution)/shard_map/serve/all_to_all | solution.py:275
  44.1 1.9 %collective-permute-start = (bf16[128,512]{1,0:T(8,128)(2,1)S(1)}, bf16[128,512]{1,0:T(8,128)(2,1)S(1)}, u32[]{:S(2)}, u32[]{:S(2)}) collective-permute-start(bf16[128,512]{1,0:T(8,128)(2,1)S(1)} %slice.90.own_ref.kv_ref), channel_id=1, source_target_pairs={{0,4},{4,8},{8,12},{12,16},{16,20},{20,24},{24,28},{28,32},{32,36}... | collective-permute-start | bytes 393224 | tf_op jit(solution)/shard_map/project/ppermute | solution.py:280
  46.0 7.0 %collective-permute-start.1 = (bf16[128,512]{1,0:T(8,128)(2,1)S(1)}, bf16[128,512]{1,0:T(8,128)(2,1)S(1)}, u32[]{:S(2)}, u32[]{:S(2)}) collective-permute-start(bf16[128,512]{1,0:T(8,128)(2,1)S(1)} %slice.90.own_ref.kv_ref), channel_id=1, source_target_pairs={{0,508},{4,0},{8,4},{12,8},{16,12},{20,16},{24,20},{28,24},{32,28}... | collective-permute-start | bytes 393224 | tf_op jit(solution)/shard_map/project/ppermute | solution.py:280
  54.1 2.1 %collective-permute-start.2 = (bf16[512,128]{1,0:T(8,128)(2,1)S(1)}, bf16[512,128]{1,0:T(8,128)(2,1)S(1)}, u32[]{:S(2)}, u32[]{:S(2)}) collective-permute-start(bf16[512,128]{1,0:T(8,128)(2,1)S(1)} %slice.63), channel_id=1, source_target_pairs={{0,4},{4,0},{1,5},{5,1},{2,6},{6,2},{3,7},{7,3},{8,12},{12,8},{9,1... | collective-permute-start | bytes 393224 | tf_op jit(solution)/shard_map/select/ppermute | solution.py:284
  57.8 15.1 %collective-permute-done.left_ref = bf16[128,512]{1,0:T(8,128)(2,1)S(1)} collective-permute-done((bf16[128,512]{1,0:T(8,128)(2,1)S(1)}, bf16[128,512]{1,0:T(8,128)(2,1)S(1)}, u32[]{:S(2)}, u32[]{:S(2)}) %collective-permute-start) | collective-permute-done | bytes 131104 | tf_op jit(solution)/shard_map/project/ppermute | solution.py:280
  72.9 1.4 local.1
  74.3 2.0 %all-to-all-done.1 = bf16[128,8,256]{2,1,0:T(8,128)(2,1)S(1)} async-done(((bf16[128,8,256]{2,1,0:T(8,128)(2,1)}), bf16[128,8,256]{2,1,0:T(8,128)(2,1)S(1)}, u32[]{:S(2)}, u32[]{:S(2)}) %all-to-all-start.1) | async-done | bytes 524320 | tf_op jit(solution)/shard_map/serve/all_to_all | solution.py:275
  76.3 2.2 %near.1 = (bf16[1024,256]{1,0:T(8,128)(2,1)}, f32[4,128]{1,0:T(4,128)S(1)}, f32[256,128]{1,0:T(8,128)S(1)}) custom-call(f32[3,2]{1,0:T(4,128)S(1)} %copy.32.bias_ref, s32[4,128]{1,0:T(4,128)S(1)} %copy-done.2, f32[256,128]{1,0:T(8,128)S(1)} %get-tuple-element.22.query_ref, bf16[1024,256]{1,0:T(8,128)(2,1)S(1)} %bitcast.16, ...), custom_call_target="tpu_custom_call" | custom-call | flops 100000000 | bytes 1447960 | tf_op jit(solution)/shard_map/near/pallas_call | solution.py:263
  78.5 9.9 %all-to-all-start.2 = ((bf16[128,8,256]{2,1,0:T(8,128)(2,1)}), bf16[128,8,256]{2,1,0:T(8,128)(2,1)S(1)}, u32[]{:S(2)}, u32[]{:S(2)}) async-start(bf16[128,8,256]{2,1,0:T(8,128)(2,1)} %bitcast.5), calls=%async_computation.2 | async-start | bytes 1048576 | tf_op jit(solution)/shard_map/near/all_to_all | solution.py:275
  88.4 3.2 %back.1 = (bf16[128,256]{1,0:T(8,128)(2,1)S(1)}, bf16[128,512]{1,0:T(8,128)(2,1)S(1)}, f32[128,512]{1,0:T(8,128)S(1)}, bf16[128,512]{1,0:T(8,128)(2,1)S(1)}, f32[4,512]{1,0:T(4,128)S(1)}) custom-call(f32[3,2]{1,0:T(4,128)S(1)} %copy.32.bias_ref, f32[128,256]{1,0:T(8,128)S(1)} %slice.60.query_ref, bf16[128,512]{1,0:T(8,128)(2,1)S(1)} %collective-permute-done.left_ref, ...), custom_call_target="tpu_custom_call" | custom-call | flops 100000000 | bytes 1331224 | tf_op jit(solution)/shard_map/back/pallas_call | solution.py:263
  91.6 1.5 fusion.3
  93.1 2.2 %collective-permute-start.6 = (f32[4,1024]{1,0:T(4,128)S(1)}, f32[4,1024]{1,0:T(4,128)S(1)}, u32[]{:S(2)}, u32[]{:S(2)}) collective-permute-start(f32[4,1024]{1,0:T(4,128)S(1)} %slice_add_fusion.1), channel_id=1, source_target_pairs={{0,2},{1,3},{2,0},{3,1},{4,6},{5,7},{6,4},{7,5},{8,10},{9,11},{10,... | collective-permute-start | bytes 49160 | tf_op jit(solution)/shard_map/virtual/ppermute | solution.py:284
  95.4 4.3 %collective-permute-start.7 = (f32[4,1024]{1,0:T(4,128)S(1)}, f32[4,1024]{1,0:T(4,128)S(1)}, u32[]{:S(2)}, u32[]{:S(2)}) collective-permute-start(f32[4,1024]{1,0:T(4,128)S(1)} %slice_add_fusion.1), channel_id=1, source_target_pairs={{0,3},{1,2},{2,1},{3,0},{4,7},{5,6},{6,5},{7,4},{8,11},{9,10},{10,... | collective-permute-start | bytes 49160 | tf_op jit(solution)/shard_map/virtual/ppermute | solution.py:284
  99.7 3.9 %collective-permute-start.5 = (f32[4,1024]{1,0:T(4,128)S(1)}, f32[4,1024]{1,0:T(4,128)S(1)}, u32[]{:S(2)}, u32[]{:S(2)}) collective-permute-start(f32[4,1024]{1,0:T(4,128)S(1)} %slice_add_fusion.1), channel_id=1, source_target_pairs={{0,1},{1,0},{2,3},{3,2},{4,5},{5,4},{6,7},{7,6},{8,9},{9,8},{10,11... | collective-permute-start | bytes 49160 | tf_op jit(solution)/shard_map/virtual/ppermute | solution.py:284
  103.6 1.9 %collective-permute-start.3 = (bf16[128,512]{1,0:T(8,128)(2,1)S(1)}, bf16[128,512]{1,0:T(8,128)(2,1)S(1)}, u32[]{:S(2)}, u32[]{:S(2)}) collective-permute-start(bf16[128,512]{1,0:T(8,128)(2,1)S(1)} %get-tuple-element.30), channel_id=1, source_target_pairs={{0,4},{4,8},{8,12},{12,16},{16,20},{20,24},{24,28},{28,32},{32,36}... | collective-permute-start | bytes 393224 | tf_op jit(solution)/shard_map/back/ppermute | solution.py:280
  105.5 7.0 %collective-permute-start.4 = (bf16[128,512]{1,0:T(8,128)(2,1)S(1)}, bf16[128,512]{1,0:T(8,128)(2,1)S(1)}, u32[]{:S(2)}, u32[]{:S(2)}) collective-permute-start(bf16[128,512]{1,0:T(8,128)(2,1)S(1)} %get-tuple-element.31), channel_id=1, source_target_pairs={{0,508},{4,0},{8,4},{12,8},{16,12},{20,16},{24,20},{28,24},{32,28}... | collective-permute-start | bytes 393224 | tf_op jit(solution)/shard_map/back/ppermute | solution.py:280
  112.6 4.5 %collective-permute-done.3.from_left_ref = bf16[128,512]{1,0:T(8,128)(2,1)S(1)} collective-permute-done((bf16[128,512]{1,0:T(8,128)(2,1)S(1)}, bf16[128,512]{1,0:T(8,128)(2,1)S(1)}, u32[]{:S(2)}, u32[]{:S(2)}) %collective-permute-start.3) | collective-permute-done | bytes 131104 | tf_op jit(solution)/shard_map/back/ppermute | solution.py:280
  117.0 3.5 %all-to-all-done.2 = bf16[128,8,256]{2,1,0:T(8,128)(2,1)S(1)} async-done(((bf16[128,8,256]{2,1,0:T(8,128)(2,1)}), bf16[128,8,256]{2,1,0:T(8,128)(2,1)S(1)}, u32[]{:S(2)}, u32[]{:S(2)}) %all-to-all-start.2) | async-done | bytes 524320 | tf_op jit(solution)/shard_map/near/all_to_all | solution.py:275
  120.9 1.9 %collective-permute-start.11 = (bf16[160,768]{1,0:T(8,128)(2,1)S(1)}, bf16[160,768]{1,0:T(8,128)(2,1)S(1)}, u32[]{:S(2)}, u32[]{:S(2)}) collective-permute-start(bf16[160,768]{1,0:T(8,128)(2,1)S(1)} %total.1.own_ref), channel_id=1, source_target_pairs={{0,4},{4,0},{1,5},{5,1},{2,6},{6,2},{3,7},{7,3},{8,12},{12,8},{9,1... | collective-permute-start | bytes 737288 | tf_op jit(solution)/shard_map/total/ppermute | solution.py:284
  122.8 1.5 collective-permute-done.11.other_ref
  124.9 17.7 %all_to_all.25 = bf16[4,144,768]{2,1,0:T(8,128)(2,1)S(1)} all-to-all(bf16[4,144,768]{2,1,0:T(8,128)(2,1)S(1)} %weight.2), channel_id=1, replica_groups=mesh['z'=16,'x'=4,'c'=2,'mp'=4] {'x'}, dimensions={0} | all-to-all | bytes 1769472 | tf_op jit(solution)/shard_map/weight/all_to_all | solution.py:275
  143.5 6.2 %all-to-all-start.4 = ((bf16[16,8,1280]{2,1,0:T(8,128)(2,1)}), bf16[16,8,1280]{2,1,0:T(8,128)(2,1)S(1)}, u32[]{:S(2)}, u32[]{:S(2)}) async-start(bf16[16,8,1280]{2,1,0:T(8,128)(2,1)} %pad_maximum_fusion), calls=%async_computation.4 | async-start | bytes 655360 | tf_op jit(solution)/shard_map/weight/all_to_all | solution.py:275
  150.2 2.4 %collective-permute-start.10 = (bf16[128,256]{1,0:T(8,128)(2,1)S(1)}, bf16[128,256]{1,0:T(8,128)(2,1)S(1)}, u32[]{:S(2)}, u32[]{:S(2)}) collective-permute-start(bf16[128,256]{1,0:T(8,128)(2,1)S(1)} %get-tuple-element.38), channel_id=1, source_target_pairs={{0,3},{1,0},{2,1},{3,2},{4,7},{5,4},{6,5},{7,6},{8,11},{9,8},{10,9... | collective-permute-start | bytes 196616 | tf_op jit(solution)/shard_map/feature/ppermute | solution.py:280
  152.6 3.6 %collective-permute-start.9 = (bf16[128,256]{1,0:T(8,128)(2,1)S(1)}, bf16[128,256]{1,0:T(8,128)(2,1)S(1)}, u32[]{:S(2)}, u32[]{:S(2)}) collective-permute-start(bf16[128,256]{1,0:T(8,128)(2,1)S(1)} %get-tuple-element.39), channel_id=1, source_target_pairs={{0,2},{1,3},{2,0},{3,1},{4,6},{5,7},{6,4},{7,5},{8,10},{9,11},{10,... | collective-permute-start | bytes 196616 | tf_op jit(solution)/shard_map/feature/ppermute | solution.py:280
  156.2 2.3 %collective-permute-start.8 = (bf16[128,256]{1,0:T(8,128)(2,1)S(1)}, bf16[128,256]{1,0:T(8,128)(2,1)S(1)}, u32[]{:S(2)}, u32[]{:S(2)}) collective-permute-start(bf16[128,256]{1,0:T(8,128)(2,1)S(1)} %get-tuple-element.37), channel_id=1, source_target_pairs={{0,1},{1,2},{2,3},{3,0},{4,5},{5,6},{6,7},{7,4},{8,9},{9,10},{10,1... | collective-permute-start | bytes 196616 | tf_op jit(solution)/shard_map/feature/ppermute | solution.py:280
  158.5 2.4 %collective-permute-done.9 = bf16[128,256]{1,0:T(8,128)(2,1)S(1)} collective-permute-done((bf16[128,256]{1,0:T(8,128)(2,1)S(1)}, bf16[128,256]{1,0:T(8,128)(2,1)S(1)}, u32[]{:S(2)}, u32[]{:S(2)}) %collective-permute-start.9) | collective-permute-done | bytes 65568 | tf_op jit(solution)/shard_map/feature/ppermute | solution.py:280
  160.9 1.4 collective-permute-done.8
  163.0 6.9 %all-to-all-done.4.parts_ref = bf16[16,8,1280]{2,1,0:T(8,128)(2,1)S(1)} async-done(((bf16[16,8,1280]{2,1,0:T(8,128)(2,1)}), bf16[16,8,1280]{2,1,0:T(8,128)(2,1)S(1)}, u32[]{:S(2)}, u32[]{:S(2)}) %all-to-all-start.4) | async-done | bytes 327712 | tf_op jit(solution)/shard_map/weight/all_to_all | solution.py:275
  (63 shorter events, 9.3 us)
Async XLA Ops:
  0.6 0.7 copy-start.1
  2.1 34.2 %all-to-all-start = ((s32[128,1,4]{2,1,0:T(1,128)}), s32[128,1,4]{2,1,0:T(1,128)S(1)}, u32[]{:S(2)}, u32[]{:S(2)}) async-start(s32[128,1,4]{2,1,0:T(1,128)} %ask.1), calls=%async_computation | async-start | bytes 131072 | tf_op jit(solution)/shard_map/ask/all_to_all | solution.py:275
  21.9 1.8 %copy-start.6 = (bf16[128,1024]{1,0:T(8,128)(2,1)S(1)}, bf16[128,1024]{1,0:T(8,128)(2,1)}, u32[]{:S(2)}) copy-start(bf16[128,1024]{1,0:T(8,128)(2,1)} %param.9) | copy-start | bytes 786436
  23.7 32.5 %copy-start.3 = (bf16[1024,3,256]{0,2,1:T(8,128)(2,1)}, bf16[1024,3,256]{0,2,1:T(8,128)(2,1)S(1)}, u32[]{:S(2)}) copy-start(bf16[1024,3,256]{0,2,1:T(8,128)(2,1)S(1)} %copy.28) | copy-start | bytes 4718596
  24.4 0.8 copy-start.5
  25.1 28.0 %copy-start.7 = (bf16[4,1024]{1,0:T(4,128)(2,1)S(1)}, bf16[4,1024]{1,0:T(4,128)(2,1)}, u32[]{:S(2)}) copy-start(bf16[4,1024]{1,0:T(4,128)(2,1)} %param.11) | copy-start | bytes 24580
  37.9 38.4 %all-to-all-start.1 = ((bf16[128,8,256]{2,1,0:T(8,128)(2,1)}), bf16[128,8,256]{2,1,0:T(8,128)(2,1)S(1)}, u32[]{:S(2)}, u32[]{:S(2)}) async-start(bf16[128,8,256]{2,1,0:T(8,128)(2,1)} %bitcast.3), calls=%async_computation.1 | async-start | bytes 1048576 | tf_op jit(solution)/shard_map/serve/all_to_all | solution.py:275
  44.1 28.9 %collective-permute-start = (bf16[128,512]{1,0:T(8,128)(2,1)S(1)}, bf16[128,512]{1,0:T(8,128)(2,1)S(1)}, u32[]{:S(2)}, u32[]{:S(2)}) collective-permute-start(bf16[128,512]{1,0:T(8,128)(2,1)S(1)} %slice.90.own_ref.kv_ref), channel_id=1, source_target_pairs={{0,4},{4,8},{8,12},{12,16},{16,20},{20,24},{24,28},{28,32},{32,36}... | collective-permute-start | bytes 393224 | tf_op jit(solution)/shard_map/project/ppermute | solution.py:280
  46.0 26.9 %collective-permute-start.1 = (bf16[128,512]{1,0:T(8,128)(2,1)S(1)}, bf16[128,512]{1,0:T(8,128)(2,1)S(1)}, u32[]{:S(2)}, u32[]{:S(2)}) collective-permute-start(bf16[128,512]{1,0:T(8,128)(2,1)S(1)} %slice.90.own_ref.kv_ref), channel_id=1, source_target_pairs={{0,508},{4,0},{8,4},{12,8},{16,12},{20,16},{24,20},{28,24},{32,28}... | collective-permute-start | bytes 393224 | tf_op jit(solution)/shard_map/project/ppermute | solution.py:280
  54.0 3.5 %copy-start.9 = (f32[3,2]{0,1:T(2,128)S(1)}, f32[3,2]{0,1:T(2,128)}, u32[]{:S(2)}) copy-start(f32[3,2]{0,1:T(2,128)} %param.12) | copy-start | bytes 76
  54.0 3.6 %copy-start.8 = (s32[128,4]{0,1:T(4,128)S(1)}, s32[128,4]{0,1:T(4,128)}, u32[]{:S(2)}) copy-start(s32[128,4]{0,1:T(4,128)} %param.15) | copy-start | bytes 6148
  54.0 18.9 %copy-start = (bf16[128,256]{1,0:T(8,128)(2,1)S(1)}, bf16[128,256]{1,0:T(8,128)(2,1)}, u32[]{:S(2)}) copy-start(bf16[128,256]{1,0:T(8,128)(2,1)} %grad_ref.3) | copy-start | bytes 196612
  54.1 22.2 %copy-start.2 = (s32[4,128]{1,0:T(4,128)S(1)}, s32[4,128]{1,0:T(4,128)}, u32[]{:S(2)}) copy-start(s32[4,128]{1,0:T(4,128)} %neighbours_ref.3) | copy-start | bytes 6148
  54.1 3.6 %collective-permute-start.2 = (bf16[512,128]{1,0:T(8,128)(2,1)S(1)}, bf16[512,128]{1,0:T(8,128)(2,1)S(1)}, u32[]{:S(2)}, u32[]{:S(2)}) collective-permute-start(bf16[512,128]{1,0:T(8,128)(2,1)S(1)} %slice.63), channel_id=1, source_target_pairs={{0,4},{4,0},{1,5},{5,1},{2,6},{6,2},{3,7},{7,3},{8,12},{12,8},{9,1... | collective-permute-start | bytes 393224 | tf_op jit(solution)/shard_map/select/ppermute | solution.py:284
  78.5 42.0 %all-to-all-start.2 = ((bf16[128,8,256]{2,1,0:T(8,128)(2,1)}), bf16[128,8,256]{2,1,0:T(8,128)(2,1)S(1)}, u32[]{:S(2)}, u32[]{:S(2)}) async-start(bf16[128,8,256]{2,1,0:T(8,128)(2,1)} %bitcast.5), calls=%async_computation.2 | async-start | bytes 1048576 | tf_op jit(solution)/shard_map/near/all_to_all | solution.py:275
  93.1 19.4 %collective-permute-start.6 = (f32[4,1024]{1,0:T(4,128)S(1)}, f32[4,1024]{1,0:T(4,128)S(1)}, u32[]{:S(2)}, u32[]{:S(2)}) collective-permute-start(f32[4,1024]{1,0:T(4,128)S(1)} %slice_add_fusion.1), channel_id=1, source_target_pairs={{0,2},{1,3},{2,0},{3,1},{4,6},{5,7},{6,4},{7,5},{8,10},{9,11},{10,... | collective-permute-start | bytes 49160 | tf_op jit(solution)/shard_map/virtual/ppermute | solution.py:284
  95.4 17.1 %collective-permute-start.7 = (f32[4,1024]{1,0:T(4,128)S(1)}, f32[4,1024]{1,0:T(4,128)S(1)}, u32[]{:S(2)}, u32[]{:S(2)}) collective-permute-start(f32[4,1024]{1,0:T(4,128)S(1)} %slice_add_fusion.1), channel_id=1, source_target_pairs={{0,3},{1,2},{2,1},{3,0},{4,7},{5,6},{6,5},{7,4},{8,11},{9,10},{10,... | collective-permute-start | bytes 49160 | tf_op jit(solution)/shard_map/virtual/ppermute | solution.py:284
  99.7 12.8 %collective-permute-start.5 = (f32[4,1024]{1,0:T(4,128)S(1)}, f32[4,1024]{1,0:T(4,128)S(1)}, u32[]{:S(2)}, u32[]{:S(2)}) collective-permute-start(f32[4,1024]{1,0:T(4,128)S(1)} %slice_add_fusion.1), channel_id=1, source_target_pairs={{0,1},{1,0},{2,3},{3,2},{4,5},{5,4},{6,7},{7,6},{8,9},{9,8},{10,11... | collective-permute-start | bytes 49160 | tf_op jit(solution)/shard_map/virtual/ppermute | solution.py:284
  103.6 13.5 %collective-permute-start.3 = (bf16[128,512]{1,0:T(8,128)(2,1)S(1)}, bf16[128,512]{1,0:T(8,128)(2,1)S(1)}, u32[]{:S(2)}, u32[]{:S(2)}) collective-permute-start(bf16[128,512]{1,0:T(8,128)(2,1)S(1)} %get-tuple-element.30), channel_id=1, source_target_pairs={{0,4},{4,8},{8,12},{12,16},{16,20},{20,24},{24,28},{28,32},{32,36}... | collective-permute-start | bytes 393224 | tf_op jit(solution)/shard_map/back/ppermute | solution.py:280
  105.5 11.5 %collective-permute-start.4 = (bf16[128,512]{1,0:T(8,128)(2,1)S(1)}, bf16[128,512]{1,0:T(8,128)(2,1)S(1)}, u32[]{:S(2)}, u32[]{:S(2)}) collective-permute-start(bf16[128,512]{1,0:T(8,128)(2,1)S(1)} %get-tuple-element.31), channel_id=1, source_target_pairs={{0,508},{4,0},{8,4},{12,8},{16,12},{20,16},{24,20},{28,24},{32,28}... | collective-permute-start | bytes 393224 | tf_op jit(solution)/shard_map/back/ppermute | solution.py:280
  120.9 3.4 %collective-permute-start.11 = (bf16[160,768]{1,0:T(8,128)(2,1)S(1)}, bf16[160,768]{1,0:T(8,128)(2,1)S(1)}, u32[]{:S(2)}, u32[]{:S(2)}) collective-permute-start(bf16[160,768]{1,0:T(8,128)(2,1)S(1)} %total.1.own_ref), channel_id=1, source_target_pairs={{0,4},{4,0},{1,5},{5,1},{2,6},{6,2},{3,7},{7,3},{8,12},{12,8},{9,1... | collective-permute-start | bytes 737288 | tf_op jit(solution)/shard_map/total/ppermute | solution.py:284
  142.6 7.2 %copy-start.4 = (bf16[1024,3,256]{0,2,1:T(8,128)(2,1)S(1)}, bf16[1024,3,256]{0,2,1:T(8,128)(2,1)}, u32[]{:S(2)}) copy-start(bf16[1024,3,256]{0,2,1:T(8,128)(2,1)} %copy-done.3) | copy-start | bytes 4718596
  143.5 26.4 %all-to-all-start.4 = ((bf16[16,8,1280]{2,1,0:T(8,128)(2,1)}), bf16[16,8,1280]{2,1,0:T(8,128)(2,1)S(1)}, u32[]{:S(2)}, u32[]{:S(2)}) async-start(bf16[16,8,1280]{2,1,0:T(8,128)(2,1)} %pad_maximum_fusion), calls=%async_computation.4 | async-start | bytes 655360 | tf_op jit(solution)/shard_map/weight/all_to_all | solution.py:275
  150.2 8.3 %collective-permute-start.10 = (bf16[128,256]{1,0:T(8,128)(2,1)S(1)}, bf16[128,256]{1,0:T(8,128)(2,1)S(1)}, u32[]{:S(2)}, u32[]{:S(2)}) collective-permute-start(bf16[128,256]{1,0:T(8,128)(2,1)S(1)} %get-tuple-element.38), channel_id=1, source_target_pairs={{0,3},{1,0},{2,1},{3,2},{4,7},{5,4},{6,5},{7,6},{8,11},{9,8},{10,9... | collective-permute-start | bytes 196616 | tf_op jit(solution)/shard_map/feature/ppermute | solution.py:280
  152.6 8.3 %collective-permute-start.9 = (bf16[128,256]{1,0:T(8,128)(2,1)S(1)}, bf16[128,256]{1,0:T(8,128)(2,1)S(1)}, u32[]{:S(2)}, u32[]{:S(2)}) collective-permute-start(bf16[128,256]{1,0:T(8,128)(2,1)S(1)} %get-tuple-element.39), channel_id=1, source_target_pairs={{0,2},{1,3},{2,0},{3,1},{4,6},{5,7},{6,4},{7,5},{8,10},{9,11},{10,... | collective-permute-start | bytes 196616 | tf_op jit(solution)/shard_map/feature/ppermute | solution.py:280
  156.2 6.2 %collective-permute-start.8 = (bf16[128,256]{1,0:T(8,128)(2,1)S(1)}, bf16[128,256]{1,0:T(8,128)(2,1)S(1)}, u32[]{:S(2)}, u32[]{:S(2)}) collective-permute-start(bf16[128,256]{1,0:T(8,128)(2,1)S(1)} %get-tuple-element.37), channel_id=1, source_target_pairs={{0,1},{1,2},{2,3},{3,0},{4,5},{5,6},{6,7},{7,4},{8,9},{9,10},{10,1... | collective-permute-start | bytes 196616 | tf_op jit(solution)/shard_map/feature/ppermute | solution.py:280

commit v6 on v5

--- a/solution.py
+++ b/solution.py
@@ -231,13 +231,11 @@
 def weight_kernel(in_own_ref, in_other_ref, own_ref, other_ref, out_ref):
     own, other = own_ref[...], other_ref[...]
     vnode = own[ROWS + 16 :].astype(F32) + other[ROWS + 16 :].astype(F32)
-    high, low = two_terms(vnode[:8] + vnode[8:])
-    tail = jnp.concatenate([high.astype(F32), low.astype(F32)], axis=0).astype(BF16)
+    vnode = vnode[:8] + vnode[8:]
     for part in range(4):
         at = slice(part * 128, (part + 1) * 128)
         term = mul(in_own_ref[at, :], own, NN) + mul(in_other_ref[at, :], other, NN)
-        out_ref[part, :128, :] = term.astype(BF16)
-        out_ref[part, 128:, :] = tail
+        out_ref[part] = jnp.concatenate([term, vnode], axis=0).astype(BF16)
 
 
 def finish_kernel(parts_ref, weight_ref, vnode_ref):
@@ -362,9 +360,9 @@
             summed = summed + shift(piece, "mp", step).astype(F32)
         feature_grad = summed.astype(BF16)
     with jax.named_scope("weight"):
-        term, = call(weight_kernel, [((4, 144, 3 * COLS), BF16)], in_own, in_other, own, other, flops=3 * 10**8)
+        term, = call(weight_kernel, [((4, 136, 3 * COLS), BF16)], in_own, in_other, own, other, flops=3 * 10**8)
         term = jnp.sum(exchange(term, "x").astype(F32), axis=0)
-        vnode = term[128:136, :512] + term[136:, :512]
+        vnode = term[128:, :512]
         tail = jnp.broadcast_to(vnode[None], (16, 8, 512))
         term = jnp.concatenate([term[:128].reshape(16, 8, 3 * COLS), tail], axis=2).astype(BF16)
         weight_grad, vnode_grad = call(

time: 172 us -> 171 us (level)
  no operation moved by 1% of the time
where the time goes in v6:
time: 171 us; the launch traced here: 170 us
  starting transfers between devices  82.4 us (48%)
  waiting for transfers between devices  48.6 us (28%)
  blocking collectives  17.2 us (10%)
  Pallas kernels  10.7 us (6%)
  local copies, waits for them, and re-layouts  4.62 us (3%)
  matrix products  3.8 us (2%)
    all_to_all x4, starting transfers between devices, exchange(): return lax.all_to_all(values, axis, split_axis=0, concat_axis=0, tiled=True)  42 us
    ppermute x7, starting transfers between devices, shift(): lax.ppermute(values, axis, [(i, (i + step) % count) for i in range(count)])  26 us
    all_to_all x4, waiting for transfers between devices, exchange(): return lax.all_to_all(values, axis, split_axis=0, concat_axis=0, tiled=True)  23.7 us
    ppermute x7, waiting for transfers between devices, shift(): lax.ppermute(values, axis, [(i, (i + step) % count) for i in range(count)])  23.4 us
    all_to_all x1, blocking collectives, exchange(): return lax.all_to_all(values, axis, split_axis=0, concat_axis=0, tiled=True)  17.2 us
    ppermute x5, starting transfers between devices, swap(): lax.ppermute(values, axis, [(i, i ^ bit) for i in range(SIZES[axis])])  14.4 us
    pallas_call x8, Pallas kernels, call(): pl.pallas_call(kernel, out_shape=shapes, in_specs=[SMEM] * scalars + [VME...  10.7 us
    unnamed x23, local copies, waits for them, and re-layouts  3.43 us
  transfers between devices with their start and end apart: 16, of which 9 were waited for; matrix products, arithmetic and copies ran while one was open for 5% of the time, Pallas kernels for 3%

profile of v6, /device:TPU:16, one launch (start us, length us, event | category | flops | bytes accessed | tf_op | source)
XLA Modules:
  0.0 170.2 jit_solution(7332851715627798314)
XLA Ops:
  2.1 19.8 %all-to-all-start = ((s32[128,1,4]{2,1,0:T(1,128)}), s32[128,1,4]{2,1,0:T(1,128)S(1)}, u32[]{:S(2)}, u32[]{:S(2)}) async-start(s32[128,1,4]{2,1,0:T(1,128)} %ask.1), calls=%async_computation | async-start | bytes 131072 | tf_op jit(solution)/shard_map/ask/all_to_all | solution.py:273
  21.9 1.8 %copy.28 = bf16[1024,3,256]{0,2,1:T(8,128)(2,1)S(1)} copy(bf16[1024,3,256]{2,0,1:T(8,128)(2,1)} %param.10) | data formatting | bytes 3145728 | tf_op args[1]
  25.1 11.2 %all-to-all-done.asked_ref = s32[128,1,4]{2,1,0:T(1,128)S(1)} async-done(((s32[128,1,4]{2,1,0:T(1,128)}), s32[128,1,4]{2,1,0:T(1,128)S(1)}, u32[]{:S(2)}, u32[]{:S(2)}) %all-to-all-start) | async-done | bytes 2080 | tf_op jit(solution)/shard_map/ask/all_to_all | solution.py:273
  36.3 1.5 serve.1
  37.9 6.2 %all-to-all-start.1 = ((bf16[128,8,256]{2,1,0:T(8,128)(2,1)}), bf16[128,8,256]{2,1,0:T(8,128)(2,1)S(1)}, u32[]{:S(2)}, u32[]{:S(2)}) async-start(bf16[128,8,256]{2,1,0:T(8,128)(2,1)} %bitcast.3), calls=%async_computation.1 | async-start | bytes 1048576 | tf_op jit(solution)/shard_map/serve/all_to_all | solution.py:273
  44.1 1.9 %collective-permute-start = (bf16[128,512]{1,0:T(8,128)(2,1)S(1)}, bf16[128,512]{1,0:T(8,128)(2,1)S(1)}, u32[]{:S(2)}, u32[]{:S(2)}) collective-permute-start(bf16[128,512]{1,0:T(8,128)(2,1)S(1)} %slice.82.own_ref.kv_ref), channel_id=1, source_target_pairs={{0,4},{4,8},{8,12},{12,16},{16,20},{20,24},{24,28},{28,32},{32,36}... | collective-permute-start | bytes 393224 | tf_op jit(solution)/shard_map/project/ppermute | solution.py:278
  46.0 7.0 %collective-permute-start.1 = (bf16[128,512]{1,0:T(8,128)(2,1)S(1)}, bf16[128,512]{1,0:T(8,128)(2,1)S(1)}, u32[]{:S(2)}, u32[]{:S(2)}) collective-permute-start(bf16[128,512]{1,0:T(8,128)(2,1)S(1)} %slice.82.own_ref.kv_ref), channel_id=1, source_target_pairs={{0,508},{4,0},{8,4},{12,8},{16,12},{20,16},{24,20},{28,24},{32,28}... | collective-permute-start | bytes 393224 | tf_op jit(solution)/shard_map/project/ppermute | solution.py:278
  54.1 2.1 %collective-permute-start.2 = (bf16[512,128]{1,0:T(8,128)(2,1)S(1)}, bf16[512,128]{1,0:T(8,128)(2,1)S(1)}, u32[]{:S(2)}, u32[]{:S(2)}) collective-permute-start(bf16[512,128]{1,0:T(8,128)(2,1)S(1)} %slice.59), channel_id=1, source_target_pairs={{0,4},{4,0},{1,5},{5,1},{2,6},{6,2},{3,7},{7,3},{8,12},{12,8},{9,1... | collective-permute-start | bytes 393224 | tf_op jit(solution)/shard_map/select/ppermute | solution.py:282
  57.8 15.1 %collective-permute-done.left_ref = bf16[128,512]{1,0:T(8,128)(2,1)S(1)} collective-permute-done((bf16[128,512]{1,0:T(8,128)(2,1)S(1)}, bf16[128,512]{1,0:T(8,128)(2,1)S(1)}, u32[]{:S(2)}, u32[]{:S(2)}) %collective-permute-start) | collective-permute-done | bytes 131104 | tf_op jit(solution)/shard_map/project/ppermute | solution.py:278
  72.9 1.4 local.1
  74.3 2.0 %all-to-all-done.1 = bf16[128,8,256]{2,1,0:T(8,128)(2,1)S(1)} async-done(((bf16[128,8,256]{2,1,0:T(8,128)(2,1)}), bf16[128,8,256]{2,1,0:T(8,128)(2,1)S(1)}, u32[]{:S(2)}, u32[]{:S(2)}) %all-to-all-start.1) | async-done | bytes 524320 | tf_op jit(solution)/shard_map/serve/all_to_all | solution.py:273
  76.3 2.2 %near.1 = (bf16[1024,256]{1,0:T(8,128)(2,1)}, f32[4,128]{1,0:T(4,128)S(1)}, f32[256,128]{1,0:T(8,128)S(1)}) custom-call(f32[3,2]{1,0:T(4,128)S(1)} %copy.32.bias_ref, s32[4,128]{1,0:T(4,128)S(1)} %copy-done.2, f32[256,128]{1,0:T(8,128)S(1)} %get-tuple-element.22.query_ref, bf16[1024,256]{1,0:T(8,128)(2,1)S(1)} %bitcast.16, ...), custom_call_target="tpu_custom_call" | custom-call | flops 100000000 | bytes 1447960 | tf_op jit(solution)/shard_map/near/pallas_call | solution.py:261
  78.5 9.9 %all-to-all-start.2 = ((bf16[128,8,256]{2,1,0:T(8,128)(2,1)}), bf16[128,8,256]{2,1,0:T(8,128)(2,1)S(1)}, u32[]{:S(2)}, u32[]{:S(2)}) async-start(bf16[128,8,256]{2,1,0:T(8,128)(2,1)} %bitcast.5), calls=%async_computation.2 | async-start | bytes 1048576 | tf_op jit(solution)/shard_map/near/all_to_all | solution.py:273
  88.4 3.2 %back.1 = (bf16[128,256]{1,0:T(8,128)(2,1)S(1)}, bf16[128,512]{1,0:T(8,128)(2,1)S(1)}, f32[128,512]{1,0:T(8,128)S(1)}, bf16[128,512]{1,0:T(8,128)(2,1)S(1)}, f32[4,512]{1,0:T(4,128)S(1)}) custom-call(f32[3,2]{1,0:T(4,128)S(1)} %copy.32.bias_ref, f32[128,256]{1,0:T(8,128)S(1)} %slice.56.query_ref, bf16[128,512]{1,0:T(8,128)(2,1)S(1)} %collective-permute-done.left_ref, ...), custom_call_target="tpu_custom_call" | custom-call | flops 100000000 | bytes 1331224 | tf_op jit(solution)/shard_map/back/pallas_call | solution.py:261
  91.6 1.5 fusion.3
  93.1 2.2 %collective-permute-start.6 = (f32[4,1024]{1,0:T(4,128)S(1)}, f32[4,1024]{1,0:T(4,128)S(1)}, u32[]{:S(2)}, u32[]{:S(2)}) collective-permute-start(f32[4,1024]{1,0:T(4,128)S(1)} %slice_add_fusion), channel_id=1, source_target_pairs={{0,2},{1,3},{2,0},{3,1},{4,6},{5,7},{6,4},{7,5},{8,10},{9,11},{10,... | collective-permute-start | bytes 49160 | tf_op jit(solution)/shard_map/virtual/ppermute | solution.py:282
  95.4 4.3 %collective-permute-start.7 = (f32[4,1024]{1,0:T(4,128)S(1)}, f32[4,1024]{1,0:T(4,128)S(1)}, u32[]{:S(2)}, u32[]{:S(2)}) collective-permute-start(f32[4,1024]{1,0:T(4,128)S(1)} %slice_add_fusion), channel_id=1, source_target_pairs={{0,3},{1,2},{2,1},{3,0},{4,7},{5,6},{6,5},{7,4},{8,11},{9,10},{10,... | collective-permute-start | bytes 49160 | tf_op jit(solution)/shard_map/virtual/ppermute | solution.py:282
  99.7 3.9 %collective-permute-start.5 = (f32[4,1024]{1,0:T(4,128)S(1)}, f32[4,1024]{1,0:T(4,128)S(1)}, u32[]{:S(2)}, u32[]{:S(2)}) collective-permute-start(f32[4,1024]{1,0:T(4,128)S(1)} %slice_add_fusion), channel_id=1, source_target_pairs={{0,1},{1,0},{2,3},{3,2},{4,5},{5,4},{6,7},{7,6},{8,9},{9,8},{10,11... | collective-permute-start | bytes 49160 | tf_op jit(solution)/shard_map/virtual/ppermute | solution.py:282
  103.6 1.9 %collective-permute-start.3 = (bf16[128,512]{1,0:T(8,128)(2,1)S(1)}, bf16[128,512]{1,0:T(8,128)(2,1)S(1)}, u32[]{:S(2)}, u32[]{:S(2)}) collective-permute-start(bf16[128,512]{1,0:T(8,128)(2,1)S(1)} %get-tuple-element.30), channel_id=1, source_target_pairs={{0,4},{4,8},{8,12},{12,16},{16,20},{20,24},{24,28},{28,32},{32,36}... | collective-permute-start | bytes 393224 | tf_op jit(solution)/shard_map/back/ppermute | solution.py:278
  105.5 7.0 %collective-permute-start.4 = (bf16[128,512]{1,0:T(8,128)(2,1)S(1)}, bf16[128,512]{1,0:T(8,128)(2,1)S(1)}, u32[]{:S(2)}, u32[]{:S(2)}) collective-permute-start(bf16[128,512]{1,0:T(8,128)(2,1)S(1)} %get-tuple-element.31), channel_id=1, source_target_pairs={{0,508},{4,0},{8,4},{12,8},{16,12},{20,16},{24,20},{28,24},{32,28}... | collective-permute-start | bytes 393224 | tf_op jit(solution)/shard_map/back/ppermute | solution.py:278
  112.6 4.5 %collective-permute-done.3.from_left_ref = bf16[128,512]{1,0:T(8,128)(2,1)S(1)} collective-permute-done((bf16[128,512]{1,0:T(8,128)(2,1)S(1)}, bf16[128,512]{1,0:T(8,128)(2,1)S(1)}, u32[]{:S(2)}, u32[]{:S(2)}) %collective-permute-start.3) | collective-permute-done | bytes 131104 | tf_op jit(solution)/shard_map/back/ppermute | solution.py:278
  117.0 3.5 %all-to-all-done.2 = bf16[128,8,256]{2,1,0:T(8,128)(2,1)S(1)} async-done(((bf16[128,8,256]{2,1,0:T(8,128)(2,1)}), bf16[128,8,256]{2,1,0:T(8,128)(2,1)S(1)}, u32[]{:S(2)}, u32[]{:S(2)}) %all-to-all-start.2) | async-done | bytes 524320 | tf_op jit(solution)/shard_map/near/all_to_all | solution.py:273
  120.9 1.9 %collective-permute-start.11 = (bf16[160,768]{1,0:T(8,128)(2,1)S(1)}, bf16[160,768]{1,0:T(8,128)(2,1)S(1)}, u32[]{:S(2)}, u32[]{:S(2)}) collective-permute-start(bf16[160,768]{1,0:T(8,128)(2,1)S(1)} %total.1.own_ref), channel_id=1, source_target_pairs={{0,4},{4,0},{1,5},{5,1},{2,6},{6,2},{3,7},{7,3},{8,12},{12,8},{9,1... | collective-permute-start | bytes 737288 | tf_op jit(solution)/shard_map/total/ppermute | solution.py:282
  122.8 1.5 collective-permute-done.11.other_ref
  124.9 17.2 %all_to_all.25 = bf16[4,136,768]{2,1,0:T(8,128)(2,1)S(1)} all-to-all(bf16[4,136,768]{2,1,0:T(8,128)(2,1)S(1)} %weight.2), channel_id=1, replica_groups=mesh['z'=16,'x'=4,'c'=2,'mp'=4] {'x'}, dimensions={0} | all-to-all | bytes 1671168 | tf_op jit(solution)/shard_map/weight/all_to_all | solution.py:273
  143.0 6.2 %all-to-all-start.4 = ((bf16[16,8,1280]{2,1,0:T(8,128)(2,1)}), bf16[16,8,1280]{2,1,0:T(8,128)(2,1)S(1)}, u32[]{:S(2)}, u32[]{:S(2)}) async-start(bf16[16,8,1280]{2,1,0:T(8,128)(2,1)} %pad_maximum_fusion), calls=%async_computation.4 | async-start | bytes 655360 | tf_op jit(solution)/shard_map/weight/all_to_all | solution.py:273
  149.6 2.4 %collective-permute-start.10 = (bf16[128,256]{1,0:T(8,128)(2,1)S(1)}, bf16[128,256]{1,0:T(8,128)(2,1)S(1)}, u32[]{:S(2)}, u32[]{:S(2)}) collective-permute-start(bf16[128,256]{1,0:T(8,128)(2,1)S(1)} %get-tuple-element.38), channel_id=1, source_target_pairs={{0,3},{1,0},{2,1},{3,2},{4,7},{5,4},{6,5},{7,6},{8,11},{9,8},{10,9... | collective-permute-start | bytes 196616 | tf_op jit(solution)/shard_map/feature/ppermute | solution.py:278
  152.0 3.6 %collective-permute-start.9 = (bf16[128,256]{1,0:T(8,128)(2,1)S(1)}, bf16[128,256]{1,0:T(8,128)(2,1)S(1)}, u32[]{:S(2)}, u32[]{:S(2)}) collective-permute-start(bf16[128,256]{1,0:T(8,128)(2,1)S(1)} %get-tuple-element.39), channel_id=1, source_target_pairs={{0,2},{1,3},{2,0},{3,1},{4,6},{5,7},{6,4},{7,5},{8,10},{9,11},{10,... | collective-permute-start | bytes 196616 | tf_op jit(solution)/shard_map/feature/ppermute | solution.py:278
  155.6 2.3 %collective-permute-start.8 = (bf16[128,256]{1,0:T(8,128)(2,1)S(1)}, bf16[128,256]{1,0:T(8,128)(2,1)S(1)}, u32[]{:S(2)}, u32[]{:S(2)}) collective-permute-start(bf16[128,256]{1,0:T(8,128)(2,1)S(1)} %get-tuple-element.37), channel_id=1, source_target_pairs={{0,1},{1,2},{2,3},{3,0},{4,5},{5,6},{6,7},{7,4},{8,9},{9,10},{10,1... | collective-permute-start | bytes 196616 | tf_op jit(solution)/shard_map/feature/ppermute | solution.py:278
  157.9 2.3 %collective-permute-done.9 = bf16[128,256]{1,0:T(8,128)(2,1)S(1)} collective-permute-done((bf16[128,256]{1,0:T(8,128)(2,1)S(1)}, bf16[128,256]{1,0:T(8,128)(2,1)S(1)}, u32[]{:S(2)}, u32[]{:S(2)}) %collective-permute-start.9) | collective-permute-done | bytes 65568 | tf_op jit(solution)/shard_map/feature/ppermute | solution.py:278
  160.2 1.5 collective-permute-done.8
  162.4 7.1 %all-to-all-done.4.parts_ref = bf16[16,8,1280]{2,1,0:T(8,128)(2,1)S(1)} async-done(((bf16[16,8,1280]{2,1,0:T(8,128)(2,1)}), bf16[16,8,1280]{2,1,0:T(8,128)(2,1)S(1)}, u32[]{:S(2)}, u32[]{:S(2)}) %all-to-all-start.4) | async-done | bytes 327712 | tf_op jit(solution)/shard_map/weight/all_to_all | solution.py:273
  (63 shorter events, 9.3 us)
Async XLA Ops:
  0.6 0.7 copy-start.1
  2.1 34.2 %all-to-all-start = ((s32[128,1,4]{2,1,0:T(1,128)}), s32[128,1,4]{2,1,0:T(1,128)S(1)}, u32[]{:S(2)}, u32[]{:S(2)}) async-start(s32[128,1,4]{2,1,0:T(1,128)} %ask.1), calls=%async_computation | async-start | bytes 131072 | tf_op jit(solution)/shard_map/ask/all_to_all | solution.py:273
  21.9 1.8 %copy-start.6 = (bf16[128,1024]{1,0:T(8,128)(2,1)S(1)}, bf16[128,1024]{1,0:T(8,128)(2,1)}, u32[]{:S(2)}) copy-start(bf16[128,1024]{1,0:T(8,128)(2,1)} %param.9) | copy-start | bytes 786436
  23.7 32.5 %copy-start.3 = (bf16[1024,3,256]{0,2,1:T(8,128)(2,1)}, bf16[1024,3,256]{0,2,1:T(8,128)(2,1)S(1)}, u32[]{:S(2)}) copy-start(bf16[1024,3,256]{0,2,1:T(8,128)(2,1)S(1)} %copy.28) | copy-start | bytes 4718596
  24.4 0.8 copy-start.5
  25.1 28.0 %copy-start.7 = (bf16[4,1024]{1,0:T(4,128)(2,1)S(1)}, bf16[4,1024]{1,0:T(4,128)(2,1)}, u32[]{:S(2)}) copy-start(bf16[4,1024]{1,0:T(4,128)(2,1)} %param.11) | copy-start | bytes 24580
  37.9 38.4 %all-to-all-start.1 = ((bf16[128,8,256]{2,1,0:T(8,128)(2,1)}), bf16[128,8,256]{2,1,0:T(8,128)(2,1)S(1)}, u32[]{:S(2)}, u32[]{:S(2)}) async-start(bf16[128,8,256]{2,1,0:T(8,128)(2,1)} %bitcast.3), calls=%async_computation.1 | async-start | bytes 1048576 | tf_op jit(solution)/shard_map/serve/all_to_all | solution.py:273
  44.1 28.9 %collective-permute-start = (bf16[128,512]{1,0:T(8,128)(2,1)S(1)}, bf16[128,512]{1,0:T(8,128)(2,1)S(1)}, u32[]{:S(2)}, u32[]{:S(2)}) collective-permute-start(bf16[128,512]{1,0:T(8,128)(2,1)S(1)} %slice.82.own_ref.kv_ref), channel_id=1, source_target_pairs={{0,4},{4,8},{8,12},{12,16},{16,20},{20,24},{24,28},{28,32},{32,36}... | collective-permute-start | bytes 393224 | tf_op jit(solution)/shard_map/project/ppermute | solution.py:278
  46.0 26.9 %collective-permute-start.1 = (bf16[128,512]{1,0:T(8,128)(2,1)S(1)}, bf16[128,512]{1,0:T(8,128)(2,1)S(1)}, u32[]{:S(2)}, u32[]{:S(2)}) collective-permute-start(bf16[128,512]{1,0:T(8,128)(2,1)S(1)} %slice.82.own_ref.kv_ref), channel_id=1, source_target_pairs={{0,508},{4,0},{8,4},{12,8},{16,12},{20,16},{24,20},{28,24},{32,28}... | collective-permute-start | bytes 393224 | tf_op jit(solution)/shard_map/project/ppermute | solution.py:278
  54.0 3.5 %copy-start.9 = (f32[3,2]{0,1:T(2,128)S(1)}, f32[3,2]{0,1:T(2,128)}, u32[]{:S(2)}) copy-start(f32[3,2]{0,1:T(2,128)} %param.12) | copy-start | bytes 76
  54.0 3.6 %copy-start.8 = (s32[128,4]{0,1:T(4,128)S(1)}, s32[128,4]{0,1:T(4,128)}, u32[]{:S(2)}) copy-start(s32[128,4]{0,1:T(4,128)} %param.15) | copy-start | bytes 6148
  54.0 18.9 %copy-start = (bf16[128,256]{1,0:T(8,128)(2,1)S(1)}, bf16[128,256]{1,0:T(8,128)(2,1)}, u32[]{:S(2)}) copy-start(bf16[128,256]{1,0:T(8,128)(2,1)} %grad_ref.3) | copy-start | bytes 196612
  54.1 22.2 %copy-start.2 = (s32[4,128]{1,0:T(4,128)S(1)}, s32[4,128]{1,0:T(4,128)}, u32[]{:S(2)}) copy-start(s32[4,128]{1,0:T(4,128)} %neighbours_ref.3) | copy-start | bytes 6148
  54.1 3.6 %collective-permute-start.2 = (bf16[512,128]{1,0:T(8,128)(2,1)S(1)}, bf16[512,128]{1,0:T(8,128)(2,1)S(1)}, u32[]{:S(2)}, u32[]{:S(2)}) collective-permute-start(bf16[512,128]{1,0:T(8,128)(2,1)S(1)} %slice.59), channel_id=1, source_target_pairs={{0,4},{4,0},{1,5},{5,1},{2,6},{6,2},{3,7},{7,3},{8,12},{12,8},{9,1... | collective-permute-start | bytes 393224 | tf_op jit(solution)/shard_map/select/ppermute | solution.py:282
  78.5 42.0 %all-to-all-start.2 = ((bf16[128,8,256]{2,1,0:T(8,128)(2,1)}), bf16[128,8,256]{2,1,0:T(8,128)(2,1)S(1)}, u32[]{:S(2)}, u32[]{:S(2)}) async-start(bf16[128,8,256]{2,1,0:T(8,128)(2,1)} %bitcast.5), calls=%async_computation.2 | async-start | bytes 1048576 | tf_op jit(solution)/shard_map/near/all_to_all | solution.py:273
  93.1 19.4 %collective-permute-start.6 = (f32[4,1024]{1,0:T(4,128)S(1)}, f32[4,1024]{1,0:T(4,128)S(1)}, u32[]{:S(2)}, u32[]{:S(2)}) collective-permute-start(f32[4,1024]{1,0:T(4,128)S(1)} %slice_add_fusion), channel_id=1, source_target_pairs={{0,2},{1,3},{2,0},{3,1},{4,6},{5,7},{6,4},{7,5},{8,10},{9,11},{10,... | collective-permute-start | bytes 49160 | tf_op jit(solution)/shard_map/virtual/ppermute | solution.py:282
  95.4 17.1 %collective-permute-start.7 = (f32[4,1024]{1,0:T(4,128)S(1)}, f32[4,1024]{1,0:T(4,128)S(1)}, u32[]{:S(2)}, u32[]{:S(2)}) collective-permute-start(f32[4,1024]{1,0:T(4,128)S(1)} %slice_add_fusion), channel_id=1, source_target_pairs={{0,3},{1,2},{2,1},{3,0},{4,7},{5,6},{6,5},{7,4},{8,11},{9,10},{10,... | collective-permute-start | bytes 49160 | tf_op jit(solution)/shard_map/virtual/ppermute | solution.py:282
  99.7 12.8 %collective-permute-start.5 = (f32[4,1024]{1,0:T(4,128)S(1)}, f32[4,1024]{1,0:T(4,128)S(1)}, u32[]{:S(2)}, u32[]{:S(2)}) collective-permute-start(f32[4,1024]{1,0:T(4,128)S(1)} %slice_add_fusion), channel_id=1, source_target_pairs={{0,1},{1,0},{2,3},{3,2},{4,5},{5,4},{6,7},{7,6},{8,9},{9,8},{10,11... | collective-permute-start | bytes 49160 | tf_op jit(solution)/shard_map/virtual/ppermute | solution.py:282
  103.6 13.5 %collective-permute-start.3 = (bf16[128,512]{1,0:T(8,128)(2,1)S(1)}, bf16[128,512]{1,0:T(8,128)(2,1)S(1)}, u32[]{:S(2)}, u32[]{:S(2)}) collective-permute-start(bf16[128,512]{1,0:T(8,128)(2,1)S(1)} %get-tuple-element.30), channel_id=1, source_target_pairs={{0,4},{4,8},{8,12},{12,16},{16,20},{20,24},{24,28},{28,32},{32,36}... | collective-permute-start | bytes 393224 | tf_op jit(solution)/shard_map/back/ppermute | solution.py:278
  105.5 11.5 %collective-permute-start.4 = (bf16[128,512]{1,0:T(8,128)(2,1)S(1)}, bf16[128,512]{1,0:T(8,128)(2,1)S(1)}, u32[]{:S(2)}, u32[]{:S(2)}) collective-permute-start(bf16[128,512]{1,0:T(8,128)(2,1)S(1)} %get-tuple-element.31), channel_id=1, source_target_pairs={{0,508},{4,0},{8,4},{12,8},{16,12},{20,16},{24,20},{28,24},{32,28}... | collective-permute-start | bytes 393224 | tf_op jit(solution)/shard_map/back/ppermute | solution.py:278
  120.9 3.4 %collective-permute-start.11 = (bf16[160,768]{1,0:T(8,128)(2,1)S(1)}, bf16[160,768]{1,0:T(8,128)(2,1)S(1)}, u32[]{:S(2)}, u32[]{:S(2)}) collective-permute-start(bf16[160,768]{1,0:T(8,128)(2,1)S(1)} %total.1.own_ref), channel_id=1, source_target_pairs={{0,4},{4,0},{1,5},{5,1},{2,6},{6,2},{3,7},{7,3},{8,12},{12,8},{9,1... | collective-permute-start | bytes 737288 | tf_op jit(solution)/shard_map/total/ppermute | solution.py:282
  142.0 7.2 %copy-start.4 = (bf16[1024,3,256]{0,2,1:T(8,128)(2,1)S(1)}, bf16[1024,3,256]{0,2,1:T(8,128)(2,1)}, u32[]{:S(2)}) copy-start(bf16[1024,3,256]{0,2,1:T(8,128)(2,1)} %copy-done.3) | copy-start | bytes 4718596
  143.0 26.5 %all-to-all-start.4 = ((bf16[16,8,1280]{2,1,0:T(8,128)(2,1)}), bf16[16,8,1280]{2,1,0:T(8,128)(2,1)S(1)}, u32[]{:S(2)}, u32[]{:S(2)}) async-start(bf16[16,8,1280]{2,1,0:T(8,128)(2,1)} %pad_maximum_fusion), calls=%async_computation.4 | async-start | bytes 655360 | tf_op jit(solution)/shard_map/weight/all_to_all | solution.py:273
  149.6 8.3 %collective-permute-start.10 = (bf16[128,256]{1,0:T(8,128)(2,1)S(1)}, bf16[128,256]{1,0:T(8,128)(2,1)S(1)}, u32[]{:S(2)}, u32[]{:S(2)}) collective-permute-start(bf16[128,256]{1,0:T(8,128)(2,1)S(1)} %get-tuple-element.38), channel_id=1, source_target_pairs={{0,3},{1,0},{2,1},{3,2},{4,7},{5,4},{6,5},{7,6},{8,11},{9,8},{10,9... | collective-permute-start | bytes 196616 | tf_op jit(solution)/shard_map/feature/ppermute | solution.py:278
  152.0 8.2 %collective-permute-start.9 = (bf16[128,256]{1,0:T(8,128)(2,1)S(1)}, bf16[128,256]{1,0:T(8,128)(2,1)S(1)}, u32[]{:S(2)}, u32[]{:S(2)}) collective-permute-start(bf16[128,256]{1,0:T(8,128)(2,1)S(1)} %get-tuple-element.39), channel_id=1, source_target_pairs={{0,2},{1,3},{2,0},{3,1},{4,6},{5,7},{6,4},{7,5},{8,10},{9,11},{10,... | collective-permute-start | bytes 196616 | tf_op jit(solution)/shard_map/feature/ppermute | solution.py:278
  155.6 6.2 %collective-permute-start.8 = (bf16[128,256]{1,0:T(8,128)(2,1)S(1)}, bf16[128,256]{1,0:T(8,128)(2,1)S(1)}, u32[]{:S(2)}, u32[]{:S(2)}) collective-permute-start(bf16[128,256]{1,0:T(8,128)(2,1)S(1)} %get-tuple-element.37), channel_id=1, source_target_pairs={{0,1},{1,2},{2,3},{3,0},{4,5},{5,6},{6,7},{7,4},{8,9},{9,10},{10,1... | collective-permute-start | bytes 196616 | tf_op jit(solution)/shard_map/feature/ppermute | solution.py:278

commit v7 on v6

--- a/solution.py
+++ b/solution.py
@@ -238,6 +238,15 @@
         out_ref[part] = jnp.concatenate([term, vnode], axis=0).astype(BF16)
 
 
+def spread_kernel(parts_ref, out_ref):
+    total = parts_ref[0].astype(F32)
+    for part in range(1, SIZES["x"]):
+        total += parts_ref[part].astype(F32)
+    for part in range(SIZES["z"]):
+        rows = [total[part * 8 : (part + 1) * 8], total[128:, :512]]
+        out_ref[part] = jnp.concatenate(rows, axis=1).astype(BF16)
+
+
 def finish_kernel(parts_ref, weight_ref, vnode_ref):
     out_scale = 1.0 / math.sqrt(ROWS * SHARDS)
     total = parts_ref[0].astype(F32)
@@ -361,10 +370,7 @@
         feature_grad = summed.astype(BF16)
     with jax.named_scope("weight"):
         term, = call(weight_kernel, [((4, 136, 3 * COLS), BF16)], in_own, in_other, own, other, flops=3 * 10**8)
-        term = jnp.sum(exchange(term, "x").astype(F32), axis=0)
-        vnode = term[128:, :512]
-        tail = jnp.broadcast_to(vnode[None], (16, 8, 512))
-        term = jnp.concatenate([term[:128].reshape(16, 8, 3 * COLS), tail], axis=2).astype(BF16)
+        term, = call(spread_kernel, [((16, 8, 3 * COLS + 512), BF16)], exchange(term, "x"))
         weight_grad, vnode_grad = call(
             finish_kernel, [((3, 8, COLS), F32), ((VIRTUAL, width_in), F32)], exchange(term, "z"),
         )

time: 171 us -> 171 us (level)
    pallas_call x8 -> x9, Pallas kernels: 10.7 us -> 11.6 us  [call(): pl.pallas_call(kernel, out_shape=shapes, in_specs=[SMEM] * scalars + [VME...]
where the time goes in v7:
time: 171 us; the launch traced here: 170 us
  starting transfers between devices  82.4 us (48%)
  waiting for transfers between devices  48.6 us (28%)
  blocking collectives  17.3 us (10%)
  Pallas kernels  11.6 us (7%)
  local copies, waits for them, and re-layouts  4.61 us (3%)
  matrix products  3.8 us (2%)
    all_to_all x4, starting transfers between devices, exchange(): return lax.all_to_all(values, axis, split_axis=0, concat_axis=0, tiled=True)  42 us
    ppermute x7, starting transfers between devices, shift(): lax.ppermute(values, axis, [(i, (i + step) % count) for i in range(count)])  26 us
    all_to_all x4, waiting for transfers between devices, exchange(): return lax.all_to_all(values, axis, split_axis=0, concat_axis=0, tiled=True)  23.7 us
    ppermute x7, waiting for transfers between devices, shift(): lax.ppermute(values, axis, [(i, (i + step) % count) for i in range(count)])  23.4 us
    all_to_all x1, blocking collectives, exchange(): return lax.all_to_all(values, axis, split_axis=0, concat_axis=0, tiled=True)  17.3 us
    ppermute x5, starting transfers between devices, swap(): lax.ppermute(values, axis, [(i, i ^ bit) for i in range(SIZES[axis])])  14.4 us
    pallas_call x9, Pallas kernels, call(): pl.pallas_call(kernel, out_shape=shapes, in_specs=[SMEM] * scalars + [VME...  11.6 us
    unnamed x23, local copies, waits for them, and re-layouts  3.44 us
  transfers between devices with their start and end apart: 16, of which 9 were waited for; matrix products, arithmetic and copies ran while one was open for 5% of the time, Pallas kernels for 3%

profile of v7, /device:TPU:16, one launch (start us, length us, event | category | flops | bytes accessed | tf_op | source)
XLA Modules:
  0.0 170.2 jit_solution(4527403980414075261)
XLA Ops:
  2.1 19.8 %all-to-all-start = ((s32[128,1,4]{2,1,0:T(1,128)}), s32[128,1,4]{2,1,0:T(1,128)S(1)}, u32[]{:S(2)}, u32[]{:S(2)}) async-start(s32[128,1,4]{2,1,0:T(1,128)} %ask.1), calls=%async_computation | async-start | bytes 131072 | tf_op jit(solution)/shard_map/ask/all_to_all | solution.py:282
  21.9 1.8 %copy.28 = bf16[1024,3,256]{0,2,1:T(8,128)(2,1)S(1)} copy(bf16[1024,3,256]{2,0,1:T(8,128)(2,1)} %param.10) | data formatting | bytes 3145728 | tf_op args[1]
  25.1 11.2 %all-to-all-done.asked_ref = s32[128,1,4]{2,1,0:T(1,128)S(1)} async-done(((s32[128,1,4]{2,1,0:T(1,128)}), s32[128,1,4]{2,1,0:T(1,128)S(1)}, u32[]{:S(2)}, u32[]{:S(2)}) %all-to-all-start) | async-done | bytes 2080 | tf_op jit(solution)/shard_map/ask/all_to_all | solution.py:282
  36.3 1.6 serve.1
  37.9 6.2 %all-to-all-start.1 = ((bf16[128,8,256]{2,1,0:T(8,128)(2,1)}), bf16[128,8,256]{2,1,0:T(8,128)(2,1)S(1)}, u32[]{:S(2)}, u32[]{:S(2)}) async-start(bf16[128,8,256]{2,1,0:T(8,128)(2,1)} %bitcast.3), calls=%async_computation.1 | async-start | bytes 1048576 | tf_op jit(solution)/shard_map/serve/all_to_all | solution.py:282
  44.1 1.9 %collective-permute-start = (bf16[128,512]{1,0:T(8,128)(2,1)S(1)}, bf16[128,512]{1,0:T(8,128)(2,1)S(1)}, u32[]{:S(2)}, u32[]{:S(2)}) collective-permute-start(bf16[128,512]{1,0:T(8,128)(2,1)S(1)} %slice.67.own_ref.kv_ref), channel_id=1, source_target_pairs={{0,4},{4,8},{8,12},{12,16},{16,20},{20,24},{24,28},{28,32},{32,36}... | collective-permute-start | bytes 393224 | tf_op jit(solution)/shard_map/project/ppermute | solution.py:287
  46.0 7.0 %collective-permute-start.1 = (bf16[128,512]{1,0:T(8,128)(2,1)S(1)}, bf16[128,512]{1,0:T(8,128)(2,1)S(1)}, u32[]{:S(2)}, u32[]{:S(2)}) collective-permute-start(bf16[128,512]{1,0:T(8,128)(2,1)S(1)} %slice.67.own_ref.kv_ref), channel_id=1, source_target_pairs={{0,508},{4,0},{8,4},{12,8},{16,12},{20,16},{24,20},{28,24},{32,28}... | collective-permute-start | bytes 393224 | tf_op jit(solution)/shard_map/project/ppermute | solution.py:287
  54.1 2.1 %collective-permute-start.2 = (bf16[512,128]{1,0:T(8,128)(2,1)S(1)}, bf16[512,128]{1,0:T(8,128)(2,1)S(1)}, u32[]{:S(2)}, u32[]{:S(2)}) collective-permute-start(bf16[512,128]{1,0:T(8,128)(2,1)S(1)} %slice.50), channel_id=1, source_target_pairs={{0,4},{4,0},{1,5},{5,1},{2,6},{6,2},{3,7},{7,3},{8,12},{12,8},{9,1... | collective-permute-start | bytes 393224 | tf_op jit(solution)/shard_map/select/ppermute | solution.py:291
  57.8 15.1 %collective-permute-done.left_ref = bf16[128,512]{1,0:T(8,128)(2,1)S(1)} collective-permute-done((bf16[128,512]{1,0:T(8,128)(2,1)S(1)}, bf16[128,512]{1,0:T(8,128)(2,1)S(1)}, u32[]{:S(2)}, u32[]{:S(2)}) %collective-permute-start) | collective-permute-done | bytes 131104 | tf_op jit(solution)/shard_map/project/ppermute | solution.py:287
  72.9 1.4 local.1
  74.3 2.0 %all-to-all-done.1 = bf16[128,8,256]{2,1,0:T(8,128)(2,1)S(1)} async-done(((bf16[128,8,256]{2,1,0:T(8,128)(2,1)}), bf16[128,8,256]{2,1,0:T(8,128)(2,1)S(1)}, u32[]{:S(2)}, u32[]{:S(2)}) %all-to-all-start.1) | async-done | bytes 524320 | tf_op jit(solution)/shard_map/serve/all_to_all | solution.py:282
  76.3 2.3 %near.1 = (bf16[1024,256]{1,0:T(8,128)(2,1)}, f32[4,128]{1,0:T(4,128)S(1)}, f32[256,128]{1,0:T(8,128)S(1)}) custom-call(f32[3,2]{1,0:T(4,128)S(1)} %copy.32.bias_ref, s32[4,128]{1,0:T(4,128)S(1)} %copy-done.2, f32[256,128]{1,0:T(8,128)S(1)} %get-tuple-element.22.query_ref, bf16[1024,256]{1,0:T(8,128)(2,1)S(1)} %bitcast.14, ...), custom_call_target="tpu_custom_call" | custom-call | flops 100000000 | bytes 1447960 | tf_op jit(solution)/shard_map/near/pallas_call | solution.py:270
  78.5 9.9 %all-to-all-start.2 = ((bf16[128,8,256]{2,1,0:T(8,128)(2,1)}), bf16[128,8,256]{2,1,0:T(8,128)(2,1)S(1)}, u32[]{:S(2)}, u32[]{:S(2)}) async-start(bf16[128,8,256]{2,1,0:T(8,128)(2,1)} %bitcast.5), calls=%async_computation.2 | async-start | bytes 1048576 | tf_op jit(solution)/shard_map/near/all_to_all | solution.py:282
  88.5 3.2 %back.1 = (bf16[128,256]{1,0:T(8,128)(2,1)S(1)}, bf16[128,512]{1,0:T(8,128)(2,1)S(1)}, f32[128,512]{1,0:T(8,128)S(1)}, bf16[128,512]{1,0:T(8,128)(2,1)S(1)}, f32[4,512]{1,0:T(4,128)S(1)}) custom-call(f32[3,2]{1,0:T(4,128)S(1)} %copy.32.bias_ref, f32[128,256]{1,0:T(8,128)S(1)} %slice.47.query_ref, bf16[128,512]{1,0:T(8,128)(2,1)S(1)} %collective-permute-done.left_ref, ...), custom_call_target="tpu_custom_call" | custom-call | flops 100000000 | bytes 1331224 | tf_op jit(solution)/shard_map/back/pallas_call | solution.py:270
  91.6 1.5 fusion.3
  93.1 2.2 %collective-permute-start.6 = (f32[4,1024]{1,0:T(4,128)S(1)}, f32[4,1024]{1,0:T(4,128)S(1)}, u32[]{:S(2)}, u32[]{:S(2)}) collective-permute-start(f32[4,1024]{1,0:T(4,128)S(1)} %slice_add_fusion), channel_id=1, source_target_pairs={{0,2},{1,3},{2,0},{3,1},{4,6},{5,7},{6,4},{7,5},{8,10},{9,11},{10,... | collective-permute-start | bytes 49160 | tf_op jit(solution)/shard_map/virtual/ppermute | solution.py:291
  95.4 4.3 %collective-permute-start.7 = (f32[4,1024]{1,0:T(4,128)S(1)}, f32[4,1024]{1,0:T(4,128)S(1)}, u32[]{:S(2)}, u32[]{:S(2)}) collective-permute-start(f32[4,1024]{1,0:T(4,128)S(1)} %slice_add_fusion), channel_id=1, source_target_pairs={{0,3},{1,2},{2,1},{3,0},{4,7},{5,6},{6,5},{7,4},{8,11},{9,10},{10,... | collective-permute-start | bytes 49160 | tf_op jit(solution)/shard_map/virtual/ppermute | solution.py:291
  99.7 3.9 %collective-permute-start.5 = (f32[4,1024]{1,0:T(4,128)S(1)}, f32[4,1024]{1,0:T(4,128)S(1)}, u32[]{:S(2)}, u32[]{:S(2)}) collective-permute-start(f32[4,1024]{1,0:T(4,128)S(1)} %slice_add_fusion), channel_id=1, source_target_pairs={{0,1},{1,0},{2,3},{3,2},{4,5},{5,4},{6,7},{7,6},{8,9},{9,8},{10,11... | collective-permute-start | bytes 49160 | tf_op jit(solution)/shard_map/virtual/ppermute | solution.py:291
  103.6 1.9 %collective-permute-start.3 = (bf16[128,512]{1,0:T(8,128)(2,1)S(1)}, bf16[128,512]{1,0:T(8,128)(2,1)S(1)}, u32[]{:S(2)}, u32[]{:S(2)}) collective-permute-start(bf16[128,512]{1,0:T(8,128)(2,1)S(1)} %get-tuple-element.30), channel_id=1, source_target_pairs={{0,4},{4,8},{8,12},{12,16},{16,20},{20,24},{24,28},{28,32},{32,36}... | collective-permute-start | bytes 393224 | tf_op jit(solution)/shard_map/back/ppermute | solution.py:287
  105.5 7.0 %collective-permute-start.4 = (bf16[128,512]{1,0:T(8,128)(2,1)S(1)}, bf16[128,512]{1,0:T(8,128)(2,1)S(1)}, u32[]{:S(2)}, u32[]{:S(2)}) collective-permute-start(bf16[128,512]{1,0:T(8,128)(2,1)S(1)} %get-tuple-element.31), channel_id=1, source_target_pairs={{0,508},{4,0},{8,4},{12,8},{16,12},{20,16},{24,20},{28,24},{32,28}... | collective-permute-start | bytes 393224 | tf_op jit(solution)/shard_map/back/ppermute | solution.py:287
  112.6 4.4 %collective-permute-done.3.from_left_ref = bf16[128,512]{1,0:T(8,128)(2,1)S(1)} collective-permute-done((bf16[128,512]{1,0:T(8,128)(2,1)S(1)}, bf16[128,512]{1,0:T(8,128)(2,1)S(1)}, u32[]{:S(2)}, u32[]{:S(2)}) %collective-permute-start.3) | collective-permute-done | bytes 131104 | tf_op jit(solution)/shard_map/back/ppermute | solution.py:287
  117.1 3.5 %all-to-all-done.2 = bf16[128,8,256]{2,1,0:T(8,128)(2,1)S(1)} async-done(((bf16[128,8,256]{2,1,0:T(8,128)(2,1)}), bf16[128,8,256]{2,1,0:T(8,128)(2,1)S(1)}, u32[]{:S(2)}, u32[]{:S(2)}) %all-to-all-start.2) | async-done | bytes 524320 | tf_op jit(solution)/shard_map/near/all_to_all | solution.py:282
  120.9 1.9 %collective-permute-start.11 = (bf16[160,768]{1,0:T(8,128)(2,1)S(1)}, bf16[160,768]{1,0:T(8,128)(2,1)S(1)}, u32[]{:S(2)}, u32[]{:S(2)}) collective-permute-start(bf16[160,768]{1,0:T(8,128)(2,1)S(1)} %total.1.own_ref), channel_id=1, source_target_pairs={{0,4},{4,0},{1,5},{5,1},{2,6},{6,2},{3,7},{7,3},{8,12},{12,8},{9,1... | collective-permute-start | bytes 737288 | tf_op jit(solution)/shard_map/total/ppermute | solution.py:291
  122.8 1.5 collective-permute-done.11.other_ref
  124.9 17.3 %all_to_all.25.parts_ref = bf16[4,136,768]{2,1,0:T(8,128)(2,1)S(1)} all-to-all(bf16[4,136,768]{2,1,0:T(8,128)(2,1)S(1)} %weight.3), channel_id=1, replica_groups=mesh['z'=16,'x'=4,'c'=2,'mp'=4] {'x'}, dimensions={0} | all-to-all | bytes 1671168 | tf_op jit(solution)/shard_map/weight/all_to_all | solution.py:282
  143.0 6.2 %all-to-all-start.4 = ((bf16[16,8,1280]{2,1,0:T(8,128)(2,1)}), bf16[16,8,1280]{2,1,0:T(8,128)(2,1)S(1)}, u32[]{:S(2)}, u32[]{:S(2)}) async-start(bf16[16,8,1280]{2,1,0:T(8,128)(2,1)} %weight.4), calls=%async_computation.4 | async-start | bytes 655360 | tf_op jit(solution)/shard_map/weight/all_to_all | solution.py:282
  149.7 2.4 %collective-permute-start.10 = (bf16[128,256]{1,0:T(8,128)(2,1)S(1)}, bf16[128,256]{1,0:T(8,128)(2,1)S(1)}, u32[]{:S(2)}, u32[]{:S(2)}) collective-permute-start(bf16[128,256]{1,0:T(8,128)(2,1)S(1)} %get-tuple-element.38), channel_id=1, source_target_pairs={{0,3},{1,0},{2,1},{3,2},{4,7},{5,4},{6,5},{7,6},{8,11},{9,8},{10,9... | collective-permute-start | bytes 196616 | tf_op jit(solution)/shard_map/feature/ppermute | solution.py:287
  152.1 3.6 %collective-permute-start.9 = (bf16[128,256]{1,0:T(8,128)(2,1)S(1)}, bf16[128,256]{1,0:T(8,128)(2,1)S(1)}, u32[]{:S(2)}, u32[]{:S(2)}) collective-permute-start(bf16[128,256]{1,0:T(8,128)(2,1)S(1)} %get-tuple-element.39), channel_id=1, source_target_pairs={{0,2},{1,3},{2,0},{3,1},{4,6},{5,7},{6,4},{7,5},{8,10},{9,11},{10,... | collective-permute-start | bytes 196616 | tf_op jit(solution)/shard_map/feature/ppermute | solution.py:287
  155.7 2.3 %collective-permute-start.8 = (bf16[128,256]{1,0:T(8,128)(2,1)S(1)}, bf16[128,256]{1,0:T(8,128)(2,1)S(1)}, u32[]{:S(2)}, u32[]{:S(2)}) collective-permute-start(bf16[128,256]{1,0:T(8,128)(2,1)S(1)} %get-tuple-element.37), channel_id=1, source_target_pairs={{0,1},{1,2},{2,3},{3,0},{4,5},{5,6},{6,7},{7,4},{8,9},{9,10},{10,1... | collective-permute-start | bytes 196616 | tf_op jit(solution)/shard_map/feature/ppermute | solution.py:287
  158.0 2.3 %collective-permute-done.9 = bf16[128,256]{1,0:T(8,128)(2,1)S(1)} collective-permute-done((bf16[128,256]{1,0:T(8,128)(2,1)S(1)}, bf16[128,256]{1,0:T(8,128)(2,1)S(1)}, u32[]{:S(2)}, u32[]{:S(2)}) %collective-permute-start.9) | collective-permute-done | bytes 65568 | tf_op jit(solution)/shard_map/feature/ppermute | solution.py:287
  160.3 1.5 collective-permute-done.8
  162.5 7.1 %all-to-all-done.4.parts_ref = bf16[16,8,1280]{2,1,0:T(8,128)(2,1)S(1)} async-done(((bf16[16,8,1280]{2,1,0:T(8,128)(2,1)}), bf16[16,8,1280]{2,1,0:T(8,128)(2,1)S(1)}, u32[]{:S(2)}, u32[]{:S(2)}) %all-to-all-start.4) | async-done | bytes 327712 | tf_op jit(solution)/shard_map/weight/all_to_all | solution.py:282
  (59 shorter events, 9.2 us)
Async XLA Ops:
  0.6 0.7 copy-start.1
  2.1 34.2 %all-to-all-start = ((s32[128,1,4]{2,1,0:T(1,128)}), s32[128,1,4]{2,1,0:T(1,128)S(1)}, u32[]{:S(2)}, u32[]{:S(2)}) async-start(s32[128,1,4]{2,1,0:T(1,128)} %ask.1), calls=%async_computation | async-start | bytes 131072 | tf_op jit(solution)/shard_map/ask/all_to_all | solution.py:282
  21.9 1.8 %copy-start.6 = (bf16[128,1024]{1,0:T(8,128)(2,1)S(1)}, bf16[128,1024]{1,0:T(8,128)(2,1)}, u32[]{:S(2)}) copy-start(bf16[128,1024]{1,0:T(8,128)(2,1)} %param.9) | copy-start | bytes 786436
  23.7 32.5 %copy-start.3 = (bf16[1024,3,256]{0,2,1:T(8,128)(2,1)}, bf16[1024,3,256]{0,2,1:T(8,128)(2,1)S(1)}, u32[]{:S(2)}) copy-start(bf16[1024,3,256]{0,2,1:T(8,128)(2,1)S(1)} %copy.28) | copy-start | bytes 4718596
  24.4 0.8 copy-start.5
  25.1 27.9 %copy-start.7 = (bf16[4,1024]{1,0:T(4,128)(2,1)S(1)}, bf16[4,1024]{1,0:T(4,128)(2,1)}, u32[]{:S(2)}) copy-start(bf16[4,1024]{1,0:T(4,128)(2,1)} %param.11) | copy-start | bytes 24580
  37.9 38.4 %all-to-all-start.1 = ((bf16[128,8,256]{2,1,0:T(8,128)(2,1)}), bf16[128,8,256]{2,1,0:T(8,128)(2,1)S(1)}, u32[]{:S(2)}, u32[]{:S(2)}) async-start(bf16[128,8,256]{2,1,0:T(8,128)(2,1)} %bitcast.3), calls=%async_computation.1 | async-start | bytes 1048576 | tf_op jit(solution)/shard_map/serve/all_to_all | solution.py:282
  44.1 28.9 %collective-permute-start = (bf16[128,512]{1,0:T(8,128)(2,1)S(1)}, bf16[128,512]{1,0:T(8,128)(2,1)S(1)}, u32[]{:S(2)}, u32[]{:S(2)}) collective-permute-start(bf16[128,512]{1,0:T(8,128)(2,1)S(1)} %slice.67.own_ref.kv_ref), channel_id=1, source_target_pairs={{0,4},{4,8},{8,12},{12,16},{16,20},{20,24},{24,28},{28,32},{32,36}... | collective-permute-start | bytes 393224 | tf_op jit(solution)/shard_map/project/ppermute | solution.py:287
  46.0 26.9 %collective-permute-start.1 = (bf16[128,512]{1,0:T(8,128)(2,1)S(1)}, bf16[128,512]{1,0:T(8,128)(2,1)S(1)}, u32[]{:S(2)}, u32[]{:S(2)}) collective-permute-start(bf16[128,512]{1,0:T(8,128)(2,1)S(1)} %slice.67.own_ref.kv_ref), channel_id=1, source_target_pairs={{0,508},{4,0},{8,4},{12,8},{16,12},{20,16},{24,20},{28,24},{32,28}... | collective-permute-start | bytes 393224 | tf_op jit(solution)/shard_map/project/ppermute | solution.py:287
  54.0 3.5 %copy-start.9 = (f32[3,2]{0,1:T(2,128)S(1)}, f32[3,2]{0,1:T(2,128)}, u32[]{:S(2)}) copy-start(f32[3,2]{0,1:T(2,128)} %param.12) | copy-start | bytes 76
  54.0 3.6 %copy-start.8 = (s32[128,4]{0,1:T(4,128)S(1)}, s32[128,4]{0,1:T(4,128)}, u32[]{:S(2)}) copy-start(s32[128,4]{0,1:T(4,128)} %param.15) | copy-start | bytes 6148
  54.0 18.9 %copy-start = (bf16[128,256]{1,0:T(8,128)(2,1)S(1)}, bf16[128,256]{1,0:T(8,128)(2,1)}, u32[]{:S(2)}) copy-start(bf16[128,256]{1,0:T(8,128)(2,1)} %grad_ref.3) | copy-start | bytes 196612
  54.1 22.2 %copy-start.2 = (s32[4,128]{1,0:T(4,128)S(1)}, s32[4,128]{1,0:T(4,128)}, u32[]{:S(2)}) copy-start(s32[4,128]{1,0:T(4,128)} %neighbours_ref.3) | copy-start | bytes 6148
  54.1 3.6 %collective-permute-start.2 = (bf16[512,128]{1,0:T(8,128)(2,1)S(1)}, bf16[512,128]{1,0:T(8,128)(2,1)S(1)}, u32[]{:S(2)}, u32[]{:S(2)}) collective-permute-start(bf16[512,128]{1,0:T(8,128)(2,1)S(1)} %slice.50), channel_id=1, source_target_pairs={{0,4},{4,0},{1,5},{5,1},{2,6},{6,2},{3,7},{7,3},{8,12},{12,8},{9,1... | collective-permute-start | bytes 393224 | tf_op jit(solution)/shard_map/select/ppermute | solution.py:291
  78.5 42.0 %all-to-all-start.2 = ((bf16[128,8,256]{2,1,0:T(8,128)(2,1)}), bf16[128,8,256]{2,1,0:T(8,128)(2,1)S(1)}, u32[]{:S(2)}, u32[]{:S(2)}) async-start(bf16[128,8,256]{2,1,0:T(8,128)(2,1)} %bitcast.5), calls=%async_computation.2 | async-start | bytes 1048576 | tf_op jit(solution)/shard_map/near/all_to_all | solution.py:282
  93.1 19.4 %collective-permute-start.6 = (f32[4,1024]{1,0:T(4,128)S(1)}, f32[4,1024]{1,0:T(4,128)S(1)}, u32[]{:S(2)}, u32[]{:S(2)}) collective-permute-start(f32[4,1024]{1,0:T(4,128)S(1)} %slice_add_fusion), channel_id=1, source_target_pairs={{0,2},{1,3},{2,0},{3,1},{4,6},{5,7},{6,4},{7,5},{8,10},{9,11},{10,... | collective-permute-start | bytes 49160 | tf_op jit(solution)/shard_map/virtual/ppermute | solution.py:291
  95.4 17.1 %collective-permute-start.7 = (f32[4,1024]{1,0:T(4,128)S(1)}, f32[4,1024]{1,0:T(4,128)S(1)}, u32[]{:S(2)}, u32[]{:S(2)}) collective-permute-start(f32[4,1024]{1,0:T(4,128)S(1)} %slice_add_fusion), channel_id=1, source_target_pairs={{0,3},{1,2},{2,1},{3,0},{4,7},{5,6},{6,5},{7,4},{8,11},{9,10},{10,... | collective-permute-start | bytes 49160 | tf_op jit(solution)/shard_map/virtual/ppermute | solution.py:291
  99.7 12.8 %collective-permute-start.5 = (f32[4,1024]{1,0:T(4,128)S(1)}, f32[4,1024]{1,0:T(4,128)S(1)}, u32[]{:S(2)}, u32[]{:S(2)}) collective-permute-start(f32[4,1024]{1,0:T(4,128)S(1)} %slice_add_fusion), channel_id=1, source_target_pairs={{0,1},{1,0},{2,3},{3,2},{4,5},{5,4},{6,7},{7,6},{8,9},{9,8},{10,11... | collective-permute-start | bytes 49160 | tf_op jit(solution)/shard_map/virtual/ppermute | solution.py:291
  103.6 13.5 %collective-permute-start.3 = (bf16[128,512]{1,0:T(8,128)(2,1)S(1)}, bf16[128,512]{1,0:T(8,128)(2,1)S(1)}, u32[]{:S(2)}, u32[]{:S(2)}) collective-permute-start(bf16[128,512]{1,0:T(8,128)(2,1)S(1)} %get-tuple-element.30), channel_id=1, source_target_pairs={{0,4},{4,8},{8,12},{12,16},{16,20},{20,24},{24,28},{28,32},{32,36}... | collective-permute-start | bytes 393224 | tf_op jit(solution)/shard_map/back/ppermute | solution.py:287
  105.5 11.5 %collective-permute-start.4 = (bf16[128,512]{1,0:T(8,128)(2,1)S(1)}, bf16[128,512]{1,0:T(8,128)(2,1)S(1)}, u32[]{:S(2)}, u32[]{:S(2)}) collective-permute-start(bf16[128,512]{1,0:T(8,128)(2,1)S(1)} %get-tuple-element.31), channel_id=1, source_target_pairs={{0,508},{4,0},{8,4},{12,8},{16,12},{20,16},{24,20},{28,24},{32,28}... | collective-permute-start | bytes 393224 | tf_op jit(solution)/shard_map/back/ppermute | solution.py:287
  120.9 3.4 %collective-permute-start.11 = (bf16[160,768]{1,0:T(8,128)(2,1)S(1)}, bf16[160,768]{1,0:T(8,128)(2,1)S(1)}, u32[]{:S(2)}, u32[]{:S(2)}) collective-permute-start(bf16[160,768]{1,0:T(8,128)(2,1)S(1)} %total.1.own_ref), channel_id=1, source_target_pairs={{0,4},{4,0},{1,5},{5,1},{2,6},{6,2},{3,7},{7,3},{8,12},{12,8},{9,1... | collective-permute-start | bytes 737288 | tf_op jit(solution)/shard_map/total/ppermute | solution.py:291
  124.9 24.4 %copy-start.4 = (bf16[1024,3,256]{0,2,1:T(8,128)(2,1)S(1)}, bf16[1024,3,256]{0,2,1:T(8,128)(2,1)}, u32[]{:S(2)}) copy-start(bf16[1024,3,256]{0,2,1:T(8,128)(2,1)} %copy-done.3) | copy-start | bytes 4718596
  143.0 26.5 %all-to-all-start.4 = ((bf16[16,8,1280]{2,1,0:T(8,128)(2,1)}), bf16[16,8,1280]{2,1,0:T(8,128)(2,1)S(1)}, u32[]{:S(2)}, u32[]{:S(2)}) async-start(bf16[16,8,1280]{2,1,0:T(8,128)(2,1)} %weight.4), calls=%async_computation.4 | async-start | bytes 655360 | tf_op jit(solution)/shard_map/weight/all_to_all | solution.py:282
  149.7 8.3 %collective-permute-start.10 = (bf16[128,256]{1,0:T(8,128)(2,1)S(1)}, bf16[128,256]{1,0:T(8,128)(2,1)S(1)}, u32[]{:S(2)}, u32[]{:S(2)}) collective-permute-start(bf16[128,256]{1,0:T(8,128)(2,1)S(1)} %get-tuple-element.38), channel_id=1, source_target_pairs={{0,3},{1,0},{2,1},{3,2},{4,7},{5,4},{6,5},{7,6},{8,11},{9,8},{10,9... | collective-permute-start | bytes 196616 | tf_op jit(solution)/shard_map/feature/ppermute | solution.py:287
  152.1 8.2 %collective-permute-start.9 = (bf16[128,256]{1,0:T(8,128)(2,1)S(1)}, bf16[128,256]{1,0:T(8,128)(2,1)S(1)}, u32[]{:S(2)}, u32[]{:S(2)}) collective-permute-start(bf16[128,256]{1,0:T(8,128)(2,1)S(1)} %get-tuple-element.39), channel_id=1, source_target_pairs={{0,2},{1,3},{2,0},{3,1},{4,6},{5,7},{6,4},{7,5},{8,10},{9,11},{10,... | collective-permute-start | bytes 196616 | tf_op jit(solution)/shard_map/feature/ppermute | solution.py:287
  155.7 6.2 %collective-permute-start.8 = (bf16[128,256]{1,0:T(8,128)(2,1)S(1)}, bf16[128,256]{1,0:T(8,128)(2,1)S(1)}, u32[]{:S(2)}, u32[]{:S(2)}) collective-permute-start(bf16[128,256]{1,0:T(8,128)(2,1)S(1)} %get-tuple-element.37), channel_id=1, source_target_pairs={{0,1},{1,2},{2,3},{3,0},{4,5},{5,6},{6,7},{7,4},{8,9},{9,10},{10,1... | collective-permute-start | bytes 196616 | tf_op jit(solution)/shard_map/feature/ppermute | solution.py:287
